TPU v7x, 256 devices: a whole 4x4x8 slice. The times are simulated.
256 devices in a mesh: inst: 32 (over x, z_hi, core), tp: 8 (over z_lo, y).
Axes of the slice: x: 4, y: 4, z: 8 (z_hi: 4, z_lo: 2; z = z_hi * 2 + z_lo), core: 2. Of those that a mesh axis runs over, the one named last changes fastest.
Arguments:
- new_states: bfloat16 [3, 1024, 4096], P(None, 'inst'), may hold values from -6 to 6
- attn_gain: bfloat16 [4096], replicated, may hold values from 0.099609375 to 1.8984375
- q_weight: bfloat16 [4096, 4096], P(None, 'tp'), may hold values from -0.09375 to 0.09375
- k_weight: bfloat16 [4096, 1024], P(None, 'tp'), may hold values from -0.1875 to 0.1875
- v_weight: bfloat16 [4096, 1024], P(None, 'tp'), may hold values from -0.09375 to 0.09375
- o_weight: bfloat16 [4096, 4096], P('tp'), may hold values from -0.5 to 0.5
- prompt_keys: bfloat16 [32, 2048, 1024], P('inst', None, 'tp'), may hold values from -100 to 100
- prompt_values: bfloat16 [32, 2048, 1024], P('inst', None, 'tp'), may hold values from -6 to 6
- owner_index: int32 [1], replicated, may hold values from 0 to 31
Outputs:
- branch_out: bfloat16 [3, 1024, 4096], P(None, 'inst')
All inputs are finite; a program needn't handle non-finite values.
Results may differ from a plain program's by a relative error of at most 0.019.
The roundings to bfloat16 on the way count: a program that leaves them out, or rounds other values in their place, can miss the bound.
Values may be sent and summed in bfloat16 or wider, within the bound.
No kernel may reach another device: no remote copies, remote signals or barrier semaphores. Data moves between devices by JAX's collectives and lax.ppermute only.
A program may use at most 64 MiB of HBM per device.

v0:
```python
import jax
import jax.numpy as jnp
import numpy as np
from jax import lax
from jax.experimental import pallas as pl
from jax.experimental.pallas import tpu as pltpu
from jax.sharding import PartitionSpec as P

HD = 128


epsilon = 1e-05

AXES = ("inst", "tp")
N_X, N_ZH, N_CORE = 4, 4, 2
N_ZL, N_Y = 2, 4


def at(x, zh, core, zl, y):
    inst = (x % N_X * N_ZH + zh % N_ZH) * N_CORE + core % N_CORE
    return inst * (N_ZL * N_Y) + zl % N_ZL * N_Y + y % N_Y


def send(block, dx=0, dzh=0, dcore=0, dzl=0, dy=0, only=lambda x, zh, core: True):
    pairs = [
        (at(x, zh, core, zl, y), at(x + dx, zh + dzh, core + dcore, zl + dzl, y + dy))
        for x in range(N_X)
        for zh in range(N_ZH)
        for core in range(N_CORE)
        for zl in range(N_ZL)
        for y in range(N_Y)
        if only(x, zh, core)
    ]
    return lax.ppermute(block, AXES, pairs)


def from_owner(pieces, at_place, root_place, size, only):
    def branch(place):
        def run(pieces):
            mine = pieces[0]
            for d in (2, 1, 3):
                got = only(pieces[d], d, place)
                mine = jnp.where(at_place == (place + d) % size, got, mine)
            return mine

        return run

    return lax.switch(root_place, [branch(a) for a in range(size)], pieces)


def broadcast(keys, values, root):
    me = lax.axis_index("inst")
    core, zh, x = me % N_CORE, me // N_CORE % N_ZH, me // (N_CORE * N_ZH)
    root_core, root_zh, root_x = root % N_CORE, root // N_CORE % N_ZH, root // (N_CORE * N_ZH)
    has_keys = core == root_core
    held = jnp.where(has_keys, keys, send(values, dcore=1))
    quarter = keys.shape[0] // N_X
    slabs = [held[d * quarter : (d + 1) * quarter] for d in range(N_X)]
    along_x = lambda a, d, place: send(a, dx=d, only=lambda x, zh, core: x == place)
    along_z = lambda a, d, place: send(a, dzh=d, only=lambda x, zh, core: zh == place)
    mine = from_owner(slabs, x, root_x, N_X, along_x)
    mine = from_owner([mine] * N_ZH, zh, root_zh, N_ZH, along_z)
    return mine, has_keys


def from_row(mine):
    row = [mine] + [send(mine, dx=dx) for dx in (1, 3, 2)]
    return row, [send(a, dcore=1) for a in row]


def project(new_states, attn_gain, q_weight, k_weight, v_weight, prompt_len):
    step_count, samples, feature_dim = new_states.shape
    rows = step_count * samples
    q_width, head_dim = q_weight.shape[1], k_weight.shape[1]
    heads, half = q_width // head_dim, head_dim // 2
    depth = 512
    frequency = np.exp(-np.arange(half) * (np.log(500000.0) / half))
    angles = (prompt_len + np.repeat(np.arange(step_count), samples))[:, None] * frequency
    cosine = np.concatenate([np.cos(angles)] * 2, axis=1).astype(np.float32)
    sine = np.concatenate([-np.sin(angles), np.sin(angles)], axis=1).astype(np.float32)

    def kernel(x_ref, gain_ref, cos_ref, sin_ref, wq_ref, wk_ref, wv_ref, q_ref, k_ref, v_ref, inv, acc):
        step = pl.program_id(0)

        @pl.when(step == 0)
        def _():
            states = x_ref[...].astype(jnp.float32)
            inv[...] = lax.rsqrt(jnp.mean(states * states, axis=-1, keepdims=True) + epsilon)
            acc[...] = jnp.zeros_like(acc)

        columns = pl.ds(pl.multiple_of(step * depth, depth), depth)
        states = x_ref[:, columns].astype(jnp.float32)
        gain = gain_ref[:, columns].astype(jnp.float32)
        normed = (states * inv[...] * gain).astype(jnp.bfloat16)
        at_column = 0
        for w_ref in (wq_ref, wk_ref, wv_ref):
            width = w_ref.shape[1]
            acc[:, at_column : at_column + width] += jnp.dot(
                normed, w_ref[...], preferred_element_type=jnp.float32
            )
            at_column += width

        @pl.when(step == pl.num_programs(0) - 1)
        def _():
            def rotated(block):
                swapped = pltpu.roll(block, half, 1)
                return (block * cos_ref[...] + swapped * sin_ref[...]).astype(jnp.bfloat16)

            for head in range(heads):
                q_ref[head] = rotated(acc[:, head * head_dim : (head + 1) * head_dim])
            k_ref[...] = rotated(acc[:, q_width : q_width + head_dim])
            v_ref[...] = acc[:, q_width + head_dim :].astype(jnp.bfloat16)

    whole = lambda *shape: pl.BlockSpec(shape, lambda i: (0,) * len(shape))
    weight = lambda width: pl.BlockSpec((depth, width), lambda i: (i, 0))
    return pl.pallas_call(
        kernel,
        grid=(feature_dim // depth,),
        in_specs=[
            whole(rows, feature_dim),
            whole(1, feature_dim),
            whole(rows, head_dim),
            whole(rows, head_dim),
            weight(q_width),
            weight(head_dim),
            weight(head_dim),
        ],
        out_specs=[whole(heads, rows, head_dim), whole(rows, head_dim), whole(rows, head_dim)],
        out_shape=[
            jax.ShapeDtypeStruct((heads, rows, head_dim), jnp.bfloat16),
            jax.ShapeDtypeStruct((rows, head_dim), jnp.bfloat16),
            jax.ShapeDtypeStruct((rows, head_dim), jnp.bfloat16),
        ],
        scratch_shapes=[
            pltpu.VMEM((rows, 1), jnp.float32),
            pltpu.VMEM((rows, q_width + 2 * head_dim), jnp.float32),
        ],
        compiler_params=pltpu.CompilerParams(vmem_limit_bytes=24 * 2**20),
        cost_estimate=pl.CostEstimate(
            flops=2 * rows * feature_dim * (q_width + 2 * head_dim),
            bytes_accessed=2 * feature_dim * (rows + q_width + 2 * head_dim),
            transcendentals=0,
        ),
    )(
        new_states.reshape(rows, feature_dim),
        attn_gain.reshape(1, feature_dim),
        cosine,
        sine,
        q_weight,
        k_weight,
        v_weight,
    )


def attend(queries, new_keys, new_values, row, other, has_keys, o_weight, step_count):
    heads, rows, head_dim = queries.shape
    samples = rows // step_count
    features = o_weight.shape[1]
    width = features // N_Y
    scale = head_dim**-0.5
    pieces, positions = len(row), row[0].shape[0]

    def kernel(place_ref, q_ref, k_ref, v_ref, o_ref, *rest):
        row_refs, other_refs, rest = rest[:pieces], rest[pieces : 2 * pieces], rest[2 * pieces :]
        out_refs, (keys, values, scores) = rest[:N_Y], rest[N_Y:]

        @pl.when(place_ref[1] == 1)
        def _():
            for p in range(pieces):
                keys[p], values[p] = row_refs[p][...], other_refs[p][...]

        @pl.when(place_ref[1] == 0)
        def _():
            for p in range(pieces):
                keys[p], values[p] = other_refs[p][...], row_refs[p][...]

        step_of = lax.broadcasted_iota(jnp.int32, (rows, 1), 0) // samples
        keys_of = [jnp.concatenate([k_ref[u * samples : (u + 1) * samples]] * step_count, axis=0).astype(jnp.float32) for u in range(step_count)]
        values_of = [jnp.concatenate([v_ref[u * samples : (u + 1) * samples]] * step_count, axis=0).astype(jnp.float32) for u in range(step_count)]
        q_all = q_ref[...].reshape(heads * rows, head_dim)
        row_max = None
        for i in range(pieces):
            s = lax.dot_general(q_all, keys[i], (((1,), (1,)), ((), ())), preferred_element_type=jnp.float32) * scale
            scores[i] = s
            top = jnp.max(s, axis=1, keepdims=True)
            row_max = top if row_max is None else jnp.maximum(row_max, top)
        row_sum = jnp.zeros((heads * rows, 1), jnp.float32)
        weighted = jnp.zeros((heads * rows, head_dim), jnp.float32)
        for i in range(pieces):
            e = jnp.exp(scores[i] - row_max)
            row_sum += jnp.sum(e, axis=1, keepdims=True)
            weighted += jnp.dot(e.astype(jnp.bfloat16), values[i], preferred_element_type=jnp.float32)
        attended = []
        for head in range(heads):
            part = slice(head * rows, (head + 1) * rows)
            q32 = q_ref[head].astype(jnp.float32)
            joint_max, own = row_max[part], []
            for u in range(step_count):
                s = jnp.sum(q32 * keys_of[u], axis=1, keepdims=True) * scale
                s = jnp.where(step_of >= u, s, -1e30)
                joint_max = jnp.maximum(joint_max, s)
                own.append(s)
            rescale = jnp.exp(row_max[part] - joint_max)
            denominator = row_sum[part] * rescale
            numerator = weighted[part] * rescale
            for u in range(step_count):
                e = jnp.where(step_of >= u, jnp.exp(own[u] - joint_max), 0.0)
                denominator += e
                numerator += e.astype(jnp.bfloat16).astype(jnp.float32) * values_of[u]
            attended.append((numerator / denominator).astype(jnp.bfloat16))
        attended = jnp.concatenate(attended, axis=1)
        for d in (2, 1, 3, 0):
            column = lax.rem(place_ref[0] + d, N_Y) * width
            o_block = o_ref[:, pl.ds(pl.multiple_of(column, width), width)]
            out_refs[d][...] = jnp.dot(attended, o_block, preferred_element_type=jnp.float32).astype(jnp.bfloat16)

    place = jnp.stack([lax.axis_index("tp") % N_Y, has_keys.astype(jnp.int32)])
    vmem = pl.BlockSpec(memory_space=pltpu.VMEM)
    return pl.pallas_call(
        kernel,
        in_specs=[pl.BlockSpec(memory_space=pltpu.SMEM)] + [vmem] * (4 + 2 * pieces),
        out_specs=[vmem] * N_Y,
        out_shape=[jax.ShapeDtypeStruct((rows, width), jnp.bfloat16)] * N_Y,
        scratch_shapes=[
            pltpu.VMEM((pieces, positions, head_dim), jnp.bfloat16),
            pltpu.VMEM((pieces, positions, head_dim), jnp.bfloat16),
            pltpu.VMEM((pieces, heads * rows, positions), jnp.float32),
        ],
        compiler_params=pltpu.CompilerParams(vmem_limit_bytes=24 * 2**20),
        cost_estimate=pl.CostEstimate(
            flops=2 * rows * features * o_weight.shape[0] + 8 * heads * rows * pieces * positions * head_dim,
            bytes_accessed=2 * o_weight.size + 4 * pieces * row[0].size,
            transcendentals=0,
        ),
    )(place, queries, new_keys, new_values, o_weight, *row, *other)


def add_up(blocks):
    got = [blocks[0]] + [send(blocks[d], dy=d) for d in (2, 1, 3)]
    along_y = sum(a.astype(jnp.float32) for a in got).astype(jnp.bfloat16)
    across = send(along_y, dzl=1)
    block = (along_y.astype(jnp.float32) + across.astype(jnp.float32)).astype(jnp.bfloat16)
    return [block] + [send(block, dy=d) for d in (1, 2, 3)]


def lay_out(blocks):
    rows, width = blocks[0].shape

    def kernel(y_ref, *rest):
        ins, out = rest[:N_Y], rest[N_Y]
        for d in range(N_Y):
            column = lax.rem(y_ref[0] + N_Y - d, N_Y) * width
            out[:, pl.ds(pl.multiple_of(column, width), width)] = ins[d][...]

    vmem = pl.BlockSpec(memory_space=pltpu.VMEM)
    return pl.pallas_call(
        kernel,
        in_specs=[pl.BlockSpec(memory_space=pltpu.SMEM)] + [vmem] * N_Y,
        out_specs=vmem,
        out_shape=jax.ShapeDtypeStruct((rows, N_Y * width), blocks[0].dtype),
        compiler_params=pltpu.CompilerParams(vmem_limit_bytes=8 * 2**20),
    )(lax.axis_index("tp").reshape(1) % N_Y, *blocks)


def on_device(
    new_states,
    attn_gain,
    q_weight,
    k_weight,
    v_weight,
    o_weight,
    prompt_keys,
    prompt_values,
    owner_index,
):
    step_count, samples, _ = new_states.shape
    piece, has_keys = broadcast(prompt_keys[0], prompt_values[0], owner_index[0])
    new_states, piece = lax.optimization_barrier((new_states, piece))
    row, other = from_row(piece)
    queries, new_keys, new_values = project(
        new_states, attn_gain, q_weight, k_weight, v_weight, prompt_keys.shape[1]
    )
    partial_blocks = attend(queries, new_keys, new_values, row, other, has_keys, o_weight, step_count)
    summed = lay_out(add_up(partial_blocks))
    return summed.reshape(step_count, samples, o_weight.shape[1])


def solution(mesh):
    placed = (
        P(None, "inst", None),
        P(),
        P(None, "tp"),
        P(None, "tp"),
        P(None, "tp"),
        P("tp", None),
        P("inst", None, "tp"),
        P("inst", None, "tp"),
        P(),
    )
    return jax.shard_map(
        on_device, mesh=mesh, in_specs=placed, out_specs=P(None, "inst", None), check_vma=False
    )
```

profile of v0, /device:TPU:65, one launch (start us, length us, event | category | flops | bytes accessed | tf_op | source)
XLA Modules:
  0.0 89.2 jit_solution(15634452027522901533)
XLA Ops:
  0.0 0.0 copy-start.11
  0.0 0.0 copy-start.3
  0.0 0.0 copy-start.2
  0.0 0.8 collective-permute-start.24
  1.7 0.9 %collective-permute-done.24 = bf16[2048,128]{1,0:T(8,128)(2,1)S(1)} collective-permute-done((bf16[2048,128]{1,0:T(8,128)(2,1)}, bf16[2048,128]{1,0:T(8,128)(2,1)S(1)}, u32[]{:S(2)}, u32[]{:S(2)}) %collective-permute-start.24) | collective-permute-done | bytes 524320 | tf_op jit(solution)/shard_map/ppermute | solution.py:34
  2.5 1.1 %bitcast_select_fusion = bf16[2048,128]{1,0:T(8,128)(2,1)S(1)} fusion(bf16[2048,128]{1,0:T(8,128)(2,1)S(1)} %collective-permute-done.24, bf16[1,2048,128]{2,1,0:T(8,128)(2,1)} %param.25, pred[]{:T(512)S(6)} %eq.83), kind=kLoop, calls=%fused_computation.8 | loop fusion | flops 262144 | bytes 1572865 | tf_op jit(solution)/shard_map/jit(_where)/select_n | solution.py:56
  3.7 0.7 fusion
  4.4 14.1 %conditional.2 = (bf16[512,128]{1,0:T(8,128)(2,1)S(1)}) conditional(s32[]{:T(128)} %clamp.7, (s32[]{:T(128)}, bf16[512,128]{1,0:T(8,128)(2,1)}, bf16[512,128]{1,0:T(8,128)(2,1)}, bf16[512,128]{1,0:T(8,128)(2,1)}, bf16[512,128]{1,0:T(8,128)(2,1)S(1)}) %tuple.30, (s32[]{:T(128)}, bf16[512,128]{1,0:T(8,128)(2,1)}, ...), branch_computations={%region_0.1_spmd, %region_1.2_spmd, %region_2.3_spmd, %region_3.4_... | conditional | flops 196611 | bytes 2752698 | solution.py:48
  4.4 0.7 collective-permute-start.6
  5.1 0.7 collective-permute-start.7
  5.7 1.3 %collective-permute-start.8 = (bf16[512,128]{1,0:T(8,128)(2,1)}, bf16[512,128]{1,0:T(8,128)(2,1)S(1)}, u32[]{:S(2)}, u32[]{:S(2)}) collective-permute-start(bf16[512,128]{1,0:T(8,128)(2,1)} %get-tuple-element.84), channel_id=1, source_target_pairs={{128,0},{129,1},{130,2},{131,3},{132,4},{133,5},{134,6},{135,7},{1... | collective-permute-start | bytes 393224 | tf_op jit(solution)/shard_map/cond/branch_2_fun/ppermute | solution.py:34
  7.0 0.0 collective-permute-done.6
  7.1 0.0 collective-permute-done.7
  7.1 9.8 %collective-permute-done.8 = bf16[512,128]{1,0:T(8,128)(2,1)S(1)} collective-permute-done((bf16[512,128]{1,0:T(8,128)(2,1)}, bf16[512,128]{1,0:T(8,128)(2,1)S(1)}, u32[]{:S(2)}, u32[]{:S(2)}) %collective-permute-start.8) | collective-permute-done | bytes 131104 | tf_op jit(solution)/shard_map/cond/branch_2_fun/ppermute | solution.py:34
  16.9 0.7 copy-done.9
  17.5 0.9 %select_select_fusion.2 = bf16[512,128]{1,0:T(8,128)(2,1)S(1)} fusion(bf16[512,128]{1,0:T(8,128)(2,1)S(1)} %collective-permute-done.6, bf16[512,128]{1,0:T(8,128)(2,1)S(1)} %collective-permute-done.7, bf16[512,128]{1,0:T(8,128)(2,1)} %copy-done.9, bf16[512,128]{1,0:T(8,128)(2,1)S(1)} %get-tuple-element.85, pred[]{:T(512)S(6)} %eq.66, pred[]{:T(512)S(6)} %eq.65, ...), kind=kLoop, calls=%fused_computation.2 | loop fusion | flops 196608 | bytes 655363 | tf_op jit(solution)/shard_map/cond/branch_2_fun/jit(_where)/select_n | solution.py:43
  18.5 16.6 %conditional.3 = (bf16[512,128]{1,0:T(8,128)(2,1)S(1)}) conditional(s32[]{:T(128)} %clamp.6, (s32[]{:T(128)}, bf16[512,128]{1,0:T(8,128)(2,1)S(1)}) %tuple.31, (s32[]{:T(128)}, bf16[512,128]{1,0:T(8,128)(2,1)S(1)}) %tuple.31, (s32[]{:T(128)}, bf16[512,128]{1,0:T(8,128)(2,1)S(1)}) %tuple.31, (s32[]{:T(128)}, ...), branch_computations={%region_4.5_spmd, %region_5.6_spmd, %region_6.7_spmd, %region_7.8_... | conditional | flops 196611 | bytes 2228382 | solution.py:48
  18.5 0.7 collective-permute-start.20
  19.2 0.7 collective-permute-start.19
  19.9 1.3 %collective-permute-start.18 = (bf16[512,128]{1,0:T(8,128)(2,1)S(1)}, bf16[512,128]{1,0:T(8,128)(2,1)}, u32[]{:S(2)}, u32[]{:S(2)}) collective-permute-start(bf16[512,128]{1,0:T(8,128)(2,1)S(1)} %get-tuple-element.96), channel_id=1, source_target_pairs={{32,16},{33,17},{34,18},{35,19},{36,20},{37,21},{38,22},{39,23},{4... | collective-permute-start | bytes 393224 | tf_op jit(solution)/shard_map/cond/branch_2_fun/ppermute | solution.py:34
  21.2 0.0 collective-permute-done.20
  21.2 0.0 collective-permute-done.19
  21.2 12.9 %collective-permute-done.18 = bf16[512,128]{1,0:T(8,128)(2,1)} collective-permute-done((bf16[512,128]{1,0:T(8,128)(2,1)S(1)}, bf16[512,128]{1,0:T(8,128)(2,1)}, u32[]{:S(2)}, u32[]{:S(2)}) %collective-permute-start.18) | collective-permute-done | bytes 131104 | tf_op jit(solution)/shard_map/cond/branch_2_fun/ppermute | solution.py:34
  34.1 0.9 %select_select_fusion.6 = bf16[512,128]{1,0:T(8,128)(2,1)S(1)} fusion(bf16[512,128]{1,0:T(8,128)(2,1)} %collective-permute-done.18, bf16[512,128]{1,0:T(8,128)(2,1)S(1)} %collective-permute-done.19, bf16[512,128]{1,0:T(8,128)(2,1)S(1)} %collective-permute-done.20, bf16[512,128]{1,0:T(8,128)(2,1)S(1)} %get-tuple-element.96, pred[]{:T(512)S(6)} %eq.78, ...), kind=kLoop, calls=%fused_computation.6 | loop fusion | flops 196608 | bytes 655363 | tf_op jit(solution)/shard_map/cond/branch_2_fun/jit(_where)/select_n | solution.py:43
  35.1 0.1 collective-permute-start.27
  35.2 0.1 collective-permute-start.26
  35.3 1.5 %collective-permute-start.25 = (bf16[512,128]{1,0:T(8,128)(2,1)S(1)}, bf16[512,128]{1,0:T(8,128)(2,1)S(1)}, u32[]{:S(2)}, u32[]{:S(2)}) collective-permute-start(bf16[512,128]{1,0:T(8,128)(2,1)S(1)} %get-tuple-element.122.rest_0_), channel_id=1, source_target_pairs={{0,64},{1,65},{2,66},{3,67},{4,68},{5,69},{6,70},{7,71},{8,72},{9,... | collective-permute-start | bytes 393224 | tf_op jit(solution)/shard_map/ppermute | solution.py:34
  36.7 0.0 copy-done.11
  36.7 1.7 %collective-permute-start.28 = (bf16[512,128]{1,0:T(8,128)(2,1)S(1)}, bf16[512,128]{1,0:T(8,128)(2,1)S(1)}, u32[]{:S(2)}, u32[]{:S(2)}) collective-permute-start(bf16[512,128]{1,0:T(8,128)(2,1)S(1)} %get-tuple-element.122.rest_0_), channel_id=1, source_target_pairs={{0,8},{1,9},{2,10},{3,11},{4,12},{5,13},{6,14},{7,15},{8,0},{9,1},... | collective-permute-start | bytes 393224 | tf_op jit(solution)/shard_map/ppermute | solution.py:34
  38.4 2.2 %collective-permute-done.27.rest_3_ = bf16[512,128]{1,0:T(8,128)(2,1)S(1)} collective-permute-done((bf16[512,128]{1,0:T(8,128)(2,1)S(1)}, bf16[512,128]{1,0:T(8,128)(2,1)S(1)}, u32[]{:S(2)}, u32[]{:S(2)}) %collective-permute-start.27) | collective-permute-done | bytes 131104 | tf_op jit(solution)/shard_map/ppermute | solution.py:34
  40.6 3.5 %collective-permute-start.31 = (bf16[512,128]{1,0:T(8,128)(2,1)S(1)}, bf16[512,128]{1,0:T(8,128)(2,1)S(1)}, u32[]{:S(2)}, u32[]{:S(2)}) collective-permute-start(bf16[512,128]{1,0:T(8,128)(2,1)S(1)} %collective-permute-done.27.rest_3_), channel_id=1, source_target_pairs={{0,8},{1,9},{2,10},{3,11},{4,12},{5,13},{6,14},{7,15},{8,0},{9,1},... | collective-permute-start | bytes 393224 | tf_op jit(solution)/shard_map/ppermute | solution.py:34
  44.0 0.0 collective-permute-done.26.rest_2_
  44.0 0.0 collective-permute-start.30
  44.1 0.5 collective-permute-done.25.rest_1_
  44.6 0.8 collective-permute-start.29
  45.4 0.1 pad_add_fusion.place_ref
  45.5 0.0 copy-done.5
  45.5 0.0 copy-done.6
  45.5 0.0 copy-done.4
  45.5 0.0 copy-done.3
  45.5 0.0 copy-start
  45.5 2.2 %copy-done = bf16[4096,512]{1,0:T(8,128)(2,1)S(1)} copy-done((bf16[4096,512]{1,0:T(8,128)(2,1)S(1)}, bf16[4096,512]{1,0:T(8,128)(2,1)}, u32[]{:S(2)}) %copy-start) | copy-done | bytes 4194328
  47.7 3.0 %shard_map.109 = (bf16[4,96,128]{2,1,0:T(8,128)(2,1)S(1)}, bf16[96,128]{1,0:T(8,128)(2,1)S(1)}, bf16[96,128]{1,0:T(8,128)(2,1)S(1)}) custom-call(bf16[96,4096]{1,0:T(8,128)(2,1)S(1)} %bitcast.13, bf16[1,4096]{1,0:T(2,128)(2,1)S(1)} %reshape.16.gain_ref, f32[96,128]{1,0:T(8,128)S(1)} %copy-done.6, f32[96,128]{1,0:T(8,128)S(1)} %copy-done.5, ...), custom_call_target="tpu_custom_call" | custom-call | flops 603979776 | bytes 7077888 | tf_op jit(solution)/shard_map/pallas_call | solution.py:116
  50.7 0.0 collective-permute-done.28.rest_4_
  50.7 0.0 collective-permute-done.31.rest_7_
  50.7 0.0 collective-permute-done.30.rest_6_
  50.7 0.0 collective-permute-done.29.rest_5_
  50.8 3.5 %shard_map.110 = (bf16[96,1024]{1,0:T(8,128)(2,1)S(1)}, bf16[96,1024]{1,0:T(8,128)(2,1)S(1)}, bf16[96,1024]{1,0:T(8,128)(2,1)S(1)}, bf16[96,1024]{1,0:T(8,128)(2,1)S(1)}) custom-call(s32[2]{0:T(128)S(1)} %pad_add_fusion.place_ref, bf16[4,96,128]{2,1,0:T(8,128)(2,1)S(1)} %get-tuple-element.109.q_ref, bf16[96,128]{1,0:T(8,128)(2,1)S(1)} %get-tuple-element.110.k_ref, ...), custom_call_target="tpu_custom_call" | custom-call | flops 1207959552 | bytes 5242880 | tf_op jit(solution)/shard_map/pallas_call | solution.py:219
  54.3 3.0 %collective-permute-start.32 = (bf16[96,1024]{1,0:T(8,128)(2,1)S(1)}, bf16[96,1024]{1,0:T(8,128)(2,1)S(1)}, u32[]{:S(2)}, u32[]{:S(2)}) collective-permute-start(bf16[96,1024]{1,0:T(8,128)(2,1)S(1)} %get-tuple-element.114), channel_id=1, source_target_pairs={{0,2},{1,3},{2,0},{3,1},{4,6},{5,7},{6,4},{7,5},{8,10},{9,11},{10,... | collective-permute-start | bytes 589832 | tf_op jit(solution)/shard_map/ppermute | solution.py:34
  57.3 0.4 collective-permute-start.33
  57.7 2.3 %collective-permute-start.34 = (bf16[96,1024]{1,0:T(8,128)(2,1)S(1)}, bf16[96,1024]{1,0:T(8,128)(2,1)S(1)}, u32[]{:S(2)}, u32[]{:S(2)}) collective-permute-start(bf16[96,1024]{1,0:T(8,128)(2,1)S(1)} %get-tuple-element.116), channel_id=1, source_target_pairs={{0,3},{1,0},{2,1},{3,2},{4,7},{5,4},{6,5},{7,6},{8,11},{9,8},{10,9... | collective-permute-start | bytes 589832 | tf_op jit(solution)/shard_map/ppermute | solution.py:34
  59.9 2.5 %collective-permute-done.32 = bf16[96,1024]{1,0:T(8,128)(2,1)S(1)} collective-permute-done((bf16[96,1024]{1,0:T(8,128)(2,1)S(1)}, bf16[96,1024]{1,0:T(8,128)(2,1)S(1)}, u32[]{:S(2)}, u32[]{:S(2)}) %collective-permute-start.32) | collective-permute-done | bytes 196640 | tf_op jit(solution)/shard_map/ppermute | solution.py:34
  62.4 4.5 %collective-permute-done.33 = bf16[96,1024]{1,0:T(8,128)(2,1)S(1)} collective-permute-done((bf16[96,1024]{1,0:T(8,128)(2,1)S(1)}, bf16[96,1024]{1,0:T(8,128)(2,1)S(1)}, u32[]{:S(2)}, u32[]{:S(2)}) %collective-permute-start.33) | collective-permute-done | bytes 196640 | tf_op jit(solution)/shard_map/ppermute | solution.py:34
  66.9 0.0 collective-permute-done.34
  66.9 0.1 add_convert_fusion.1
  67.1 0.1 collective-permute-start.35
  67.2 5.6 %collective-permute-done.35 = bf16[96,1024]{1,0:T(8,128)(2,1)S(1)} collective-permute-done((bf16[96,1024]{1,0:T(8,128)(2,1)S(1)}, bf16[96,1024]{1,0:T(8,128)(2,1)S(1)}, u32[]{:S(2)}, u32[]{:S(2)}) %collective-permute-start.35) | collective-permute-done | bytes 196640 | tf_op jit(solution)/shard_map/ppermute | solution.py:34
  72.8 3.1 %collective-permute-start.38 = (bf16[96,1024]{1,0:T(8,128)(2,1)S(1)}, bf16[96,1024]{1,0:T(8,128)(2,1)S(1)}, u32[]{:S(2)}, u32[]{:S(2)}) collective-permute-start(bf16[96,1024]{1,0:T(8,128)(2,1)S(1)} %add_convert_fusion.rest_0_), channel_id=1, source_target_pairs={{0,3},{1,0},{2,1},{3,2},{4,7},{5,4},{6,5},{7,6},{8,11},{9,8},{10,9... | collective-permute-start | bytes 589832 | tf_op jit(solution)/shard_map/ppermute | solution.py:34
  75.9 0.2 collective-permute-start.37
  76.2 0.4 collective-permute-start.36
  76.6 7.0 %collective-permute-done.38.rest_3_ = bf16[96,1024]{1,0:T(8,128)(2,1)S(1)} collective-permute-done((bf16[96,1024]{1,0:T(8,128)(2,1)S(1)}, bf16[96,1024]{1,0:T(8,128)(2,1)S(1)}, u32[]{:S(2)}, u32[]{:S(2)}) %collective-permute-start.38) | collective-permute-done | bytes 196640 | tf_op jit(solution)/shard_map/ppermute | solution.py:34
  83.6 0.0 collective-permute-done.37.rest_2_
  83.6 4.7 %collective-permute-done.36.rest_1_ = bf16[96,1024]{1,0:T(8,128)(2,1)S(1)} collective-permute-done((bf16[96,1024]{1,0:T(8,128)(2,1)S(1)}, bf16[96,1024]{1,0:T(8,128)(2,1)S(1)}, u32[]{:S(2)}, u32[]{:S(2)}) %collective-permute-start.36) | collective-permute-done | bytes 196640 | tf_op jit(solution)/shard_map/ppermute | solution.py:34
  88.3 0.9 %shard_map.111 = bf16[96,4096]{1,0:T(8,128)(2,1)} custom-call(s32[1]{0:T(128)S(6)} %select_n.196.y_ref, bf16[96,1024]{1,0:T(8,128)(2,1)S(1)} %add_convert_fusion.rest_0_, bf16[96,1024]{1,0:T(8,128)(2,1)S(1)} %collective-permute-done.36.rest_1_, bf16[96,1024]{1,0:T(8,128)(2,1)S(1)} %collective-permute-done.37.rest_2_, ...), custom_call_target="tpu_custom_call" | custom-call | tf_op jit(solution)/shard_map/pallas_call | solution.py:256
  (9 shorter events, 0.1 us)
Async XLA Ops:
  0.0 45.5 %copy-start.5 = (f32[96,128]{1,0:T(8,128)S(1)}, f32[96,128]{1,0:T(8,128)}, u32[]{:S(2)}) copy-start(f32[96,128]{1,0:T(8,128)} %constant.149.clone.sin_ref) | copy-start | bytes 147460
  0.0 45.5 %copy-start.6 = (f32[96,128]{1,0:T(8,128)S(1)}, f32[96,128]{1,0:T(8,128)}, u32[]{:S(2)}) copy-start(f32[96,128]{1,0:T(8,128)} %constant.148.clone.cos_ref) | copy-start | bytes 147460
  0.0 45.5 %copy-start.4 = (bf16[3,32,4096]{2,1,0:T(8,128)(2,1)S(1)}, bf16[3,32,4096]{2,1,0:T(8,128)(2,1)}, u32[]{:S(2)}) copy-start(bf16[3,32,4096]{2,1,0:T(8,128)(2,1)} %param.19) | copy-start | bytes 2359300
  0.0 36.7 %copy-start.11 = (bf16[4096]{0:T(1024)(128)(2,1)S(1)}, bf16[4096]{0:T(1024)(128)(2,1)}, u32[]{:S(2)}) copy-start(bf16[4096]{0:T(1024)(128)(2,1)} %param.20) | copy-start | bytes 24580
  0.0 45.4 %copy-start.3 = (bf16[4096,128]{1,0:T(8,128)(2,1)S(1)}, bf16[4096,128]{1,0:T(8,128)(2,1)}, u32[]{:S(2)}) copy-start(bf16[4096,128]{1,0:T(8,128)(2,1)} %wv_ref.1) | copy-start | bytes 3145732
  0.0 45.4 %copy-start.2 = (bf16[4096,128]{1,0:T(8,128)(2,1)S(1)}, bf16[4096,128]{1,0:T(8,128)(2,1)}, u32[]{:S(2)}) copy-start(bf16[4096,128]{1,0:T(8,128)(2,1)} %wk_ref.1) | copy-start | bytes 3145732
  0.0 2.5 %collective-permute-start.24 = (bf16[2048,128]{1,0:T(8,128)(2,1)}, bf16[2048,128]{1,0:T(8,128)(2,1)S(1)}, u32[]{:S(2)}, u32[]{:S(2)}) collective-permute-start(bf16[2048,128]{1,0:T(8,128)(2,1)} %bitcast.14), channel_id=1, source_target_pairs={{0,8},{1,9},{2,10},{3,11},{4,12},{5,13},{6,14},{7,15},{8,0},{9,1},... | collective-permute-start | bytes 1572872 | tf_op jit(solution)/shard_map/ppermute | solution.py:34
  4.4 2.7 %collective-permute-start.6 = (bf16[512,128]{1,0:T(8,128)(2,1)}, bf16[512,128]{1,0:T(8,128)(2,1)S(1)}, u32[]{:S(2)}, u32[]{:S(2)}) collective-permute-start(bf16[512,128]{1,0:T(8,128)(2,1)} %get-tuple-element.82), channel_id=1, source_target_pairs={{128,64},{129,65},{130,66},{131,67},{132,68},{133,69},{134,70},{13... | collective-permute-start | bytes 393224 | tf_op jit(solution)/shard_map/cond/branch_2_fun/ppermute | solution.py:34
  5.1 2.0 %collective-permute-start.7 = (bf16[512,128]{1,0:T(8,128)(2,1)}, bf16[512,128]{1,0:T(8,128)(2,1)S(1)}, u32[]{:S(2)}, u32[]{:S(2)}) collective-permute-start(bf16[512,128]{1,0:T(8,128)(2,1)} %get-tuple-element.83), channel_id=1, source_target_pairs={{128,192},{129,193},{130,194},{131,195},{132,196},{133,197},{134,1... | collective-permute-start | bytes 393224 | tf_op jit(solution)/shard_map/cond/branch_2_fun/ppermute | solution.py:34
  5.7 11.1 %collective-permute-start.8 = (bf16[512,128]{1,0:T(8,128)(2,1)}, bf16[512,128]{1,0:T(8,128)(2,1)S(1)}, u32[]{:S(2)}, u32[]{:S(2)}) collective-permute-start(bf16[512,128]{1,0:T(8,128)(2,1)} %get-tuple-element.84), channel_id=1, source_target_pairs={{128,0},{129,1},{130,2},{131,3},{132,4},{133,5},{134,6},{135,7},{1... | collective-permute-start | bytes 393224 | tf_op jit(solution)/shard_map/cond/branch_2_fun/ppermute | solution.py:34
  16.9 0.7 copy-start.9
  18.5 2.7 %collective-permute-start.20 = (bf16[512,128]{1,0:T(8,128)(2,1)S(1)}, bf16[512,128]{1,0:T(8,128)(2,1)S(1)}, u32[]{:S(2)}, u32[]{:S(2)}) collective-permute-start(bf16[512,128]{1,0:T(8,128)(2,1)S(1)} %get-tuple-element.96), channel_id=1, source_target_pairs={{32,0},{33,1},{34,2},{35,3},{36,4},{37,5},{38,6},{39,7},{40,8},{41... | collective-permute-start | bytes 393224 | tf_op jit(solution)/shard_map/cond/branch_2_fun/ppermute | solution.py:34
  19.2 2.0 %collective-permute-start.19 = (bf16[512,128]{1,0:T(8,128)(2,1)S(1)}, bf16[512,128]{1,0:T(8,128)(2,1)S(1)}, u32[]{:S(2)}, u32[]{:S(2)}) collective-permute-start(bf16[512,128]{1,0:T(8,128)(2,1)S(1)} %get-tuple-element.96), channel_id=1, source_target_pairs={{32,48},{33,49},{34,50},{35,51},{36,52},{37,53},{38,54},{39,55},{4... | collective-permute-start | bytes 393224 | tf_op jit(solution)/shard_map/cond/branch_2_fun/ppermute | solution.py:34
  19.9 14.3 %collective-permute-start.18 = (bf16[512,128]{1,0:T(8,128)(2,1)S(1)}, bf16[512,128]{1,0:T(8,128)(2,1)}, u32[]{:S(2)}, u32[]{:S(2)}) collective-permute-start(bf16[512,128]{1,0:T(8,128)(2,1)S(1)} %get-tuple-element.96), channel_id=1, source_target_pairs={{32,16},{33,17},{34,18},{35,19},{36,20},{37,21},{38,22},{39,23},{4... | collective-permute-start | bytes 393224 | tf_op jit(solution)/shard_map/cond/branch_2_fun/ppermute | solution.py:34
  35.1 5.5 %collective-permute-start.27 = (bf16[512,128]{1,0:T(8,128)(2,1)S(1)}, bf16[512,128]{1,0:T(8,128)(2,1)S(1)}, u32[]{:S(2)}, u32[]{:S(2)}) collective-permute-start(bf16[512,128]{1,0:T(8,128)(2,1)S(1)} %get-tuple-element.122.rest_0_), channel_id=1, source_target_pairs={{0,128},{1,129},{2,130},{3,131},{4,132},{5,133},{6,134},{7,135},{8... | collective-permute-start | bytes 393224 | tf_op jit(solution)/shard_map/ppermute | solution.py:34
  35.2 8.9 %collective-permute-start.26 = (bf16[512,128]{1,0:T(8,128)(2,1)S(1)}, bf16[512,128]{1,0:T(8,128)(2,1)S(1)}, u32[]{:S(2)}, u32[]{:S(2)}) collective-permute-start(bf16[512,128]{1,0:T(8,128)(2,1)S(1)} %get-tuple-element.122.rest_0_), channel_id=1, source_target_pairs={{0,192},{1,193},{2,194},{3,195},{4,196},{5,197},{6,198},{7,199},{8... | collective-permute-start | bytes 393224 | tf_op jit(solution)/shard_map/ppermute | solution.py:34
  35.3 9.3 %collective-permute-start.25 = (bf16[512,128]{1,0:T(8,128)(2,1)S(1)}, bf16[512,128]{1,0:T(8,128)(2,1)S(1)}, u32[]{:S(2)}, u32[]{:S(2)}) collective-permute-start(bf16[512,128]{1,0:T(8,128)(2,1)S(1)} %get-tuple-element.122.rest_0_), channel_id=1, source_target_pairs={{0,64},{1,65},{2,66},{3,67},{4,68},{5,69},{6,70},{7,71},{8,72},{9,... | collective-permute-start | bytes 393224 | tf_op jit(solution)/shard_map/ppermute | solution.py:34
  36.7 14.0 %collective-permute-start.28 = (bf16[512,128]{1,0:T(8,128)(2,1)S(1)}, bf16[512,128]{1,0:T(8,128)(2,1)S(1)}, u32[]{:S(2)}, u32[]{:S(2)}) collective-permute-start(bf16[512,128]{1,0:T(8,128)(2,1)S(1)} %get-tuple-element.122.rest_0_), channel_id=1, source_target_pairs={{0,8},{1,9},{2,10},{3,11},{4,12},{5,13},{6,14},{7,15},{8,0},{9,1},... | collective-permute-start | bytes 393224 | tf_op jit(solution)/shard_map/ppermute | solution.py:34
  40.6 10.1 %collective-permute-start.31 = (bf16[512,128]{1,0:T(8,128)(2,1)S(1)}, bf16[512,128]{1,0:T(8,128)(2,1)S(1)}, u32[]{:S(2)}, u32[]{:S(2)}) collective-permute-start(bf16[512,128]{1,0:T(8,128)(2,1)S(1)} %collective-permute-done.27.rest_3_), channel_id=1, source_target_pairs={{0,8},{1,9},{2,10},{3,11},{4,12},{5,13},{6,14},{7,15},{8,0},{9,1},... | collective-permute-start | bytes 393224 | tf_op jit(solution)/shard_map/ppermute | solution.py:34
  44.0 6.7 %collective-permute-start.30 = (bf16[512,128]{1,0:T(8,128)(2,1)S(1)}, bf16[512,128]{1,0:T(8,128)(2,1)S(1)}, u32[]{:S(2)}, u32[]{:S(2)}) collective-permute-start(bf16[512,128]{1,0:T(8,128)(2,1)S(1)} %collective-permute-done.26.rest_2_), channel_id=1, source_target_pairs={{0,8},{1,9},{2,10},{3,11},{4,12},{5,13},{6,14},{7,15},{8,0},{9,1},... | collective-permute-start | bytes 393224 | tf_op jit(solution)/shard_map/ppermute | solution.py:34
  44.6 6.2 %collective-permute-start.29 = (bf16[512,128]{1,0:T(8,128)(2,1)S(1)}, bf16[512,128]{1,0:T(8,128)(2,1)S(1)}, u32[]{:S(2)}, u32[]{:S(2)}) collective-permute-start(bf16[512,128]{1,0:T(8,128)(2,1)S(1)} %collective-permute-done.25.rest_1_), channel_id=1, source_target_pairs={{0,8},{1,9},{2,10},{3,11},{4,12},{5,13},{6,14},{7,15},{8,0},{9,1},... | collective-permute-start | bytes 393224 | tf_op jit(solution)/shard_map/ppermute | solution.py:34
  45.5 2.2 %copy-start = (bf16[4096,512]{1,0:T(8,128)(2,1)S(1)}, bf16[4096,512]{1,0:T(8,128)(2,1)}, u32[]{:S(2)}) copy-start(bf16[4096,512]{1,0:T(8,128)(2,1)} %wq_ref.1) | copy-start | bytes 12582916
  47.7 3.1 %copy-start.1 = (bf16[512,4096]{1,0:T(8,128)(2,1)S(1)}, bf16[512,4096]{1,0:T(8,128)(2,1)}, u32[]{:S(2)}) copy-start(bf16[512,4096]{1,0:T(8,128)(2,1)} %o_ref.1) | copy-start | bytes 12582916
  54.3 8.1 %collective-permute-start.32 = (bf16[96,1024]{1,0:T(8,128)(2,1)S(1)}, bf16[96,1024]{1,0:T(8,128)(2,1)S(1)}, u32[]{:S(2)}, u32[]{:S(2)}) collective-permute-start(bf16[96,1024]{1,0:T(8,128)(2,1)S(1)} %get-tuple-element.114), channel_id=1, source_target_pairs={{0,2},{1,3},{2,0},{3,1},{4,6},{5,7},{6,4},{7,5},{8,10},{9,11},{10,... | collective-permute-start | bytes 589832 | tf_op jit(solution)/shard_map/ppermute | solution.py:34
  57.3 9.7 %collective-permute-start.33 = (bf16[96,1024]{1,0:T(8,128)(2,1)S(1)}, bf16[96,1024]{1,0:T(8,128)(2,1)S(1)}, u32[]{:S(2)}, u32[]{:S(2)}) collective-permute-start(bf16[96,1024]{1,0:T(8,128)(2,1)S(1)} %get-tuple-element.115), channel_id=1, source_target_pairs={{0,1},{1,2},{2,3},{3,0},{4,5},{5,6},{6,7},{7,4},{8,9},{9,10},{10,1... | collective-permute-start | bytes 589832 | tf_op jit(solution)/shard_map/ppermute | solution.py:34
  57.7 9.3 %collective-permute-start.34 = (bf16[96,1024]{1,0:T(8,128)(2,1)S(1)}, bf16[96,1024]{1,0:T(8,128)(2,1)S(1)}, u32[]{:S(2)}, u32[]{:S(2)}) collective-permute-start(bf16[96,1024]{1,0:T(8,128)(2,1)S(1)} %get-tuple-element.116), channel_id=1, source_target_pairs={{0,3},{1,0},{2,1},{3,2},{4,7},{5,4},{6,5},{7,6},{8,11},{9,8},{10,9... | collective-permute-start | bytes 589832 | tf_op jit(solution)/shard_map/ppermute | solution.py:34
  67.1 5.7 %collective-permute-start.35 = (bf16[96,1024]{1,0:T(8,128)(2,1)S(1)}, bf16[96,1024]{1,0:T(8,128)(2,1)S(1)}, u32[]{:S(2)}, u32[]{:S(2)}) collective-permute-start(bf16[96,1024]{1,0:T(8,128)(2,1)S(1)} %add_convert_fusion.1), channel_id=1, source_target_pairs={{0,4},{1,5},{2,6},{3,7},{4,0},{5,1},{6,2},{7,3},{8,12},{9,13},{10,... | collective-permute-start | bytes 589832 | tf_op jit(solution)/shard_map/ppermute | solution.py:34
  72.8 10.7 %collective-permute-start.38 = (bf16[96,1024]{1,0:T(8,128)(2,1)S(1)}, bf16[96,1024]{1,0:T(8,128)(2,1)S(1)}, u32[]{:S(2)}, u32[]{:S(2)}) collective-permute-start(bf16[96,1024]{1,0:T(8,128)(2,1)S(1)} %add_convert_fusion.rest_0_), channel_id=1, source_target_pairs={{0,3},{1,0},{2,1},{3,2},{4,7},{5,4},{6,5},{7,6},{8,11},{9,8},{10,9... | collective-permute-start | bytes 589832 | tf_op jit(solution)/shard_map/ppermute | solution.py:34
  75.9 7.6 %collective-permute-start.37 = (bf16[96,1024]{1,0:T(8,128)(2,1)S(1)}, bf16[96,1024]{1,0:T(8,128)(2,1)S(1)}, u32[]{:S(2)}, u32[]{:S(2)}) collective-permute-start(bf16[96,1024]{1,0:T(8,128)(2,1)S(1)} %add_convert_fusion.rest_0_), channel_id=1, source_target_pairs={{0,2},{1,3},{2,0},{3,1},{4,6},{5,7},{6,4},{7,5},{8,10},{9,11},{10,... | collective-permute-start | bytes 589832 | tf_op jit(solution)/shard_map/ppermute | solution.py:34
  76.2 12.1 %collective-permute-start.36 = (bf16[96,1024]{1,0:T(8,128)(2,1)S(1)}, bf16[96,1024]{1,0:T(8,128)(2,1)S(1)}, u32[]{:S(2)}, u32[]{:S(2)}) collective-permute-start(bf16[96,1024]{1,0:T(8,128)(2,1)S(1)} %add_convert_fusion.rest_0_), channel_id=1, source_target_pairs={{0,1},{1,2},{2,3},{3,0},{4,5},{5,6},{6,7},{7,4},{8,9},{9,10},{10,1... | collective-permute-start | bytes 589832 | tf_op jit(solution)/shard_map/ppermute | solution.py:34
where the time goes:
time: 90.7 us; the launch traced here: 89.2 us
  waiting for transfers between devices  50.6 us (56%)
  starting transfers between devices  23.1 us (25%)
  Pallas kernels  7.45 us (8%)
  local copies, waits for them, and re-layouts  3.62 us (4%)
  other arithmetic  3.2 us (4%)
  between operations  1.04 us (1%)
    ppermute x21, waiting for transfers between devices, send(): return lax.ppermute(block, AXES, pairs)  50.6 us
    ppermute x21, starting transfers between devices, send(): return lax.ppermute(block, AXES, pairs)  23.1 us
    pallas_call x1, Pallas kernels, attend(): pl.pallas_call(kernel, in_specs=[pl.BlockSpec(memory_space=pltpu.SMEM)] +...  3.5 us
    pallas_call x1, Pallas kernels, project(): pl.pallas_call(kernel, grid=(feature_dim // depth,), in_specs=[whole(rows...  3.02 us
    unnamed x16, local copies, waits for them, and re-layouts  2.21 us
    select_n x2, other arithmetic, run(): mine = jnp.where(at_place == (place + d) % size, got, mine)  1.86 us
  transfers between devices with their start and end apart: 21, of which 10 were waited for; matrix products, arithmetic and copies ran while one was open for 0% of the time, Pallas kernels for 3%

commit v1 on v0

--- a/solution.py
+++ b/solution.py
@@ -7,6 +7,7 @@
 from jax.sharding import PartitionSpec as P
 
 HD = 128
+PARTS = 2
 
 
 epsilon = 1e-05
@@ -34,18 +35,18 @@
     return lax.ppermute(block, AXES, pairs)
 
 
-def from_owner(pieces, at_place, root_place, size, only):
-    def branch(place):
-        def run(pieces):
-            mine = pieces[0]
+def over_rows(piece, zh, root_zh):
+    def branch(from_zh):
+        def run(piece):
+            mine = piece
             for d in (2, 1, 3):
-                got = only(pieces[d], d, place)
-                mine = jnp.where(at_place == (place + d) % size, got, mine)
+                got = send(piece, dzh=d, only=lambda x, zh, core: zh == from_zh)
+                mine = jnp.where(zh == (from_zh + d) % N_ZH, got, mine)
             return mine
 
         return run
 
-    return lax.switch(root_place, [branch(a) for a in range(size)], pieces)
+    return lax.switch(root_zh, [branch(a) for a in range(N_ZH)], piece)
 
 
 def broadcast(keys, values, root):
@@ -53,13 +54,18 @@
     core, zh, x = me % N_CORE, me // N_CORE % N_ZH, me // (N_CORE * N_ZH)
     root_core, root_zh, root_x = root % N_CORE, root // N_CORE % N_ZH, root // (N_CORE * N_ZH)
     has_keys = core == root_core
-    held = jnp.where(has_keys, keys, send(values, dcore=1))
+    got_values = send(values, dcore=1)
     quarter = keys.shape[0] // N_X
-    slabs = [held[d * quarter : (d + 1) * quarter] for d in range(N_X)]
-    along_x = lambda a, d, place: send(a, dx=d, only=lambda x, zh, core: x == place)
-    along_z = lambda a, d, place: send(a, dzh=d, only=lambda x, zh, core: zh == place)
-    mine = from_owner(slabs, x, root_x, N_X, along_x)
-    mine = from_owner([mine] * N_ZH, zh, root_zh, N_ZH, along_z)
+
+    def slab(d):
+        part = slice(d * quarter, (d + 1) * quarter)
+        return jnp.where(has_keys, keys[part], got_values[part])
+
+    got = {d: send(slab(d), dx=d) for d in (2, 1, 3)}
+    mine = slab(0)
+    for d in (2, 1, 3):
+        mine = jnp.where((x - root_x) % N_X == d, got[d], mine)
+    mine = over_rows(mine, zh, root_zh)
     return mine, has_keys
 
 
@@ -156,13 +162,13 @@
     heads, rows, head_dim = queries.shape
     samples = rows // step_count
     features = o_weight.shape[1]
-    width = features // N_Y
+    width = features // (N_Y * PARTS)
     scale = head_dim**-0.5
     pieces, positions = len(row), row[0].shape[0]
 
     def kernel(place_ref, q_ref, k_ref, v_ref, o_ref, *rest):
         row_refs, other_refs, rest = rest[:pieces], rest[pieces : 2 * pieces], rest[2 * pieces :]
-        out_refs, (keys, values, scores) = rest[:N_Y], rest[N_Y:]
+        out_refs, (keys, values, scores) = rest[: PARTS * N_Y], rest[PARTS * N_Y :]
 
         @pl.when(place_ref[1] == 1)
         def _():
@@ -209,18 +215,18 @@
                 numerator += e.astype(jnp.bfloat16).astype(jnp.float32) * values_of[u]
             attended.append((numerator / denominator).astype(jnp.bfloat16))
         attended = jnp.concatenate(attended, axis=1)
-        for d in (2, 1, 3, 0):
-            column = lax.rem(place_ref[0] + d, N_Y) * width
+        for i in range(PARTS * N_Y):
+            column = lax.rem(place_ref[0] + i % N_Y, N_Y) * (PARTS * width) + i // N_Y * width
             o_block = o_ref[:, pl.ds(pl.multiple_of(column, width), width)]
-            out_refs[d][...] = jnp.dot(attended, o_block, preferred_element_type=jnp.float32).astype(jnp.bfloat16)
+            out_refs[i][...] = jnp.dot(attended, o_block, preferred_element_type=jnp.float32).astype(jnp.bfloat16)
 
     place = jnp.stack([lax.axis_index("tp") % N_Y, has_keys.astype(jnp.int32)])
     vmem = pl.BlockSpec(memory_space=pltpu.VMEM)
     return pl.pallas_call(
         kernel,
         in_specs=[pl.BlockSpec(memory_space=pltpu.SMEM)] + [vmem] * (4 + 2 * pieces),
-        out_specs=[vmem] * N_Y,
-        out_shape=[jax.ShapeDtypeStruct((rows, width), jnp.bfloat16)] * N_Y,
+        out_specs=[vmem] * (PARTS * N_Y),
+        out_shape=[jax.ShapeDtypeStruct((rows, width), jnp.bfloat16)] * (PARTS * N_Y),
         scratch_shapes=[
             pltpu.VMEM((pieces, positions, head_dim), jnp.bfloat16),
             pltpu.VMEM((pieces, positions, head_dim), jnp.bfloat16),
@@ -235,31 +241,34 @@
     )(place, queries, new_keys, new_values, o_weight, *row, *other)
 
 
-def add_up(blocks):
-    got = [blocks[0]] + [send(blocks[d], dy=d) for d in (2, 1, 3)]
-    along_y = sum(a.astype(jnp.float32) for a in got).astype(jnp.bfloat16)
-    across = send(along_y, dzl=1)
-    block = (along_y.astype(jnp.float32) + across.astype(jnp.float32)).astype(jnp.bfloat16)
-    return [block] + [send(block, dy=d) for d in (1, 2, 3)]
-
-
-def lay_out(blocks):
-    rows, width = blocks[0].shape
+def add_up(parts):
+    got = [[blocks[0]] + [send(blocks[d], dy=d) for d in (1, 2, 3)] for blocks in parts]
+    along_y = [sum(a.astype(jnp.float32) for a in terms).astype(jnp.bfloat16) for terms in got]
+    across = [send(a, dzl=1) for a in along_y]
+    blocks = [
+        (a.astype(jnp.float32) + b.astype(jnp.float32)).astype(jnp.bfloat16)
+        for a, b in zip(along_y, across)
+    ]
+    return [[block] + [send(block, dy=d) for d in (1, 2, 3)] for block in blocks]
+
+
+def lay_out(parts):
+    rows, width = parts[0][0].shape
 
     def kernel(y_ref, *rest):
-        ins, out = rest[:N_Y], rest[N_Y]
-        for d in range(N_Y):
-            column = lax.rem(y_ref[0] + N_Y - d, N_Y) * width
-            out[:, pl.ds(pl.multiple_of(column, width), width)] = ins[d][...]
+        ins, out = rest[: PARTS * N_Y], rest[PARTS * N_Y]
+        for i in range(PARTS * N_Y):
+            column = lax.rem(y_ref[0] + N_Y - i % N_Y, N_Y) * (PARTS * width) + i // N_Y * width
+            out[:, pl.ds(pl.multiple_of(column, width), width)] = ins[i][...]
 
     vmem = pl.BlockSpec(memory_space=pltpu.VMEM)
     return pl.pallas_call(
         kernel,
-        in_specs=[pl.BlockSpec(memory_space=pltpu.SMEM)] + [vmem] * N_Y,
+        in_specs=[pl.BlockSpec(memory_space=pltpu.SMEM)] + [vmem] * (PARTS * N_Y),
         out_specs=vmem,
-        out_shape=jax.ShapeDtypeStruct((rows, N_Y * width), blocks[0].dtype),
+        out_shape=jax.ShapeDtypeStruct((rows, PARTS * N_Y * width), parts[0][0].dtype),
         compiler_params=pltpu.CompilerParams(vmem_limit_bytes=8 * 2**20),
-    )(lax.axis_index("tp").reshape(1) % N_Y, *blocks)
+    )(lax.axis_index("tp").reshape(1) % N_Y, *[block for blocks in parts for block in blocks])
 
 
 def on_device(
@@ -281,7 +290,7 @@
         new_states, attn_gain, q_weight, k_weight, v_weight, prompt_keys.shape[1]
     )
     partial_blocks = attend(queries, new_keys, new_values, row, other, has_keys, o_weight, step_count)
-    summed = lay_out(add_up(partial_blocks))
+    summed = lay_out(add_up([partial_blocks[i * N_Y : (i + 1) * N_Y] for i in range(PARTS)]))
     return summed.reshape(step_count, samples, o_weight.shape[1])
 
 

time: 90.7 us -> 83.1 us (0.916)
  the two profiles are of different devices: /device:TPU:65 before, /device:TPU:32 now
where the time goes in v1:
time: 83.1 us; the launch traced here: 82 us
  waiting for transfers between devices  36.2 us (44%)
  starting transfers between devices  31.8 us (38%)
  Pallas kernels  7.48 us (9%)
  other arithmetic  3.26 us (4%)
  local copies, waits for them, and re-layouts  2.23 us (3%)
  between operations  1.03 us (1%)
    ppermute x28, waiting for transfers between devices, send(): return lax.ppermute(block, AXES, pairs)  36.2 us
    ppermute x28, starting transfers between devices, send(): return lax.ppermute(block, AXES, pairs)  31.8 us
    pallas_call x1, Pallas kernels, attend(): pl.pallas_call(kernel, in_specs=[pl.BlockSpec(memory_space=pltpu.SMEM)] +...  3.52 us
    pallas_call x1, Pallas kernels, project(): pl.pallas_call(kernel, grid=(feature_dim // depth,), in_specs=[whole(rows...  3.02 us
    unnamed x18, local copies, waits for them, and re-layouts  2.21 us
    select_n x1, other arithmetic, slab(): return jnp.where(has_keys, keys[part], got_values[part])  1.98 us
  transfers between devices with their start and end apart: 28, of which 16 were waited for; matrix products, arithmetic and copies ran while one was open for 0% of the time, Pallas kernels for 4%

profile of v1, /device:TPU:32, one launch (start us, length us, event | category | flops | bytes accessed | tf_op | source)
XLA Modules:
  0.0 82.0 jit_solution(3946805512615898697)
XLA Ops:
  0.0 0.1 collective-permute-start.12
  1.0 1.3 %collective-permute-done.12 = bf16[2048,128]{1,0:T(8,128)(2,1)S(1)} collective-permute-done((bf16[2048,128]{1,0:T(8,128)(2,1)}, bf16[2048,128]{1,0:T(8,128)(2,1)S(1)}, u32[]{:S(2)}, u32[]{:S(2)}) %collective-permute-start.12) | collective-permute-done | bytes 524320 | tf_op jit(solution)/shard_map/ppermute | solution.py:35
  2.2 2.0 %slice_select_fusion.1 = (bf16[512,128]{1,0:T(8,128)(2,1)}, bf16[512,128]{1,0:T(8,128)(2,1)}, bf16[512,128]{1,0:T(8,128)(2,1)}) fusion(bf16[2048,128]{1,0:T(8,128)(2,1)S(1)} %collective-permute-done.12, bf16[1,2048,128]{2,1,0:T(8,128)(2,1)} %param.21, pred[]{:T(512)S(6)} %eq.59), kind=kLoop, calls=%fused_computation.12 | loop fusion | flops 196608 | bytes 1179649 | tf_op jit(solution)/shard_map/jit(_where)/select_n | solution.py:62
  4.2 3.0 %collective-permute-start.15 = (bf16[512,128]{1,0:T(8,128)(2,1)}, bf16[512,128]{1,0:T(8,128)(2,1)}, u32[]{:S(2)}, u32[]{:S(2)}) collective-permute-start(bf16[512,128]{1,0:T(8,128)(2,1)} %get-tuple-element.60), channel_id=1, source_target_pairs={{0,128},{1,129},{2,130},{3,131},{4,132},{5,133},{6,134},{7,135},{8... | collective-permute-start | bytes 393224 | tf_op jit(solution)/shard_map/ppermute | solution.py:35
  7.3 0.6 collective-permute-start.14
  7.9 2.6 %collective-permute-start.13 = (bf16[512,128]{1,0:T(8,128)(2,1)}, bf16[512,128]{1,0:T(8,128)(2,1)}, u32[]{:S(2)}, u32[]{:S(2)}) collective-permute-start(bf16[512,128]{1,0:T(8,128)(2,1)} %get-tuple-element.62), channel_id=1, source_target_pairs={{0,192},{1,193},{2,194},{3,195},{4,196},{5,197},{6,198},{7,199},{8... | collective-permute-start | bytes 393224 | tf_op jit(solution)/shard_map/ppermute | solution.py:35
  10.5 1.9 %collective-permute-done.15 = bf16[512,128]{1,0:T(8,128)(2,1)} collective-permute-done((bf16[512,128]{1,0:T(8,128)(2,1)}, bf16[512,128]{1,0:T(8,128)(2,1)}, u32[]{:S(2)}, u32[]{:S(2)}) %collective-permute-start.15) | collective-permute-done | bytes 131104 | tf_op jit(solution)/shard_map/ppermute | solution.py:35
  12.4 2.2 %collective-permute-done.14 = bf16[512,128]{1,0:T(8,128)(2,1)} collective-permute-done((bf16[512,128]{1,0:T(8,128)(2,1)}, bf16[512,128]{1,0:T(8,128)(2,1)}, u32[]{:S(2)}, u32[]{:S(2)}) %collective-permute-start.14) | collective-permute-done | bytes 131104 | tf_op jit(solution)/shard_map/ppermute | solution.py:35
  14.6 0.0 collective-permute-done.13
  14.6 1.0 %fusion.2 = bf16[512,128]{1,0:T(8,128)(2,1)S(1)} fusion(bf16[512,128]{1,0:T(8,128)(2,1)} %collective-permute-done.13, bf16[512,128]{1,0:T(8,128)(2,1)} %collective-permute-done.14, bf16[512,128]{1,0:T(8,128)(2,1)} %collective-permute-done.15, bf16[2048,128]{1,0:T(8,128)(2,1)} %copy-done.7, bf16[1,2048,128]{2,1,0:T(8,128)(2,1)} %param.21, pred[]{:T(512)S(6)} %eq.62, ...), kind=kLoop, calls=%fused_computation.11 | loop fusion | flops 262144 | bytes 786436 | tf_op jit(solution)/shard_map/jit(_where)/select_n | solution.py:67
  15.6 16.9 %conditional.1 = (bf16[512,128]{1,0:T(8,128)(2,1)S(1)}) conditional(s32[]{:T(128)} %clamp.3, (s32[]{:T(128)}, bf16[512,128]{1,0:T(8,128)(2,1)S(1)}) %tuple.18, (s32[]{:T(128)}, bf16[512,128]{1,0:T(8,128)(2,1)S(1)}) %tuple.18, (s32[]{:T(128)}, bf16[512,128]{1,0:T(8,128)(2,1)S(1)}) %tuple.18, (s32[]{:T(128)}, ...), branch_computations={%region_0.1_spmd, %region_1.2_spmd, %region_2.3_spmd, %region_3.4_... | conditional | flops 196611 | bytes 2228382 | solution.py:49
  15.7 0.7 collective-permute-start.11
  16.4 1.3 %collective-permute-start.10 = (bf16[512,128]{1,0:T(8,128)(2,1)S(1)}, bf16[512,128]{1,0:T(8,128)(2,1)S(1)}, u32[]{:S(2)}, u32[]{:S(2)}) collective-permute-start(bf16[512,128]{1,0:T(8,128)(2,1)S(1)} %get-tuple-element.33), channel_id=1, source_target_pairs={{48,0},{49,1},{50,2},{51,3},{52,4},{53,5},{54,6},{55,7},{56,8},{57... | collective-permute-start | bytes 393224 | tf_op jit(solution)/shard_map/cond/branch_3_fun/ppermute | solution.py:35
  17.7 1.3 %collective-permute-start.9 = (bf16[512,128]{1,0:T(8,128)(2,1)S(1)}, bf16[512,128]{1,0:T(8,128)(2,1)}, u32[]{:S(2)}, u32[]{:S(2)}) collective-permute-start(bf16[512,128]{1,0:T(8,128)(2,1)S(1)} %get-tuple-element.33), channel_id=1, source_target_pairs={{48,32},{49,33},{50,34},{51,35},{52,36},{53,37},{54,38},{55,39},{5... | collective-permute-start | bytes 393224 | tf_op jit(solution)/shard_map/cond/branch_3_fun/ppermute | solution.py:35
  19.0 0.0 collective-permute-done.11
  19.0 13.5 %collective-permute-done.10 = bf16[512,128]{1,0:T(8,128)(2,1)S(1)} collective-permute-done((bf16[512,128]{1,0:T(8,128)(2,1)S(1)}, bf16[512,128]{1,0:T(8,128)(2,1)S(1)}, u32[]{:S(2)}, u32[]{:S(2)}) %collective-permute-start.10) | collective-permute-done | bytes 131104 | tf_op jit(solution)/shard_map/cond/branch_3_fun/ppermute | solution.py:35
  32.5 0.0 collective-permute-done.9
  32.5 1.8 %collective-permute-start.18 = (bf16[512,128]{1,0:T(8,128)(2,1)S(1)}, bf16[512,128]{1,0:T(8,128)(2,1)S(1)}, u32[]{:S(2)}, u32[]{:S(2)}) collective-permute-start(bf16[512,128]{1,0:T(8,128)(2,1)S(1)} %get-tuple-element.63.rest_0_), channel_id=1, source_target_pairs={{0,128},{1,129},{2,130},{3,131},{4,132},{5,133},{6,134},{7,135},{8... | collective-permute-start | bytes 393224 | tf_op jit(solution)/shard_map/ppermute | solution.py:35
  34.4 2.7 %collective-permute-start.17 = (bf16[512,128]{1,0:T(8,128)(2,1)S(1)}, bf16[512,128]{1,0:T(8,128)(2,1)S(1)}, u32[]{:S(2)}, u32[]{:S(2)}) collective-permute-start(bf16[512,128]{1,0:T(8,128)(2,1)S(1)} %get-tuple-element.63.rest_0_), channel_id=1, source_target_pairs={{0,192},{1,193},{2,194},{3,195},{4,196},{5,197},{6,198},{7,199},{8... | collective-permute-start | bytes 393224 | tf_op jit(solution)/shard_map/ppermute | solution.py:35
  37.1 0.0 collective-permute-start.16
  37.1 0.1 collective-permute-start.19
  37.2 3.0 %collective-permute-done.18.rest_3_ = bf16[512,128]{1,0:T(8,128)(2,1)S(1)} collective-permute-done((bf16[512,128]{1,0:T(8,128)(2,1)S(1)}, bf16[512,128]{1,0:T(8,128)(2,1)S(1)}, u32[]{:S(2)}, u32[]{:S(2)}) %collective-permute-start.18) | collective-permute-done | bytes 131104 | tf_op jit(solution)/shard_map/ppermute | solution.py:35
  40.2 0.0 collective-permute-start.22
  40.2 2.0 %collective-permute-done.17.rest_2_ = bf16[512,128]{1,0:T(8,128)(2,1)S(1)} collective-permute-done((bf16[512,128]{1,0:T(8,128)(2,1)S(1)}, bf16[512,128]{1,0:T(8,128)(2,1)S(1)}, u32[]{:S(2)}, u32[]{:S(2)}) %collective-permute-start.17) | collective-permute-done | bytes 131104 | tf_op jit(solution)/shard_map/ppermute | solution.py:35
  42.2 0.0 collective-permute-start.21
  42.2 1.1 %collective-permute-done.16.rest_1_ = bf16[512,128]{1,0:T(8,128)(2,1)S(1)} collective-permute-done((bf16[512,128]{1,0:T(8,128)(2,1)S(1)}, bf16[512,128]{1,0:T(8,128)(2,1)S(1)}, u32[]{:S(2)}, u32[]{:S(2)}) %collective-permute-start.16) | collective-permute-done | bytes 131104 | tf_op jit(solution)/shard_map/ppermute | solution.py:35
  43.3 0.0 collective-permute-start.20
  43.3 0.1 pad_add_fusion.place_ref
  43.4 0.0 copy-start
  43.4 2.2 %copy-done = bf16[4096,512]{1,0:T(8,128)(2,1)S(1)} copy-done((bf16[4096,512]{1,0:T(8,128)(2,1)S(1)}, bf16[4096,512]{1,0:T(8,128)(2,1)}, u32[]{:S(2)}) %copy-start) | copy-done | bytes 4194328
  45.6 3.0 %shard_map.109 = (bf16[4,96,128]{2,1,0:T(8,128)(2,1)S(1)}, bf16[96,128]{1,0:T(8,128)(2,1)S(1)}, bf16[96,128]{1,0:T(8,128)(2,1)S(1)}) custom-call(bf16[96,4096]{1,0:T(8,128)(2,1)S(1)} %bitcast.19, bf16[1,4096]{1,0:T(2,128)(2,1)S(1)} %reshape.20.gain_ref, f32[96,128]{1,0:T(8,128)S(1)} %copy-done.6, f32[96,128]{1,0:T(8,128)S(1)} %copy-done.5, ...), custom_call_target="tpu_custom_call" | custom-call | flops 603979776 | bytes 7077888 | tf_op jit(solution)/shard_map/pallas_call | solution.py:122
  48.6 0.0 collective-permute-done.19.rest_4_
  48.6 0.0 collective-permute-done.21.rest_6_
  48.6 0.0 collective-permute-done.20.rest_5_
  48.6 3.5 %shard_map.110 = (bf16[96,512]{1,0:T(8,128)(2,1)S(1)}, bf16[96,512]{1,0:T(8,128)(2,1)S(1)}, bf16[96,512]{1,0:T(8,128)(2,1)S(1)}, bf16[96,512]{1,0:T(8,128)(2,1)S...) custom-call(s32[2]{0:T(128)S(1)} %pad_add_fusion.place_ref, ...), custom_call_target="tpu_custom_call" | custom-call | flops 1207959552 | bytes 5242880 | tf_op jit(solution)/shard_map/pallas_call | solution.py:225
  52.2 1.8 %collective-permute-start.23 = (bf16[96,512]{1,0:T(8,128)(2,1)S(1)}, bf16[96,512]{1,0:T(8,128)(2,1)S(1)}, u32[]{:S(2)}, u32[]{:S(2)}) collective-permute-start(bf16[96,512]{1,0:T(8,128)(2,1)S(1)} %get-tuple-element.53), channel_id=1, source_target_pairs={{0,1},{1,2},{2,3},{3,0},{4,5},{5,6},{6,7},{7,4},{8,9},{9,10},{10,1... | collective-permute-start | bytes 294920 | tf_op jit(solution)/shard_map/ppermute | solution.py:35
  54.0 2.9 %collective-permute-start.24 = (bf16[96,512]{1,0:T(8,128)(2,1)S(1)}, bf16[96,512]{1,0:T(8,128)(2,1)S(1)}, u32[]{:S(2)}, u32[]{:S(2)}) collective-permute-start(bf16[96,512]{1,0:T(8,128)(2,1)S(1)} %get-tuple-element.54), channel_id=1, source_target_pairs={{0,2},{1,3},{2,0},{3,1},{4,6},{5,7},{6,4},{7,5},{8,10},{9,11},{10,... | collective-permute-start | bytes 294920 | tf_op jit(solution)/shard_map/ppermute | solution.py:35
  56.9 1.3 %collective-permute-start.25 = (bf16[96,512]{1,0:T(8,128)(2,1)S(1)}, bf16[96,512]{1,0:T(8,128)(2,1)S(1)}, u32[]{:S(2)}, u32[]{:S(2)}) collective-permute-start(bf16[96,512]{1,0:T(8,128)(2,1)S(1)} %get-tuple-element.55), channel_id=1, source_target_pairs={{0,3},{1,0},{2,1},{3,2},{4,7},{5,4},{6,5},{7,6},{8,11},{9,8},{10,9... | collective-permute-start | bytes 294920 | tf_op jit(solution)/shard_map/ppermute | solution.py:35
  58.3 0.7 collective-permute-start.30
  58.9 0.8 collective-permute-start.31
  59.7 1.9 %collective-permute-start.32 = (bf16[96,512]{1,0:T(8,128)(2,1)S(1)}, bf16[96,512]{1,0:T(8,128)(2,1)S(1)}, u32[]{:S(2)}, u32[]{:S(2)}) collective-permute-start(bf16[96,512]{1,0:T(8,128)(2,1)S(1)} %get-tuple-element.59), channel_id=1, source_target_pairs={{0,3},{1,0},{2,1},{3,2},{4,7},{5,4},{6,5},{7,6},{8,11},{9,8},{10,9... | collective-permute-start | bytes 294920 | tf_op jit(solution)/shard_map/ppermute | solution.py:35
  61.6 1.0 %collective-permute-done.24 = bf16[96,512]{1,0:T(8,128)(2,1)S(1)} collective-permute-done((bf16[96,512]{1,0:T(8,128)(2,1)S(1)}, bf16[96,512]{1,0:T(8,128)(2,1)S(1)}, u32[]{:S(2)}, u32[]{:S(2)}) %collective-permute-start.24) | collective-permute-done | bytes 98336 | tf_op jit(solution)/shard_map/ppermute | solution.py:35
  62.6 0.0 collective-permute-done.25
  62.6 0.1 add_convert_fusion.3
  62.6 0.1 collective-permute-start.26
  62.7 1.9 %collective-permute-done.30 = bf16[96,512]{1,0:T(8,128)(2,1)S(1)} collective-permute-done((bf16[96,512]{1,0:T(8,128)(2,1)S(1)}, bf16[96,512]{1,0:T(8,128)(2,1)S(1)}, u32[]{:S(2)}, u32[]{:S(2)}) %collective-permute-start.30) | collective-permute-done | bytes 98336 | tf_op jit(solution)/shard_map/ppermute | solution.py:35
  64.7 1.7 %collective-permute-done.31 = bf16[96,512]{1,0:T(8,128)(2,1)S(1)} collective-permute-done((bf16[96,512]{1,0:T(8,128)(2,1)S(1)}, bf16[96,512]{1,0:T(8,128)(2,1)S(1)}, u32[]{:S(2)}, u32[]{:S(2)}) %collective-permute-start.31) | collective-permute-done | bytes 98336 | tf_op jit(solution)/shard_map/ppermute | solution.py:35
  66.4 0.2 collective-permute-done.32
  66.6 0.1 add_convert_fusion.1
  66.6 0.1 collective-permute-start.33
  66.7 0.6 collective-permute-done.26
  67.4 1.9 %collective-permute-start.29 = (bf16[96,512]{1,0:T(8,128)(2,1)S(1)}, bf16[96,512]{1,0:T(8,128)(2,1)S(1)}, u32[]{:S(2)}, u32[]{:S(2)}) collective-permute-start(bf16[96,512]{1,0:T(8,128)(2,1)S(1)} %add_convert_fusion.2.rest_0_), channel_id=1, source_target_pairs={{0,3},{1,0},{2,1},{3,2},{4,7},{5,4},{6,5},{7,6},{8,11},{9,8},{10,9... | collective-permute-start | bytes 294920 | tf_op jit(solution)/shard_map/ppermute | solution.py:35
  69.3 1.1 %collective-permute-start.28 = (bf16[96,512]{1,0:T(8,128)(2,1)S(1)}, bf16[96,512]{1,0:T(8,128)(2,1)S(1)}, u32[]{:S(2)}, u32[]{:S(2)}) collective-permute-start(bf16[96,512]{1,0:T(8,128)(2,1)S(1)} %add_convert_fusion.2.rest_0_), channel_id=1, source_target_pairs={{0,2},{1,3},{2,0},{3,1},{4,6},{5,7},{6,4},{7,5},{8,10},{9,11},{10,... | collective-permute-start | bytes 294920 | tf_op jit(solution)/shard_map/ppermute | solution.py:35
  70.4 1.3 %collective-permute-start.27 = (bf16[96,512]{1,0:T(8,128)(2,1)S(1)}, bf16[96,512]{1,0:T(8,128)(2,1)S(1)}, u32[]{:S(2)}, u32[]{:S(2)}) collective-permute-start(bf16[96,512]{1,0:T(8,128)(2,1)S(1)} %add_convert_fusion.2.rest_0_), channel_id=1, source_target_pairs={{0,1},{1,2},{2,3},{3,0},{4,5},{5,6},{6,7},{7,4},{8,9},{9,10},{10,1... | collective-permute-start | bytes 294920 | tf_op jit(solution)/shard_map/ppermute | solution.py:35
  71.8 0.0 collective-permute-done.33
  71.8 2.1 %collective-permute-start.36 = (bf16[96,512]{1,0:T(8,128)(2,1)S(1)}, bf16[96,512]{1,0:T(8,128)(2,1)S(1)}, u32[]{:S(2)}, u32[]{:S(2)}) collective-permute-start(bf16[96,512]{1,0:T(8,128)(2,1)S(1)} %add_convert_fusion.rest_4_), channel_id=1, source_target_pairs={{0,3},{1,0},{2,1},{3,2},{4,7},{5,4},{6,5},{7,6},{8,11},{9,8},{10,9... | collective-permute-start | bytes 294920 | tf_op jit(solution)/shard_map/ppermute | solution.py:35
  73.9 1.1 %collective-permute-start.35 = (bf16[96,512]{1,0:T(8,128)(2,1)S(1)}, bf16[96,512]{1,0:T(8,128)(2,1)S(1)}, u32[]{:S(2)}, u32[]{:S(2)}) collective-permute-start(bf16[96,512]{1,0:T(8,128)(2,1)S(1)} %add_convert_fusion.rest_4_), channel_id=1, source_target_pairs={{0,2},{1,3},{2,0},{3,1},{4,6},{5,7},{6,4},{7,5},{8,10},{9,11},{10,... | collective-permute-start | bytes 294920 | tf_op jit(solution)/shard_map/ppermute | solution.py:35
  75.0 0.0 collective-permute-done.29.rest_3_
  75.0 0.3 collective-permute-start.34
  75.3 0.6 collective-permute-done.28.rest_2_
  75.8 2.3 %collective-permute-done.27.rest_1_ = bf16[96,512]{1,0:T(8,128)(2,1)S(1)} collective-permute-done((bf16[96,512]{1,0:T(8,128)(2,1)S(1)}, bf16[96,512]{1,0:T(8,128)(2,1)S(1)}, u32[]{:S(2)}, u32[]{:S(2)}) %collective-permute-start.27) | collective-permute-done | bytes 98336 | tf_op jit(solution)/shard_map/ppermute | solution.py:35
  78.1 1.9 %collective-permute-done.35.rest_6_ = bf16[96,512]{1,0:T(8,128)(2,1)S(1)} collective-permute-done((bf16[96,512]{1,0:T(8,128)(2,1)S(1)}, bf16[96,512]{1,0:T(8,128)(2,1)S(1)}, u32[]{:S(2)}, u32[]{:S(2)}) %collective-permute-start.35) | collective-permute-done | bytes 98336 | tf_op jit(solution)/shard_map/ppermute | solution.py:35
  80.0 1.0 %collective-permute-done.34.rest_5_ = bf16[96,512]{1,0:T(8,128)(2,1)S(1)} collective-permute-done((bf16[96,512]{1,0:T(8,128)(2,1)S(1)}, bf16[96,512]{1,0:T(8,128)(2,1)S(1)}, u32[]{:S(2)}, u32[]{:S(2)}) %collective-permute-start.34) | collective-permute-done | bytes 98336 | tf_op jit(solution)/shard_map/ppermute | solution.py:35
  81.1 0.9 %shard_map.111 = bf16[96,4096]{1,0:T(8,128)(2,1)} custom-call(s32[1]{0:T(128)S(6)} %select_n.160.y_ref, bf16[96,512]{1,0:T(8,128)(2,1)S(1)} %add_convert_fusion.2.rest_0_, bf16[96,512]{1,0:T(8,128)(2,1)S(1)} %collective-permute-done.27.rest_1_, bf16[96,512]{1,0:T(8,128)(2,1)S(1)} %collective-permute-done.28.rest_2_, ...), custom_call_target="tpu_custom_call" | custom-call | tf_op jit(solution)/shard_map/pallas_call | solution.py:265
  (23 shorter events, 0.1 us)
Async XLA Ops:
  0.0 43.3 %copy-start.5 = (f32[96,128]{1,0:T(8,128)S(1)}, f32[96,128]{1,0:T(8,128)}, u32[]{:S(2)}) copy-start(f32[96,128]{1,0:T(8,128)} %constant.134.clone.sin_ref) | copy-start | bytes 147460
  0.0 43.3 %copy-start.6 = (f32[96,128]{1,0:T(8,128)S(1)}, f32[96,128]{1,0:T(8,128)}, u32[]{:S(2)}) copy-start(f32[96,128]{1,0:T(8,128)} %constant.133.clone.cos_ref) | copy-start | bytes 147460
  0.0 43.3 %copy-start.4 = (bf16[3,32,4096]{2,1,0:T(8,128)(2,1)S(1)}, bf16[3,32,4096]{2,1,0:T(8,128)(2,1)}, u32[]{:S(2)}) copy-start(bf16[3,32,4096]{2,1,0:T(8,128)(2,1)} %param.15) | copy-start | bytes 2359300
  0.0 37.1 %copy-start.8 = (bf16[4096]{0:T(1024)(128)(2,1)S(1)}, bf16[4096]{0:T(1024)(128)(2,1)}, u32[]{:S(2)}) copy-start(bf16[4096]{0:T(1024)(128)(2,1)} %param.16) | copy-start | bytes 24580
  0.0 43.3 %copy-start.3 = (bf16[4096,128]{1,0:T(8,128)(2,1)S(1)}, bf16[4096,128]{1,0:T(8,128)(2,1)}, u32[]{:S(2)}) copy-start(bf16[4096,128]{1,0:T(8,128)(2,1)} %wv_ref.1) | copy-start | bytes 3145732
  0.0 43.3 %copy-start.2 = (bf16[4096,128]{1,0:T(8,128)(2,1)S(1)}, bf16[4096,128]{1,0:T(8,128)(2,1)}, u32[]{:S(2)}) copy-start(bf16[4096,128]{1,0:T(8,128)(2,1)} %wk_ref.1) | copy-start | bytes 3145732
  0.0 2.2 %collective-permute-start.12 = (bf16[2048,128]{1,0:T(8,128)(2,1)}, bf16[2048,128]{1,0:T(8,128)(2,1)S(1)}, u32[]{:S(2)}, u32[]{:S(2)}) collective-permute-start(bf16[2048,128]{1,0:T(8,128)(2,1)} %bitcast.20), channel_id=1, source_target_pairs={{0,8},{1,9},{2,10},{3,11},{4,12},{5,13},{6,14},{7,15},{8,0},{9,1},... | collective-permute-start | bytes 1572872 | tf_op jit(solution)/shard_map/ppermute | solution.py:35
  2.2 12.4 %copy-start.7 = (bf16[2048,128]{1,0:T(8,128)(2,1)}, bf16[2048,128]{1,0:T(8,128)(2,1)S(1)}, u32[]{:S(2)}) copy-start(bf16[2048,128]{1,0:T(8,128)(2,1)S(1)} %collective-permute-done.12) | copy-start | bytes 1572868
  4.2 8.2 %collective-permute-start.15 = (bf16[512,128]{1,0:T(8,128)(2,1)}, bf16[512,128]{1,0:T(8,128)(2,1)}, u32[]{:S(2)}, u32[]{:S(2)}) collective-permute-start(bf16[512,128]{1,0:T(8,128)(2,1)} %get-tuple-element.60), channel_id=1, source_target_pairs={{0,128},{1,129},{2,130},{3,131},{4,132},{5,133},{6,134},{7,135},{8... | collective-permute-start | bytes 393224 | tf_op jit(solution)/shard_map/ppermute | solution.py:35
  7.3 7.4 %collective-permute-start.14 = (bf16[512,128]{1,0:T(8,128)(2,1)}, bf16[512,128]{1,0:T(8,128)(2,1)}, u32[]{:S(2)}, u32[]{:S(2)}) collective-permute-start(bf16[512,128]{1,0:T(8,128)(2,1)} %get-tuple-element.61), channel_id=1, source_target_pairs={{0,64},{1,65},{2,66},{3,67},{4,68},{5,69},{6,70},{7,71},{8,72},{9,... | collective-permute-start | bytes 393224 | tf_op jit(solution)/shard_map/ppermute | solution.py:35
  7.9 6.8 %collective-permute-start.13 = (bf16[512,128]{1,0:T(8,128)(2,1)}, bf16[512,128]{1,0:T(8,128)(2,1)}, u32[]{:S(2)}, u32[]{:S(2)}) collective-permute-start(bf16[512,128]{1,0:T(8,128)(2,1)} %get-tuple-element.62), channel_id=1, source_target_pairs={{0,192},{1,193},{2,194},{3,195},{4,196},{5,197},{6,198},{7,199},{8... | collective-permute-start | bytes 393224 | tf_op jit(solution)/shard_map/ppermute | solution.py:35
  15.7 3.3 %collective-permute-start.11 = (bf16[512,128]{1,0:T(8,128)(2,1)S(1)}, bf16[512,128]{1,0:T(8,128)(2,1)S(1)}, u32[]{:S(2)}, u32[]{:S(2)}) collective-permute-start(bf16[512,128]{1,0:T(8,128)(2,1)S(1)} %get-tuple-element.33), channel_id=1, source_target_pairs={{48,16},{49,17},{50,18},{51,19},{52,20},{53,21},{54,22},{55,23},{5... | collective-permute-start | bytes 393224 | tf_op jit(solution)/shard_map/cond/branch_3_fun/ppermute | solution.py:35
  16.4 16.1 %collective-permute-start.10 = (bf16[512,128]{1,0:T(8,128)(2,1)S(1)}, bf16[512,128]{1,0:T(8,128)(2,1)S(1)}, u32[]{:S(2)}, u32[]{:S(2)}) collective-permute-start(bf16[512,128]{1,0:T(8,128)(2,1)S(1)} %get-tuple-element.33), channel_id=1, source_target_pairs={{48,0},{49,1},{50,2},{51,3},{52,4},{53,5},{54,6},{55,7},{56,8},{57... | collective-permute-start | bytes 393224 | tf_op jit(solution)/shard_map/cond/branch_3_fun/ppermute | solution.py:35
  17.7 14.8 %collective-permute-start.9 = (bf16[512,128]{1,0:T(8,128)(2,1)S(1)}, bf16[512,128]{1,0:T(8,128)(2,1)}, u32[]{:S(2)}, u32[]{:S(2)}) collective-permute-start(bf16[512,128]{1,0:T(8,128)(2,1)S(1)} %get-tuple-element.33), channel_id=1, source_target_pairs={{48,32},{49,33},{50,34},{51,35},{52,36},{53,37},{54,38},{55,39},{5... | collective-permute-start | bytes 393224 | tf_op jit(solution)/shard_map/cond/branch_3_fun/ppermute | solution.py:35
  32.5 7.7 %collective-permute-start.18 = (bf16[512,128]{1,0:T(8,128)(2,1)S(1)}, bf16[512,128]{1,0:T(8,128)(2,1)S(1)}, u32[]{:S(2)}, u32[]{:S(2)}) collective-permute-start(bf16[512,128]{1,0:T(8,128)(2,1)S(1)} %get-tuple-element.63.rest_0_), channel_id=1, source_target_pairs={{0,128},{1,129},{2,130},{3,131},{4,132},{5,133},{6,134},{7,135},{8... | collective-permute-start | bytes 393224 | tf_op jit(solution)/shard_map/ppermute | solution.py:35
  34.4 7.8 %collective-permute-start.17 = (bf16[512,128]{1,0:T(8,128)(2,1)S(1)}, bf16[512,128]{1,0:T(8,128)(2,1)S(1)}, u32[]{:S(2)}, u32[]{:S(2)}) collective-permute-start(bf16[512,128]{1,0:T(8,128)(2,1)S(1)} %get-tuple-element.63.rest_0_), channel_id=1, source_target_pairs={{0,192},{1,193},{2,194},{3,195},{4,196},{5,197},{6,198},{7,199},{8... | collective-permute-start | bytes 393224 | tf_op jit(solution)/shard_map/ppermute | solution.py:35
  37.1 6.2 %collective-permute-start.16 = (bf16[512,128]{1,0:T(8,128)(2,1)S(1)}, bf16[512,128]{1,0:T(8,128)(2,1)S(1)}, u32[]{:S(2)}, u32[]{:S(2)}) collective-permute-start(bf16[512,128]{1,0:T(8,128)(2,1)S(1)} %get-tuple-element.63.rest_0_), channel_id=1, source_target_pairs={{0,64},{1,65},{2,66},{3,67},{4,68},{5,69},{6,70},{7,71},{8,72},{9,... | collective-permute-start | bytes 393224 | tf_op jit(solution)/shard_map/ppermute | solution.py:35
  37.1 11.5 %collective-permute-start.19 = (bf16[512,128]{1,0:T(8,128)(2,1)S(1)}, bf16[512,128]{1,0:T(8,128)(2,1)S(1)}, u32[]{:S(2)}, u32[]{:S(2)}) collective-permute-start(bf16[512,128]{1,0:T(8,128)(2,1)S(1)} %get-tuple-element.63.rest_0_), channel_id=1, source_target_pairs={{0,8},{1,9},{2,10},{3,11},{4,12},{5,13},{6,14},{7,15},{8,0},{9,1},... | collective-permute-start | bytes 393224 | tf_op jit(solution)/shard_map/ppermute | solution.py:35
  40.2 8.4 %collective-permute-start.22 = (bf16[512,128]{1,0:T(8,128)(2,1)S(1)}, bf16[512,128]{1,0:T(8,128)(2,1)S(1)}, u32[]{:S(2)}, u32[]{:S(2)}) collective-permute-start(bf16[512,128]{1,0:T(8,128)(2,1)S(1)} %collective-permute-done.18.rest_3_), channel_id=1, source_target_pairs={{0,8},{1,9},{2,10},{3,11},{4,12},{5,13},{6,14},{7,15},{8,0},{9,1},... | collective-permute-start | bytes 393224 | tf_op jit(solution)/shard_map/ppermute | solution.py:35
  42.2 6.4 %collective-permute-start.21 = (bf16[512,128]{1,0:T(8,128)(2,1)S(1)}, bf16[512,128]{1,0:T(8,128)(2,1)S(1)}, u32[]{:S(2)}, u32[]{:S(2)}) collective-permute-start(bf16[512,128]{1,0:T(8,128)(2,1)S(1)} %collective-permute-done.17.rest_2_), channel_id=1, source_target_pairs={{0,8},{1,9},{2,10},{3,11},{4,12},{5,13},{6,14},{7,15},{8,0},{9,1},... | collective-permute-start | bytes 393224 | tf_op jit(solution)/shard_map/ppermute | solution.py:35
  43.3 5.4 %collective-permute-start.20 = (bf16[512,128]{1,0:T(8,128)(2,1)S(1)}, bf16[512,128]{1,0:T(8,128)(2,1)S(1)}, u32[]{:S(2)}, u32[]{:S(2)}) collective-permute-start(bf16[512,128]{1,0:T(8,128)(2,1)S(1)} %collective-permute-done.16.rest_1_), channel_id=1, source_target_pairs={{0,8},{1,9},{2,10},{3,11},{4,12},{5,13},{6,14},{7,15},{8,0},{9,1},... | collective-permute-start | bytes 393224 | tf_op jit(solution)/shard_map/ppermute | solution.py:35
  43.4 2.2 %copy-start = (bf16[4096,512]{1,0:T(8,128)(2,1)S(1)}, bf16[4096,512]{1,0:T(8,128)(2,1)}, u32[]{:S(2)}) copy-start(bf16[4096,512]{1,0:T(8,128)(2,1)} %wq_ref.1) | copy-start | bytes 12582916
  45.6 3.1 %copy-start.1 = (bf16[512,4096]{1,0:T(8,128)(2,1)S(1)}, bf16[512,4096]{1,0:T(8,128)(2,1)}, u32[]{:S(2)}) copy-start(bf16[512,4096]{1,0:T(8,128)(2,1)} %o_ref.1) | copy-start | bytes 12582916
  52.2 7.6 %collective-permute-start.23 = (bf16[96,512]{1,0:T(8,128)(2,1)S(1)}, bf16[96,512]{1,0:T(8,128)(2,1)S(1)}, u32[]{:S(2)}, u32[]{:S(2)}) collective-permute-start(bf16[96,512]{1,0:T(8,128)(2,1)S(1)} %get-tuple-element.53), channel_id=1, source_target_pairs={{0,1},{1,2},{2,3},{3,0},{4,5},{5,6},{6,7},{7,4},{8,9},{9,10},{10,1... | collective-permute-start | bytes 294920 | tf_op jit(solution)/shard_map/ppermute | solution.py:35
  54.0 8.6 %collective-permute-start.24 = (bf16[96,512]{1,0:T(8,128)(2,1)S(1)}, bf16[96,512]{1,0:T(8,128)(2,1)S(1)}, u32[]{:S(2)}, u32[]{:S(2)}) collective-permute-start(bf16[96,512]{1,0:T(8,128)(2,1)S(1)} %get-tuple-element.54), channel_id=1, source_target_pairs={{0,2},{1,3},{2,0},{3,1},{4,6},{5,7},{6,4},{7,5},{8,10},{9,11},{10,... | collective-permute-start | bytes 294920 | tf_op jit(solution)/shard_map/ppermute | solution.py:35
  56.9 5.7 %collective-permute-start.25 = (bf16[96,512]{1,0:T(8,128)(2,1)S(1)}, bf16[96,512]{1,0:T(8,128)(2,1)S(1)}, u32[]{:S(2)}, u32[]{:S(2)}) collective-permute-start(bf16[96,512]{1,0:T(8,128)(2,1)S(1)} %get-tuple-element.55), channel_id=1, source_target_pairs={{0,3},{1,0},{2,1},{3,2},{4,7},{5,4},{6,5},{7,6},{8,11},{9,8},{10,9... | collective-permute-start | bytes 294920 | tf_op jit(solution)/shard_map/ppermute | solution.py:35
  58.3 6.4 %collective-permute-start.30 = (bf16[96,512]{1,0:T(8,128)(2,1)S(1)}, bf16[96,512]{1,0:T(8,128)(2,1)S(1)}, u32[]{:S(2)}, u32[]{:S(2)}) collective-permute-start(bf16[96,512]{1,0:T(8,128)(2,1)S(1)} %get-tuple-element.57), channel_id=1, source_target_pairs={{0,1},{1,2},{2,3},{3,0},{4,5},{5,6},{6,7},{7,4},{8,9},{9,10},{10,1... | collective-permute-start | bytes 294920 | tf_op jit(solution)/shard_map/ppermute | solution.py:35
  58.9 7.5 %collective-permute-start.31 = (bf16[96,512]{1,0:T(8,128)(2,1)S(1)}, bf16[96,512]{1,0:T(8,128)(2,1)S(1)}, u32[]{:S(2)}, u32[]{:S(2)}) collective-permute-start(bf16[96,512]{1,0:T(8,128)(2,1)S(1)} %get-tuple-element.58), channel_id=1, source_target_pairs={{0,2},{1,3},{2,0},{3,1},{4,6},{5,7},{6,4},{7,5},{8,10},{9,11},{10,... | collective-permute-start | bytes 294920 | tf_op jit(solution)/shard_map/ppermute | solution.py:35
  59.7 6.8 %collective-permute-start.32 = (bf16[96,512]{1,0:T(8,128)(2,1)S(1)}, bf16[96,512]{1,0:T(8,128)(2,1)S(1)}, u32[]{:S(2)}, u32[]{:S(2)}) collective-permute-start(bf16[96,512]{1,0:T(8,128)(2,1)S(1)} %get-tuple-element.59), channel_id=1, source_target_pairs={{0,3},{1,0},{2,1},{3,2},{4,7},{5,4},{6,5},{7,6},{8,11},{9,8},{10,9... | collective-permute-start | bytes 294920 | tf_op jit(solution)/shard_map/ppermute | solution.py:35
  62.6 4.7 %collective-permute-start.26 = (bf16[96,512]{1,0:T(8,128)(2,1)S(1)}, bf16[96,512]{1,0:T(8,128)(2,1)S(1)}, u32[]{:S(2)}, u32[]{:S(2)}) collective-permute-start(bf16[96,512]{1,0:T(8,128)(2,1)S(1)} %add_convert_fusion.3), channel_id=1, source_target_pairs={{0,4},{1,5},{2,6},{3,7},{4,0},{5,1},{6,2},{7,3},{8,12},{9,13},{10,... | collective-permute-start | bytes 294920 | tf_op jit(solution)/shard_map/ppermute | solution.py:35
  66.6 5.1 %collective-permute-start.33 = (bf16[96,512]{1,0:T(8,128)(2,1)S(1)}, bf16[96,512]{1,0:T(8,128)(2,1)S(1)}, u32[]{:S(2)}, u32[]{:S(2)}) collective-permute-start(bf16[96,512]{1,0:T(8,128)(2,1)S(1)} %add_convert_fusion.1), channel_id=1, source_target_pairs={{0,4},{1,5},{2,6},{3,7},{4,0},{5,1},{6,2},{7,3},{8,12},{9,13},{10,... | collective-permute-start | bytes 294920 | tf_op jit(solution)/shard_map/ppermute | solution.py:35
  67.4 7.6 %collective-permute-start.29 = (bf16[96,512]{1,0:T(8,128)(2,1)S(1)}, bf16[96,512]{1,0:T(8,128)(2,1)S(1)}, u32[]{:S(2)}, u32[]{:S(2)}) collective-permute-start(bf16[96,512]{1,0:T(8,128)(2,1)S(1)} %add_convert_fusion.2.rest_0_), channel_id=1, source_target_pairs={{0,3},{1,0},{2,1},{3,2},{4,7},{5,4},{6,5},{7,6},{8,11},{9,8},{10,9... | collective-permute-start | bytes 294920 | tf_op jit(solution)/shard_map/ppermute | solution.py:35
  69.3 6.5 %collective-permute-start.28 = (bf16[96,512]{1,0:T(8,128)(2,1)S(1)}, bf16[96,512]{1,0:T(8,128)(2,1)S(1)}, u32[]{:S(2)}, u32[]{:S(2)}) collective-permute-start(bf16[96,512]{1,0:T(8,128)(2,1)S(1)} %add_convert_fusion.2.rest_0_), channel_id=1, source_target_pairs={{0,2},{1,3},{2,0},{3,1},{4,6},{5,7},{6,4},{7,5},{8,10},{9,11},{10,... | collective-permute-start | bytes 294920 | tf_op jit(solution)/shard_map/ppermute | solution.py:35
  70.4 7.7 %collective-permute-start.27 = (bf16[96,512]{1,0:T(8,128)(2,1)S(1)}, bf16[96,512]{1,0:T(8,128)(2,1)S(1)}, u32[]{:S(2)}, u32[]{:S(2)}) collective-permute-start(bf16[96,512]{1,0:T(8,128)(2,1)S(1)} %add_convert_fusion.2.rest_0_), channel_id=1, source_target_pairs={{0,1},{1,2},{2,3},{3,0},{4,5},{5,6},{6,7},{7,4},{8,9},{9,10},{10,1... | collective-permute-start | bytes 294920 | tf_op jit(solution)/shard_map/ppermute | solution.py:35
  71.8 6.3 %collective-permute-start.36 = (bf16[96,512]{1,0:T(8,128)(2,1)S(1)}, bf16[96,512]{1,0:T(8,128)(2,1)S(1)}, u32[]{:S(2)}, u32[]{:S(2)}) collective-permute-start(bf16[96,512]{1,0:T(8,128)(2,1)S(1)} %add_convert_fusion.rest_4_), channel_id=1, source_target_pairs={{0,3},{1,0},{2,1},{3,2},{4,7},{5,4},{6,5},{7,6},{8,11},{9,8},{10,9... | collective-permute-start | bytes 294920 | tf_op jit(solution)/shard_map/ppermute | solution.py:35
  73.9 6.1 %collective-permute-start.35 = (bf16[96,512]{1,0:T(8,128)(2,1)S(1)}, bf16[96,512]{1,0:T(8,128)(2,1)S(1)}, u32[]{:S(2)}, u32[]{:S(2)}) collective-permute-start(bf16[96,512]{1,0:T(8,128)(2,1)S(1)} %add_convert_fusion.rest_4_), channel_id=1, source_target_pairs={{0,2},{1,3},{2,0},{3,1},{4,6},{5,7},{6,4},{7,5},{8,10},{9,11},{10,... | collective-permute-start | bytes 294920 | tf_op jit(solution)/shard_map/ppermute | solution.py:35
  75.0 6.1 %collective-permute-start.34 = (bf16[96,512]{1,0:T(8,128)(2,1)S(1)}, bf16[96,512]{1,0:T(8,128)(2,1)S(1)}, u32[]{:S(2)}, u32[]{:S(2)}) collective-permute-start(bf16[96,512]{1,0:T(8,128)(2,1)S(1)} %add_convert_fusion.rest_4_), channel_id=1, source_target_pairs={{0,1},{1,2},{2,3},{3,0},{4,5},{5,6},{6,7},{7,4},{8,9},{9,10},{10,1... | collective-permute-start | bytes 294920 | tf_op jit(solution)/shard_map/ppermute | solution.py:35

commit v2 on v1

v2 whole, which is shorter than its diff:
```python
import jax
import jax.numpy as jnp
import numpy as np
from jax import lax
from jax.experimental import pallas as pl
from jax.experimental.pallas import tpu as pltpu
from jax.sharding import PartitionSpec as P

HD = 128
PARTS = 2
BRING_GRANT = 16
QKV_GRANT = 56
ROW_ORDER = (2, 3, 1)


epsilon = 1e-05

AXES = ("inst", "tp")
N_X, N_ZH, N_CORE = 4, 4, 2
N_ZL, N_Y = 2, 4


def at(x, zh, core, zl, y):
    inst = (x % N_X * N_ZH + zh % N_ZH) * N_CORE + core % N_CORE
    return inst * (N_ZL * N_Y) + zl % N_ZL * N_Y + y % N_Y


def send(block, dx=0, dzh=0, dcore=0, dzl=0, dy=0, only=lambda x, zh, core: True):
    pairs = [
        (at(x, zh, core, zl, y), at(x + dx, zh + dzh, core + dcore, zl + dzl, y + dy))
        for x in range(N_X)
        for zh in range(N_ZH)
        for core in range(N_CORE)
        for zl in range(N_ZL)
        for y in range(N_Y)
        if only(x, zh, core)
    ]
    return lax.ppermute(block, AXES, pairs)


VMEM = pl.BlockSpec(memory_space=pltpu.VMEM)
SMEM = pl.BlockSpec(memory_space=pltpu.SMEM)


def pick(pieces, index):
    def kernel(index_ref, *refs):
        for d, ref in enumerate(refs[:-1]):

            @pl.when(index_ref[0] == d)
            def _():
                refs[-1][...] = ref[...]

    return pl.pallas_call(
        kernel,
        in_specs=[SMEM] + [VMEM] * len(pieces),
        out_specs=VMEM,
        out_shape=jax.ShapeDtypeStruct(pieces[0].shape, pieces[0].dtype),
        compiler_params=pltpu.CompilerParams(vmem_limit_bytes=4 * 2**20),
    )(index.reshape(1), *pieces)


def slabs_of(first, keys, values):
    size, width = keys.shape[0] // N_X, keys.shape[1]

    def kernel(first_ref, keys_ref, values_ref, *slabs):
        for want, ref in ((1, keys_ref), (0, values_ref)):

            @pl.when(first_ref[0] == want)
            def _():
                for d in range(N_X):
                    slabs[d][...] = ref[d * size : (d + 1) * size]

    return pl.pallas_call(
        kernel,
        in_specs=[SMEM, VMEM, VMEM],
        out_specs=[VMEM] * N_X,
        out_shape=[jax.ShapeDtypeStruct((size, width), keys.dtype)] * N_X,
        compiler_params=pltpu.CompilerParams(vmem_limit_bytes=4 * 2**20),
    )(first.astype(jnp.int32).reshape(1), keys, values)


def over_rows(piece, zh, root_zh):
    def branch(from_zh):
        def run(piece):
            only = lambda x, zh, core: zh == from_zh
            got = {d: send(piece, dzh=d, only=only) for d in ROW_ORDER}
            place = sum(((from_zh + d) % N_ZH == zh) * (i + 1) for i, d in enumerate(ROW_ORDER))
            return pick([piece] + [got[d] for d in ROW_ORDER], place)

        return run

    return lax.switch(root_zh, [branch(a) for a in range(N_ZH)], piece)


def broadcast(keys, values, root, gain, beside):
    me = lax.axis_index("inst")
    core, zh, x = me % N_CORE, me // N_CORE % N_ZH, me // (N_CORE * N_ZH)
    root_core, root_zh, root_x = root % N_CORE, root // N_CORE % N_ZH, root // (N_CORE * N_ZH)
    has_keys = core == root_core
    got_values, gain = lax.optimization_barrier((send(values, dcore=1), gain.reshape(1, -1)))
    slabs = slabs_of(has_keys, keys, got_values)
    got = [slabs[0]] + [send(slabs[d], dx=d) for d in (1, 2, 3)]
    got, result = lax.optimization_barrier((got, beside(gain)))
    mine = pick(got, (x - root_x) % N_X)
    return over_rows(mine, zh, root_zh), has_keys, result


def from_row(mine, projected, o_weight):
    row = [mine] + [send(mine, dx=dx) for dx in (1, 3, 2)]
    other = [send(a, dcore=1) for a in row]
    row, projected, o_weight = lax.optimization_barrier((row, projected, o_weight))
    other, ready = lax.optimization_barrier((other, bring_in(projected, o_weight)))
    return row, other, ready


def bring_in(small, weight):
    chunks = 8
    size = weight.shape[0] // chunks

    def kernel(*refs):
        small_ref, weight_hbm, small_out, weight_out, sems = refs
        gets = [
            pltpu.make_async_copy(weight_hbm.at[pl.ds(i * size, size), :], weight_out.at[pl.ds(i * size, size), :], sems.at[i])
            for i in range(chunks)
        ]
        for get in gets:
            get.start()
        small_out[...] = small_ref[...]
        for get in gets:
            get.wait()

    return pl.pallas_call(
        kernel,
        in_specs=[VMEM, pl.BlockSpec(memory_space=pl.ANY)],
        out_specs=[VMEM] * 2,
        out_shape=[jax.ShapeDtypeStruct(a.shape, a.dtype) for a in (small, weight)],
        scratch_shapes=[pltpu.SemaphoreType.DMA((chunks,))],
        compiler_params=pltpu.CompilerParams(vmem_limit_bytes=BRING_GRANT * 2**20),
        cost_estimate=pl.CostEstimate(flops=0, bytes_accessed=2 * weight.size, transcendentals=0),
    )(small, weight)


def project(new_states, attn_gain, q_weight, k_weight, v_weight, prompt_len):
    step_count, samples, feature_dim = new_states.shape
    rows = step_count * samples
    q_width, head_dim = q_weight.shape[1], k_weight.shape[1]
    heads, half = q_width // head_dim, head_dim // 2
    depth = 512
    frequency = np.exp(-np.arange(half) * (np.log(500000.0) / half))
    angles = (prompt_len + np.repeat(np.arange(step_count), samples))[:, None] * frequency
    cosine = np.concatenate([np.cos(angles)] * 2, axis=1).astype(np.float32)
    sine = np.concatenate([-np.sin(angles), np.sin(angles)], axis=1).astype(np.float32)

    chunks = feature_dim // depth

    def kernel(x_hbm, gain_ref, cos_ref, sin_ref, wq_hbm, wk_hbm, wv_hbm, out_ref, x, wq, wk, wv, acc, sems):
        get_x = pltpu.make_async_copy(x_hbm, x, sems.at[0, chunks])
        get_x.start()
        gets = []
        for i in range(chunks):
            part = pl.ds(i * depth, depth)
            gets.append(
                [
                    pltpu.make_async_copy(hbm.at[part, :], ref.at[part, :], sems.at[j, i])
                    for j, (hbm, ref) in enumerate(((wq_hbm, wq), (wk_hbm, wk), (wv_hbm, wv)))
                ]
            )
            for get in gets[-1]:
                get.start()
        get_x.wait()
        squares = jnp.zeros((rows, 1), jnp.float32)
        for i in range(chunks):
            states = x[:, i * depth : (i + 1) * depth].astype(jnp.float32)
            squares += jnp.sum(states * states, axis=-1, keepdims=True)
        inv = lax.rsqrt(squares / feature_dim + epsilon)
        for i in range(chunks):
            part = slice(i * depth, (i + 1) * depth)
            states = x[:, part].astype(jnp.float32)
            gain = gain_ref[:, part].astype(jnp.float32)
            normed = (states * inv * gain).astype(jnp.bfloat16)
            at_column = 0
            for get, w in zip(gets[i], (wq, wk, wv)):
                get.wait()
                columns = slice(at_column, at_column + w.shape[1])
                product = jnp.dot(normed, w[part, :], preferred_element_type=jnp.float32)
                if i == 0:
                    acc[:, columns] = product
                else:
                    acc[:, columns] += product
                at_column += w.shape[1]

        def rotated(block):
            swapped = pltpu.roll(block, half, 1)
            return (block * cos_ref[...] + swapped * sin_ref[...]).astype(jnp.bfloat16)

        for head in range(heads):
            out_ref[head] = rotated(acc[:, head * head_dim : (head + 1) * head_dim])
        out_ref[heads] = rotated(acc[:, q_width : q_width + head_dim])
        out_ref[heads + 1] = acc[:, q_width + head_dim :].astype(jnp.bfloat16)

    anywhere = pl.BlockSpec(memory_space=pl.ANY)
    return pl.pallas_call(
        kernel,
        in_specs=[anywhere, VMEM, VMEM, VMEM, anywhere, anywhere, anywhere],
        out_specs=VMEM,
        out_shape=jax.ShapeDtypeStruct((heads + 2, rows, head_dim), jnp.bfloat16),
        scratch_shapes=[
            pltpu.VMEM((rows, feature_dim), jnp.bfloat16),
            pltpu.VMEM((feature_dim, q_width), jnp.bfloat16),
            pltpu.VMEM((feature_dim, head_dim), jnp.bfloat16),
            pltpu.VMEM((feature_dim, head_dim), jnp.bfloat16),
            pltpu.VMEM((rows, q_width + 2 * head_dim), jnp.float32),
            pltpu.SemaphoreType.DMA((3, chunks + 1)),
        ],
        compiler_params=pltpu.CompilerParams(vmem_limit_bytes=QKV_GRANT * 2**20),
        cost_estimate=pl.CostEstimate(
            flops=2 * rows * feature_dim * (q_width + 2 * head_dim),
            bytes_accessed=2 * feature_dim * (rows + q_width + 2 * head_dim),
            transcendentals=0,
        ),
    )(
        new_states.reshape(rows, feature_dim),
        attn_gain,
        cosine,
        sine,
        q_weight,
        k_weight,
        v_weight,
    )


def attend(projected, row, other, has_keys, o_weight, step_count):
    heads, rows, head_dim = projected.shape[0] - 2, *projected.shape[1:]
    samples = rows // step_count
    features = o_weight.shape[1]
    width = features // (N_Y * PARTS)
    scale = head_dim**-0.5
    pieces, positions = len(row), row[0].shape[0]

    def kernel(place_ref, qkv_ref, o_ref, *rest):
        row_refs, other_refs, rest = rest[:pieces], rest[pieces : 2 * pieces], rest[2 * pieces :]
        out_refs, (keys, values, scores) = rest[: PARTS * N_Y], rest[PARTS * N_Y :]

        @pl.when(place_ref[1] == 1)
        def _():
            for p in range(pieces):
                keys[p], values[p] = row_refs[p][...], other_refs[p][...]

        @pl.when(place_ref[1] == 0)
        def _():
            for p in range(pieces):
                keys[p], values[p] = other_refs[p][...], row_refs[p][...]

        step_of = lax.broadcasted_iota(jnp.int32, (rows, 1), 0) // samples
        keys_of = [jnp.concatenate([qkv_ref[heads, u * samples : (u + 1) * samples]] * step_count, axis=0).astype(jnp.float32) for u in range(step_count)]
        values_of = [jnp.concatenate([qkv_ref[heads + 1, u * samples : (u + 1) * samples]] * step_count, axis=0).astype(jnp.float32) for u in range(step_count)]
        q_all = qkv_ref[:heads].reshape(heads * rows, head_dim)
        row_max = None
        for i in range(pieces):
            s = lax.dot_general(q_all, keys[i], (((1,), (1,)), ((), ())), preferred_element_type=jnp.float32)
            scores[i] = s
            top = jnp.max(s, axis=1, keepdims=True)
            row_max = top if row_max is None else jnp.maximum(row_max, top)
        row_sum = jnp.zeros((heads * rows, 1), jnp.float32)
        weighted = jnp.zeros((heads * rows, head_dim), jnp.float32)
        for i in range(pieces):
            e = jnp.exp2((scores[i] - row_max) * (scale * np.log2(np.e)))
            row_sum += jnp.sum(e, axis=1, keepdims=True)
            weighted += jnp.dot(e.astype(jnp.bfloat16), values[i], preferred_element_type=jnp.float32)
        row_max = row_max * scale
        attended = []
        for head in range(heads):
            part = slice(head * rows, (head + 1) * rows)
            q32 = qkv_ref[head].astype(jnp.float32)
            joint_max, own = row_max[part], []
            for u in range(step_count):
                s = jnp.sum(q32 * keys_of[u], axis=1, keepdims=True) * scale
                s = jnp.where(step_of >= u, s, -1e30)
                joint_max = jnp.maximum(joint_max, s)
                own.append(s)
            rescale = jnp.exp(row_max[part] - joint_max)
            denominator = row_sum[part] * rescale
            numerator = weighted[part] * rescale
            for u in range(step_count):
                e = jnp.where(step_of >= u, jnp.exp(own[u] - joint_max), 0.0)
                denominator += e
                numerator += e.astype(jnp.bfloat16).astype(jnp.float32) * values_of[u]
            attended.append((numerator / denominator).astype(jnp.bfloat16))
        attended = jnp.concatenate(attended, axis=1)
        for i in range(PARTS * N_Y):
            column = lax.rem(place_ref[0] + i % N_Y, N_Y) * (PARTS * width) + i // N_Y * width
            o_block = o_ref[:, pl.ds(pl.multiple_of(column, width), width)]
            out_refs[i][...] = jnp.dot(attended, o_block, preferred_element_type=jnp.float32).astype(jnp.bfloat16)

    place = jnp.stack([lax.axis_index("tp") % N_Y, has_keys.astype(jnp.int32)])
    vmem = pl.BlockSpec(memory_space=pltpu.VMEM)
    return pl.pallas_call(
        kernel,
        in_specs=[pl.BlockSpec(memory_space=pltpu.SMEM)] + [vmem] * (2 + 2 * pieces),
        out_specs=[vmem] * (PARTS * N_Y),
        out_shape=[jax.ShapeDtypeStruct((rows, width), jnp.bfloat16)] * (PARTS * N_Y),
        scratch_shapes=[
            pltpu.VMEM((pieces, positions, head_dim), jnp.bfloat16),
            pltpu.VMEM((pieces, positions, head_dim), jnp.bfloat16),
            pltpu.VMEM((pieces, heads * rows, positions), jnp.float32),
        ],
        compiler_params=pltpu.CompilerParams(vmem_limit_bytes=24 * 2**20),
        cost_estimate=pl.CostEstimate(
            flops=2 * rows * features * o_weight.shape[0] + 8 * heads * rows * pieces * positions * head_dim,
            bytes_accessed=2 * o_weight.size + 4 * pieces * row[0].size,
            transcendentals=0,
        ),
    )(place, projected, o_weight, *row, *other)


def add_up(parts):
    got = [[blocks[0]] + [send(blocks[d], dy=d) for d in (1, 2, 3)] for blocks in parts]
    along_y = [sum(a.astype(jnp.float32) for a in terms).astype(jnp.bfloat16) for terms in got]
    across = [send(a, dzl=1) for a in along_y]
    blocks = [
        (a.astype(jnp.float32) + b.astype(jnp.float32)).astype(jnp.bfloat16)
        for a, b in zip(along_y, across)
    ]
    return [[block] + [send(block, dy=d) for d in (1, 2, 3)] for block in blocks]


def lay_out(parts):
    rows, width = parts[0][0].shape

    def kernel(y_ref, *rest):
        ins, out = rest[: PARTS * N_Y], rest[PARTS * N_Y]
        for i in range(PARTS * N_Y):
            column = lax.rem(y_ref[0] + N_Y - i % N_Y, N_Y) * (PARTS * width) + i // N_Y * width
            out[:, pl.ds(pl.multiple_of(column, width), width)] = ins[i][...]

    vmem = pl.BlockSpec(memory_space=pltpu.VMEM)
    return pl.pallas_call(
        kernel,
        in_specs=[pl.BlockSpec(memory_space=pltpu.SMEM)] + [vmem] * (PARTS * N_Y),
        out_specs=vmem,
        out_shape=jax.ShapeDtypeStruct((rows, PARTS * N_Y * width), parts[0][0].dtype),
        compiler_params=pltpu.CompilerParams(vmem_limit_bytes=8 * 2**20),
    )(lax.axis_index("tp").reshape(1) % N_Y, *[block for blocks in parts for block in blocks])


def on_device(
    new_states,
    attn_gain,
    q_weight,
    k_weight,
    v_weight,
    o_weight,
    prompt_keys,
    prompt_values,
    owner_index,
):
    step_count, samples, _ = new_states.shape
    project_all = lambda gain: project(
        new_states, gain, q_weight, k_weight, v_weight, prompt_keys.shape[1]
    )
    piece, has_keys, projected = broadcast(
        prompt_keys[0], prompt_values[0], owner_index[0], attn_gain, project_all
    )
    row, other, (projected, o_near) = from_row(piece, projected, o_weight)
    partial_blocks = attend(projected, row, other, has_keys, o_near, step_count)
    summed = lay_out(add_up([partial_blocks[i * N_Y : (i + 1) * N_Y] for i in range(PARTS)]))
    return summed.reshape(step_count, samples, o_weight.shape[1])


def solution(mesh):
    placed = (
        P(None, "inst", None),
        P(),
        P(None, "tp"),
        P(None, "tp"),
        P(None, "tp"),
        P("tp", None),
        P("inst", None, "tp"),
        P("inst", None, "tp"),
        P(),
    )
    return jax.shard_map(
        on_device, mesh=mesh, in_specs=placed, out_specs=P(None, "inst", None), check_vma=False
    )
```

time: 83.1 us -> 79.2 us (0.953); the launches traced: 82 us -> 79.4 us
  waiting for transfers between devices: 36.2 us -> 16.3 us
  starting transfers between devices: 31.8 us -> 44.7 us
  Pallas kernels: 7.48 us -> 11.8 us
  local copies, waits for them, and re-layouts: 2.23 us -> 5.44 us
  other arithmetic: 3.26 us -> 0.24 us
    ppermute x28, waiting for transfers between devices: 36.2 us -> 16.3 us  [send(): return lax.ppermute(block, AXES, pairs)]
    ppermute x28, starting transfers between devices: 31.8 us -> 44.7 us  [send(): return lax.ppermute(block, AXES, pairs)]
    pallas_call x1 -> x5, Pallas kernels: 3.02 us -> 7.34 us  [the longest x1 6.85 us: project(): pl.pallas_call(kernel, in_specs=[anywhere, VMEM, VMEM, VMEM, anywhere, an...]
    select_n x3 -> x0, other arithmetic: 3.03 us -> none  [the longest x1 1.98 us: slab(): return jnp.where(has_keys, keys[part], got_values[part])]
    unnamed x18 -> x6, local copies, waits for them, and re-layouts: 2.21 us -> 4.14 us
    reshape x1, local copies, waits for them, and re-layouts: 0.01 us -> 1.3 us  [broadcast(): gain.reshape(1, -1)]
  transfers between devices with their start and end apart: 28 -> 28, of which waited for: 16 -> 10; matrix products, arithmetic and copies ran while one was open for 0% -> 2% of each run, Pallas kernels for 4% -> 9%
where the time goes in v2:
time: 79.2 us; the launch traced here: 79.4 us
  starting transfers between devices  44.7 us (56%)
  waiting for transfers between devices  16.3 us (21%)
  Pallas kernels  11.8 us (15%)
  local copies, waits for them, and re-layouts  5.44 us (7%)
  between operations  0.83 us (1%)
    ppermute x28, starting transfers between devices, send(): return lax.ppermute(block, AXES, pairs)  44.7 us
    ppermute x28, waiting for transfers between devices, send(): return lax.ppermute(block, AXES, pairs)  16.3 us
    pallas_call x1, Pallas kernels, project(): pl.pallas_call(kernel, in_specs=[anywhere, VMEM, VMEM, VMEM, anywhere, an...  6.85 us
    unnamed x6, local copies, waits for them, and re-layouts  4.14 us
    pallas_call x1, Pallas kernels, attend(): pl.pallas_call(kernel, in_specs=[pl.BlockSpec(memory_space=pltpu.SMEM)] +...  3.55 us
  transfers between devices with their start and end apart: 28, of which 10 were waited for; matrix products, arithmetic and copies ran while one was open for 2% of the time, Pallas kernels for 9%

profile of v2, /device:TPU:32, one launch (start us, length us, event | category | flops | bytes accessed | tf_op | source)
XLA Modules:
  0.0 79.4 jit_solution(12850411277007489012)
XLA Ops:
  0.0 0.0 collective-permute-start.12
  0.7 1.3 %reshape.32.gain_ref = bf16[1,4096]{1,0:T(2,128)(2,1)} reshape(bf16[4096]{0:T(1024)(128)(2,1)} %param.16) | data formatting | bytes 16384 | tf_op jit(solution)/shard_map/reshape | solution.py:100
  2.0 0.1 collective-permute-done.12.values_ref
  2.1 1.0 %copy-done.2 = bf16[1,2048,128]{2,1,0:T(8,128)(2,1)S(1)} copy-done((bf16[1,2048,128]{2,1,0:T(8,128)(2,1)S(1)}, bf16[1,2048,128]{2,1,0:T(8,128)(2,1)}, u32[]{:S(2)}) %copy-start.2) | copy-done | bytes 524312
  3.2 1.6 %collective-permute-start.13 = (bf16[512,128]{1,0:T(8,128)(2,1)S(1)}, bf16[512,128]{1,0:T(8,128)(2,1)S(1)}, u32[]{:S(2)}, u32[]{:S(2)}) collective-permute-start(bf16[512,128]{1,0:T(8,128)(2,1)S(1)} %get-tuple-element.69), channel_id=1, source_target_pairs={{0,64},{1,65},{2,66},{3,67},{4,68},{5,69},{6,70},{7,71},{8,72},{9,... | collective-permute-start | bytes 393224 | tf_op jit(solution)/shard_map/ppermute | solution.py:38
  4.8 2.7 %collective-permute-start.14 = (bf16[512,128]{1,0:T(8,128)(2,1)S(1)}, bf16[512,128]{1,0:T(8,128)(2,1)S(1)}, u32[]{:S(2)}, u32[]{:S(2)}) collective-permute-start(bf16[512,128]{1,0:T(8,128)(2,1)S(1)} %get-tuple-element.70), channel_id=1, source_target_pairs={{0,128},{1,129},{2,130},{3,131},{4,132},{5,133},{6,134},{7,135},{8... | collective-permute-start | bytes 393224 | tf_op jit(solution)/shard_map/ppermute | solution.py:38
  7.5 1.4 %collective-permute-start.15 = (bf16[512,128]{1,0:T(8,128)(2,1)S(1)}, bf16[512,128]{1,0:T(8,128)(2,1)S(1)}, u32[]{:S(2)}, u32[]{:S(2)}) collective-permute-start(bf16[512,128]{1,0:T(8,128)(2,1)S(1)} %get-tuple-element.71), channel_id=1, source_target_pairs={{0,192},{1,193},{2,194},{3,195},{4,196},{5,197},{6,198},{7,199},{8... | collective-permute-start | bytes 393224 | tf_op jit(solution)/shard_map/ppermute | solution.py:38
  9.0 6.9 %shard_map.110.refs_0_ = bf16[6,96,128]{2,1,0:T(8,128)(2,1)} custom-call(bf16[96,4096]{1,0:T(8,128)(2,1)} %bitcast.18, bf16[1,4096]{1,0:T(2,128)(2,1)} %reshape.32.gain_ref, f32[96,128]{1,0:T(8,128)} %constant.141.clone.cos_ref, f32[96,128]{1,0:T(8,128)} %constant.142.clone.sin_ref, bf16[4096,512]{1,0:T(8,128)(2,1)} %wq_hbm.1, bf16[4096,128]{1,0:T(8,128)(2,1)} %wk_hbm.1, ...), custom_call_target="tpu_custom_call" | custom-call | flops 603979776 | bytes 7077888 | tf_op jit(solution)/shard_map/pallas_call | solution.py:202
  15.8 0.0 collective-permute-done.13.refs_1_
  15.8 0.0 collective-permute-done.14.refs_2_
  15.8 0.0 collective-permute-done.15.refs_3_
  15.9 13.3 %conditional.1 = (bf16[512,128]{1,0:T(8,128)(2,1)S(1)}) conditional(s32[]{:T(128)} %clamp.3, (s32[]{:T(128)}, bf16[512,128]{1,0:T(8,128)(2,1)S(1)}) %tuple.23, (s32[]{:T(128)}, bf16[512,128]{1,0:T(8,128)(2,1)S(1)}) %tuple.23, (s32[]{:T(128)}, bf16[512,128]{1,0:T(8,128)(2,1)S(1)}) %tuple.23, (s32[]{:T(128)}, ...), branch_computations={%region_0.1_spmd, %region_1.2_spmd, %region_2.3_spmd, %region_3.4_... | conditional | flops 8 | bytes 1573074 | solution.py:92
  15.9 5.2 %collective-permute-start.2 = (bf16[512,128]{1,0:T(8,128)(2,1)S(1)}, bf16[512,128]{1,0:T(8,128)(2,1)S(1)}, u32[]{:S(2)}, u32[]{:S(2)}) collective-permute-start(bf16[512,128]{1,0:T(8,128)(2,1)S(1)} %get-tuple-element.26.refs_0_), channel_id=1, source_target_pairs={{0,16},{1,17},{2,18},{3,19},{4,20},{5,21},{6,22},{7,23},{8,24},{9,... | collective-permute-start | bytes 393224 | tf_op jit(solution)/shard_map/cond/branch_0_fun/ppermute | solution.py:38
  21.1 2.8 %collective-permute-start.1 = (bf16[512,128]{1,0:T(8,128)(2,1)S(1)}, bf16[512,128]{1,0:T(8,128)(2,1)S(1)}, u32[]{:S(2)}, u32[]{:S(2)}) collective-permute-start(bf16[512,128]{1,0:T(8,128)(2,1)S(1)} %get-tuple-element.26.refs_0_), channel_id=1, source_target_pairs={{0,48},{1,49},{2,50},{3,51},{4,52},{5,53},{6,54},{7,55},{8,56},{9,... | collective-permute-start | bytes 393224 | tf_op jit(solution)/shard_map/cond/branch_0_fun/ppermute | solution.py:38
  23.9 1.6 %collective-permute-start = (bf16[512,128]{1,0:T(8,128)(2,1)S(1)}, bf16[512,128]{1,0:T(8,128)(2,1)S(1)}, u32[]{:S(2)}, u32[]{:S(2)}) collective-permute-start(bf16[512,128]{1,0:T(8,128)(2,1)S(1)} %get-tuple-element.26.refs_0_), channel_id=1, source_target_pairs={{0,32},{1,33},{2,34},{3,35},{4,36},{5,37},{6,38},{7,39},{8,40},{9,... | collective-permute-start | bytes 393224 | tf_op jit(solution)/shard_map/cond/branch_0_fun/ppermute | solution.py:38
  25.5 3.2 %collective-permute-done.2.refs_3_ = bf16[512,128]{1,0:T(8,128)(2,1)S(1)} collective-permute-done((bf16[512,128]{1,0:T(8,128)(2,1)S(1)}, bf16[512,128]{1,0:T(8,128)(2,1)S(1)}, u32[]{:S(2)}, u32[]{:S(2)}) %collective-permute-start.2) | collective-permute-done | bytes 131104 | tf_op jit(solution)/shard_map/cond/branch_0_fun/ppermute | solution.py:38
  28.7 0.0 collective-permute-done.1.refs_2_
  28.7 0.5 collective-permute-done.refs_1_
  29.2 0.8 collective-permute-start.21
  30.0 2.6 %collective-permute-start.19 = (bf16[512,128]{1,0:T(8,128)(2,1)S(1)}, bf16[512,128]{1,0:T(8,128)(2,1)S(1)}, u32[]{:S(2)}, u32[]{:S(2)}) collective-permute-start(bf16[512,128]{1,0:T(8,128)(2,1)S(1)} %get-tuple-element.100.rest_0_), channel_id=1, source_target_pairs={{0,192},{1,193},{2,194},{3,195},{4,196},{5,197},{6,198},{7,199},{8... | collective-permute-start | bytes 393224 | tf_op jit(solution)/shard_map/ppermute | solution.py:38
  32.6 0.0 collective-permute-start.17
  32.6 0.0 collective-permute-start.16
  32.6 4.0 %collective-permute-done.21.rest_3_ = bf16[512,128]{1,0:T(8,128)(2,1)S(1)} collective-permute-done((bf16[512,128]{1,0:T(8,128)(2,1)S(1)}, bf16[512,128]{1,0:T(8,128)(2,1)S(1)}, u32[]{:S(2)}, u32[]{:S(2)}) %collective-permute-start.21) | collective-permute-done | bytes 131104 | tf_op jit(solution)/shard_map/ppermute | solution.py:38
  36.6 0.0 collective-permute-start.22
  36.6 0.0 collective-permute-done.19.rest_2_
  36.6 0.5 collective-permute-start.20
  37.1 1.6 %collective-permute-done.17.rest_1_ = bf16[512,128]{1,0:T(8,128)(2,1)S(1)} collective-permute-done((bf16[512,128]{1,0:T(8,128)(2,1)S(1)}, bf16[512,128]{1,0:T(8,128)(2,1)S(1)}, u32[]{:S(2)}, u32[]{:S(2)}) %collective-permute-start.17) | collective-permute-done | bytes 131104 | tf_op jit(solution)/shard_map/ppermute | solution.py:38
  38.8 0.0 collective-permute-start.18
  38.8 0.1 pad_add_fusion.place_ref
  38.9 2.2 %copy-done = bf16[512,4096]{1,0:T(8,128)(2,1)S(1)} copy-done((bf16[512,4096]{1,0:T(8,128)(2,1)S(1)}, bf16[512,4096]{1,0:T(8,128)(2,1)}, u32[]{:S(2)}) %copy-start) | copy-done | bytes 4194328
  41.0 0.9 %copy-done.1 = bf16[6,96,128]{2,1,0:T(8,128)(2,1)S(1)} copy-done((bf16[6,96,128]{2,1,0:T(8,128)(2,1)S(1)}, bf16[6,96,128]{2,1,0:T(8,128)(2,1)}, u32[]{:S(2)}) %copy-start.1) | copy-done | bytes 147480
  41.9 0.4 shard_map.112
  42.3 0.0 collective-permute-done.16.rest_4_
  42.3 0.0 collective-permute-done.22.rest_7_
  42.4 0.0 collective-permute-done.20.rest_6_
  42.4 0.0 collective-permute-done.18.rest_5_
  42.4 3.5 %shard_map.113 = (bf16[96,512]{1,0:T(8,128)(2,1)S(1)}, bf16[96,512]{1,0:T(8,128)(2,1)S(1)}, bf16[96,512]{1,0:T(8,128)(2,1)S(1)}, bf16[96,512]{1,0:T(8,128)(2,1)S...) custom-call(s32[2]{0:T(128)S(1)} %pad_add_fusion.place_ref, ...), custom_call_target="tpu_custom_call" | custom-call | flops 1207959552 | bytes 5242880 | tf_op jit(solution)/shard_map/pallas_call | solution.py:297
  45.9 1.7 %collective-permute-start.23 = (bf16[96,512]{1,0:T(8,128)(2,1)S(1)}, bf16[96,512]{1,0:T(8,128)(2,1)S(1)}, u32[]{:S(2)}, u32[]{:S(2)}) collective-permute-start(bf16[96,512]{1,0:T(8,128)(2,1)S(1)} %get-tuple-element.93), channel_id=1, source_target_pairs={{0,1},{1,2},{2,3},{3,0},{4,5},{5,6},{6,7},{7,4},{8,9},{9,10},{10,1... | collective-permute-start | bytes 294920 | tf_op jit(solution)/shard_map/ppermute | solution.py:38
  47.6 2.9 %collective-permute-start.24 = (bf16[96,512]{1,0:T(8,128)(2,1)S(1)}, bf16[96,512]{1,0:T(8,128)(2,1)S(1)}, u32[]{:S(2)}, u32[]{:S(2)}) collective-permute-start(bf16[96,512]{1,0:T(8,128)(2,1)S(1)} %get-tuple-element.94), channel_id=1, source_target_pairs={{0,2},{1,3},{2,0},{3,1},{4,6},{5,7},{6,4},{7,5},{8,10},{9,11},{10,... | collective-permute-start | bytes 294920 | tf_op jit(solution)/shard_map/ppermute | solution.py:38
  50.5 1.3 %collective-permute-start.25 = (bf16[96,512]{1,0:T(8,128)(2,1)S(1)}, bf16[96,512]{1,0:T(8,128)(2,1)S(1)}, u32[]{:S(2)}, u32[]{:S(2)}) collective-permute-start(bf16[96,512]{1,0:T(8,128)(2,1)S(1)} %get-tuple-element.95), channel_id=1, source_target_pairs={{0,3},{1,0},{2,1},{3,2},{4,7},{5,4},{6,5},{7,6},{8,11},{9,8},{10,9... | collective-permute-start | bytes 294920 | tf_op jit(solution)/shard_map/ppermute | solution.py:38
  51.8 0.7 collective-permute-start.30
  52.5 0.8 collective-permute-start.31
  53.3 0.0 collective-permute-done.23
  53.3 1.9 %collective-permute-start.32 = (bf16[96,512]{1,0:T(8,128)(2,1)S(1)}, bf16[96,512]{1,0:T(8,128)(2,1)S(1)}, u32[]{:S(2)}, u32[]{:S(2)}) collective-permute-start(bf16[96,512]{1,0:T(8,128)(2,1)S(1)} %get-tuple-element.99), channel_id=1, source_target_pairs={{0,3},{1,0},{2,1},{3,2},{4,7},{5,4},{6,5},{7,6},{8,11},{9,8},{10,9... | collective-permute-start | bytes 294920 | tf_op jit(solution)/shard_map/ppermute | solution.py:38
  55.2 1.0 %collective-permute-done.24 = bf16[96,512]{1,0:T(8,128)(2,1)S(1)} collective-permute-done((bf16[96,512]{1,0:T(8,128)(2,1)S(1)}, bf16[96,512]{1,0:T(8,128)(2,1)S(1)}, u32[]{:S(2)}, u32[]{:S(2)}) %collective-permute-start.24) | collective-permute-done | bytes 98336 | tf_op jit(solution)/shard_map/ppermute | solution.py:38
  56.2 0.1 add_convert_fusion.3
  56.2 4.2 %collective-permute-start.26 = (bf16[96,512]{1,0:T(8,128)(2,1)S(1)}, bf16[96,512]{1,0:T(8,128)(2,1)S(1)}, u32[]{:S(2)}, u32[]{:S(2)}) collective-permute-start(bf16[96,512]{1,0:T(8,128)(2,1)S(1)} %add_convert_fusion.3), channel_id=1, source_target_pairs={{0,4},{1,5},{2,6},{3,7},{4,0},{5,1},{6,2},{7,3},{8,12},{9,13},{10,... | collective-permute-start | bytes 294920 | tf_op jit(solution)/shard_map/ppermute | solution.py:38
  60.4 0.0 collective-permute-done.30
  60.4 0.0 collective-permute-done.31
  60.4 0.1 add_convert_fusion.1
  60.5 3.9 %collective-permute-start.33 = (bf16[96,512]{1,0:T(8,128)(2,1)S(1)}, bf16[96,512]{1,0:T(8,128)(2,1)S(1)}, u32[]{:S(2)}, u32[]{:S(2)}) collective-permute-start(bf16[96,512]{1,0:T(8,128)(2,1)S(1)} %add_convert_fusion.1), channel_id=1, source_target_pairs={{0,4},{1,5},{2,6},{3,7},{4,0},{5,1},{6,2},{7,3},{8,12},{9,13},{10,... | collective-permute-start | bytes 294920 | tf_op jit(solution)/shard_map/ppermute | solution.py:38
  64.4 2.5 %collective-permute-start.29 = (bf16[96,512]{1,0:T(8,128)(2,1)S(1)}, bf16[96,512]{1,0:T(8,128)(2,1)S(1)}, u32[]{:S(2)}, u32[]{:S(2)}) collective-permute-start(bf16[96,512]{1,0:T(8,128)(2,1)S(1)} %add_convert_fusion.2.rest_0_), channel_id=1, source_target_pairs={{0,3},{1,0},{2,1},{3,2},{4,7},{5,4},{6,5},{7,6},{8,11},{9,8},{10,9... | collective-permute-start | bytes 294920 | tf_op jit(solution)/shard_map/ppermute | solution.py:38
  66.9 1.0 %collective-permute-start.28 = (bf16[96,512]{1,0:T(8,128)(2,1)S(1)}, bf16[96,512]{1,0:T(8,128)(2,1)S(1)}, u32[]{:S(2)}, u32[]{:S(2)}) collective-permute-start(bf16[96,512]{1,0:T(8,128)(2,1)S(1)} %add_convert_fusion.2.rest_0_), channel_id=1, source_target_pairs={{0,2},{1,3},{2,0},{3,1},{4,6},{5,7},{6,4},{7,5},{8,10},{9,11},{10,... | collective-permute-start | bytes 294920 | tf_op jit(solution)/shard_map/ppermute | solution.py:38
  67.9 0.4 collective-permute-start.27
  68.3 2.9 %collective-permute-start.36 = (bf16[96,512]{1,0:T(8,128)(2,1)S(1)}, bf16[96,512]{1,0:T(8,128)(2,1)S(1)}, u32[]{:S(2)}, u32[]{:S(2)}) collective-permute-start(bf16[96,512]{1,0:T(8,128)(2,1)S(1)} %add_convert_fusion.rest_4_), channel_id=1, source_target_pairs={{0,3},{1,0},{2,1},{3,2},{4,7},{5,4},{6,5},{7,6},{8,11},{9,8},{10,9... | collective-permute-start | bytes 294920 | tf_op jit(solution)/shard_map/ppermute | solution.py:38
  71.3 1.3 %collective-permute-start.35 = (bf16[96,512]{1,0:T(8,128)(2,1)S(1)}, bf16[96,512]{1,0:T(8,128)(2,1)S(1)}, u32[]{:S(2)}, u32[]{:S(2)}) collective-permute-start(bf16[96,512]{1,0:T(8,128)(2,1)S(1)} %add_convert_fusion.rest_4_), channel_id=1, source_target_pairs={{0,2},{1,3},{2,0},{3,1},{4,6},{5,7},{6,4},{7,5},{8,10},{9,11},{10,... | collective-permute-start | bytes 294920 | tf_op jit(solution)/shard_map/ppermute | solution.py:38
  72.6 0.0 collective-permute-done.29.rest_3_
  72.6 0.0 collective-permute-start.34
  72.6 0.6 collective-permute-done.28.rest_2_
  73.2 2.3 %collective-permute-done.27.rest_1_ = bf16[96,512]{1,0:T(8,128)(2,1)S(1)} collective-permute-done((bf16[96,512]{1,0:T(8,128)(2,1)S(1)}, bf16[96,512]{1,0:T(8,128)(2,1)S(1)}, u32[]{:S(2)}, u32[]{:S(2)}) %collective-permute-start.27) | collective-permute-done | bytes 98336 | tf_op jit(solution)/shard_map/ppermute | solution.py:38
  75.5 0.0 collective-permute-done.36.rest_7_
  75.5 1.9 %collective-permute-done.35.rest_6_ = bf16[96,512]{1,0:T(8,128)(2,1)S(1)} collective-permute-done((bf16[96,512]{1,0:T(8,128)(2,1)S(1)}, bf16[96,512]{1,0:T(8,128)(2,1)S(1)}, u32[]{:S(2)}, u32[]{:S(2)}) %collective-permute-start.35) | collective-permute-done | bytes 98336 | tf_op jit(solution)/shard_map/ppermute | solution.py:38
  77.4 1.1 %collective-permute-done.34.rest_5_ = bf16[96,512]{1,0:T(8,128)(2,1)S(1)} collective-permute-done((bf16[96,512]{1,0:T(8,128)(2,1)S(1)}, bf16[96,512]{1,0:T(8,128)(2,1)S(1)}, u32[]{:S(2)}, u32[]{:S(2)}) %collective-permute-start.34) | collective-permute-done | bytes 98336 | tf_op jit(solution)/shard_map/ppermute | solution.py:38
  78.5 0.9 %shard_map.114 = bf16[96,4096]{1,0:T(8,128)(2,1)} custom-call(s32[1]{0:T(128)S(6)} %select_n.46.y_ref, bf16[96,512]{1,0:T(8,128)(2,1)S(1)} %add_convert_fusion.2.rest_0_, bf16[96,512]{1,0:T(8,128)(2,1)S(1)} %collective-permute-done.27.rest_1_, bf16[96,512]{1,0:T(8,128)(2,1)S(1)} %collective-permute-done.28.rest_2_, ...), custom_call_target="tpu_custom_call" | custom-call | tf_op jit(solution)/shard_map/pallas_call | solution.py:337
  (12 shorter events, 0.2 us)
Async XLA Ops:
  0.0 2.1 %collective-permute-start.12 = (bf16[2048,128]{1,0:T(8,128)(2,1)}, bf16[2048,128]{1,0:T(8,128)(2,1)S(1)}, u32[]{:S(2)}, u32[]{:S(2)}) collective-permute-start(bf16[2048,128]{1,0:T(8,128)(2,1)} %bitcast.19), channel_id=1, source_target_pairs={{0,8},{1,9},{2,10},{3,11},{4,12},{5,13},{6,14},{7,15},{8,0},{9,1},... | collective-permute-start | bytes 1572872 | tf_op jit(solution)/shard_map/ppermute | solution.py:38
  2.1 1.0 %copy-start.2 = (bf16[1,2048,128]{2,1,0:T(8,128)(2,1)S(1)}, bf16[1,2048,128]{2,1,0:T(8,128)(2,1)}, u32[]{:S(2)}) copy-start(bf16[1,2048,128]{2,1,0:T(8,128)(2,1)} %param.21) | copy-start | bytes 1572868
  3.2 12.6 %collective-permute-start.13 = (bf16[512,128]{1,0:T(8,128)(2,1)S(1)}, bf16[512,128]{1,0:T(8,128)(2,1)S(1)}, u32[]{:S(2)}, u32[]{:S(2)}) collective-permute-start(bf16[512,128]{1,0:T(8,128)(2,1)S(1)} %get-tuple-element.69), channel_id=1, source_target_pairs={{0,64},{1,65},{2,66},{3,67},{4,68},{5,69},{6,70},{7,71},{8,72},{9,... | collective-permute-start | bytes 393224 | tf_op jit(solution)/shard_map/ppermute | solution.py:38
  4.8 11.0 %collective-permute-start.14 = (bf16[512,128]{1,0:T(8,128)(2,1)S(1)}, bf16[512,128]{1,0:T(8,128)(2,1)S(1)}, u32[]{:S(2)}, u32[]{:S(2)}) collective-permute-start(bf16[512,128]{1,0:T(8,128)(2,1)S(1)} %get-tuple-element.70), channel_id=1, source_target_pairs={{0,128},{1,129},{2,130},{3,131},{4,132},{5,133},{6,134},{7,135},{8... | collective-permute-start | bytes 393224 | tf_op jit(solution)/shard_map/ppermute | solution.py:38
  7.5 8.3 %collective-permute-start.15 = (bf16[512,128]{1,0:T(8,128)(2,1)S(1)}, bf16[512,128]{1,0:T(8,128)(2,1)S(1)}, u32[]{:S(2)}, u32[]{:S(2)}) collective-permute-start(bf16[512,128]{1,0:T(8,128)(2,1)S(1)} %get-tuple-element.71), channel_id=1, source_target_pairs={{0,192},{1,193},{2,194},{3,195},{4,196},{5,197},{6,198},{7,199},{8... | collective-permute-start | bytes 393224 | tf_op jit(solution)/shard_map/ppermute | solution.py:38
  15.9 12.8 %collective-permute-start.2 = (bf16[512,128]{1,0:T(8,128)(2,1)S(1)}, bf16[512,128]{1,0:T(8,128)(2,1)S(1)}, u32[]{:S(2)}, u32[]{:S(2)}) collective-permute-start(bf16[512,128]{1,0:T(8,128)(2,1)S(1)} %get-tuple-element.26.refs_0_), channel_id=1, source_target_pairs={{0,16},{1,17},{2,18},{3,19},{4,20},{5,21},{6,22},{7,23},{8,24},{9,... | collective-permute-start | bytes 393224 | tf_op jit(solution)/shard_map/cond/branch_0_fun/ppermute | solution.py:38
  21.1 7.6 %collective-permute-start.1 = (bf16[512,128]{1,0:T(8,128)(2,1)S(1)}, bf16[512,128]{1,0:T(8,128)(2,1)S(1)}, u32[]{:S(2)}, u32[]{:S(2)}) collective-permute-start(bf16[512,128]{1,0:T(8,128)(2,1)S(1)} %get-tuple-element.26.refs_0_), channel_id=1, source_target_pairs={{0,48},{1,49},{2,50},{3,51},{4,52},{5,53},{6,54},{7,55},{8,56},{9,... | collective-permute-start | bytes 393224 | tf_op jit(solution)/shard_map/cond/branch_0_fun/ppermute | solution.py:38
  23.9 5.3 %collective-permute-start = (bf16[512,128]{1,0:T(8,128)(2,1)S(1)}, bf16[512,128]{1,0:T(8,128)(2,1)S(1)}, u32[]{:S(2)}, u32[]{:S(2)}) collective-permute-start(bf16[512,128]{1,0:T(8,128)(2,1)S(1)} %get-tuple-element.26.refs_0_), channel_id=1, source_target_pairs={{0,32},{1,33},{2,34},{3,35},{4,36},{5,37},{6,38},{7,39},{8,40},{9,... | collective-permute-start | bytes 393224 | tf_op jit(solution)/shard_map/cond/branch_0_fun/ppermute | solution.py:38
  29.2 7.4 %collective-permute-start.21 = (bf16[512,128]{1,0:T(8,128)(2,1)S(1)}, bf16[512,128]{1,0:T(8,128)(2,1)S(1)}, u32[]{:S(2)}, u32[]{:S(2)}) collective-permute-start(bf16[512,128]{1,0:T(8,128)(2,1)S(1)} %get-tuple-element.100.rest_0_), channel_id=1, source_target_pairs={{0,128},{1,129},{2,130},{3,131},{4,132},{5,133},{6,134},{7,135},{8... | collective-permute-start | bytes 393224 | tf_op jit(solution)/shard_map/ppermute | solution.py:38
  30.0 6.6 %collective-permute-start.19 = (bf16[512,128]{1,0:T(8,128)(2,1)S(1)}, bf16[512,128]{1,0:T(8,128)(2,1)S(1)}, u32[]{:S(2)}, u32[]{:S(2)}) collective-permute-start(bf16[512,128]{1,0:T(8,128)(2,1)S(1)} %get-tuple-element.100.rest_0_), channel_id=1, source_target_pairs={{0,192},{1,193},{2,194},{3,195},{4,196},{5,197},{6,198},{7,199},{8... | collective-permute-start | bytes 393224 | tf_op jit(solution)/shard_map/ppermute | solution.py:38
  32.6 6.2 %collective-permute-start.17 = (bf16[512,128]{1,0:T(8,128)(2,1)S(1)}, bf16[512,128]{1,0:T(8,128)(2,1)S(1)}, u32[]{:S(2)}, u32[]{:S(2)}) collective-permute-start(bf16[512,128]{1,0:T(8,128)(2,1)S(1)} %get-tuple-element.100.rest_0_), channel_id=1, source_target_pairs={{0,64},{1,65},{2,66},{3,67},{4,68},{5,69},{6,70},{7,71},{8,72},{9,... | collective-permute-start | bytes 393224 | tf_op jit(solution)/shard_map/ppermute | solution.py:38
  32.6 9.7 %collective-permute-start.16 = (bf16[512,128]{1,0:T(8,128)(2,1)S(1)}, bf16[512,128]{1,0:T(8,128)(2,1)S(1)}, u32[]{:S(2)}, u32[]{:S(2)}) collective-permute-start(bf16[512,128]{1,0:T(8,128)(2,1)S(1)} %get-tuple-element.100.rest_0_), channel_id=1, source_target_pairs={{0,8},{1,9},{2,10},{3,11},{4,12},{5,13},{6,14},{7,15},{8,0},{9,1},... | collective-permute-start | bytes 393224 | tf_op jit(solution)/shard_map/ppermute | solution.py:38
  36.6 5.7 %collective-permute-start.22 = (bf16[512,128]{1,0:T(8,128)(2,1)S(1)}, bf16[512,128]{1,0:T(8,128)(2,1)S(1)}, u32[]{:S(2)}, u32[]{:S(2)}) collective-permute-start(bf16[512,128]{1,0:T(8,128)(2,1)S(1)} %collective-permute-done.21.rest_3_), channel_id=1, source_target_pairs={{0,8},{1,9},{2,10},{3,11},{4,12},{5,13},{6,14},{7,15},{8,0},{9,1},... | collective-permute-start | bytes 393224 | tf_op jit(solution)/shard_map/ppermute | solution.py:38
  36.6 5.7 %collective-permute-start.20 = (bf16[512,128]{1,0:T(8,128)(2,1)S(1)}, bf16[512,128]{1,0:T(8,128)(2,1)S(1)}, u32[]{:S(2)}, u32[]{:S(2)}) collective-permute-start(bf16[512,128]{1,0:T(8,128)(2,1)S(1)} %collective-permute-done.19.rest_2_), channel_id=1, source_target_pairs={{0,8},{1,9},{2,10},{3,11},{4,12},{5,13},{6,14},{7,15},{8,0},{9,1},... | collective-permute-start | bytes 393224 | tf_op jit(solution)/shard_map/ppermute | solution.py:38
  38.8 3.6 %collective-permute-start.18 = (bf16[512,128]{1,0:T(8,128)(2,1)S(1)}, bf16[512,128]{1,0:T(8,128)(2,1)S(1)}, u32[]{:S(2)}, u32[]{:S(2)}) collective-permute-start(bf16[512,128]{1,0:T(8,128)(2,1)S(1)} %collective-permute-done.17.rest_1_), channel_id=1, source_target_pairs={{0,8},{1,9},{2,10},{3,11},{4,12},{5,13},{6,14},{7,15},{8,0},{9,1},... | collective-permute-start | bytes 393224 | tf_op jit(solution)/shard_map/ppermute | solution.py:38
  38.8 2.2 %copy-start = (bf16[512,4096]{1,0:T(8,128)(2,1)S(1)}, bf16[512,4096]{1,0:T(8,128)(2,1)}, u32[]{:S(2)}) copy-start(bf16[512,4096]{1,0:T(8,128)(2,1)} %refs_1_) | copy-start | bytes 12582916
  41.0 0.9 %copy-start.1 = (bf16[6,96,128]{2,1,0:T(8,128)(2,1)S(1)}, bf16[6,96,128]{2,1,0:T(8,128)(2,1)}, u32[]{:S(2)}) copy-start(bf16[6,96,128]{2,1,0:T(8,128)(2,1)} %shard_map.110.refs_0_) | copy-start | bytes 442372
  45.9 7.4 %collective-permute-start.23 = (bf16[96,512]{1,0:T(8,128)(2,1)S(1)}, bf16[96,512]{1,0:T(8,128)(2,1)S(1)}, u32[]{:S(2)}, u32[]{:S(2)}) collective-permute-start(bf16[96,512]{1,0:T(8,128)(2,1)S(1)} %get-tuple-element.93), channel_id=1, source_target_pairs={{0,1},{1,2},{2,3},{3,0},{4,5},{5,6},{6,7},{7,4},{8,9},{9,10},{10,1... | collective-permute-start | bytes 294920 | tf_op jit(solution)/shard_map/ppermute | solution.py:38
  47.6 8.6 %collective-permute-start.24 = (bf16[96,512]{1,0:T(8,128)(2,1)S(1)}, bf16[96,512]{1,0:T(8,128)(2,1)S(1)}, u32[]{:S(2)}, u32[]{:S(2)}) collective-permute-start(bf16[96,512]{1,0:T(8,128)(2,1)S(1)} %get-tuple-element.94), channel_id=1, source_target_pairs={{0,2},{1,3},{2,0},{3,1},{4,6},{5,7},{6,4},{7,5},{8,10},{9,11},{10,... | collective-permute-start | bytes 294920 | tf_op jit(solution)/shard_map/ppermute | solution.py:38
  50.5 5.7 %collective-permute-start.25 = (bf16[96,512]{1,0:T(8,128)(2,1)S(1)}, bf16[96,512]{1,0:T(8,128)(2,1)S(1)}, u32[]{:S(2)}, u32[]{:S(2)}) collective-permute-start(bf16[96,512]{1,0:T(8,128)(2,1)S(1)} %get-tuple-element.95), channel_id=1, source_target_pairs={{0,3},{1,0},{2,1},{3,2},{4,7},{5,4},{6,5},{7,6},{8,11},{9,8},{10,9... | collective-permute-start | bytes 294920 | tf_op jit(solution)/shard_map/ppermute | solution.py:38
  51.8 8.6 %collective-permute-start.30 = (bf16[96,512]{1,0:T(8,128)(2,1)S(1)}, bf16[96,512]{1,0:T(8,128)(2,1)S(1)}, u32[]{:S(2)}, u32[]{:S(2)}) collective-permute-start(bf16[96,512]{1,0:T(8,128)(2,1)S(1)} %get-tuple-element.97), channel_id=1, source_target_pairs={{0,1},{1,2},{2,3},{3,0},{4,5},{5,6},{6,7},{7,4},{8,9},{9,10},{10,1... | collective-permute-start | bytes 294920 | tf_op jit(solution)/shard_map/ppermute | solution.py:38
  52.5 7.9 %collective-permute-start.31 = (bf16[96,512]{1,0:T(8,128)(2,1)S(1)}, bf16[96,512]{1,0:T(8,128)(2,1)S(1)}, u32[]{:S(2)}, u32[]{:S(2)}) collective-permute-start(bf16[96,512]{1,0:T(8,128)(2,1)S(1)} %get-tuple-element.98), channel_id=1, source_target_pairs={{0,2},{1,3},{2,0},{3,1},{4,6},{5,7},{6,4},{7,5},{8,10},{9,11},{10,... | collective-permute-start | bytes 294920 | tf_op jit(solution)/shard_map/ppermute | solution.py:38
  53.3 7.1 %collective-permute-start.32 = (bf16[96,512]{1,0:T(8,128)(2,1)S(1)}, bf16[96,512]{1,0:T(8,128)(2,1)S(1)}, u32[]{:S(2)}, u32[]{:S(2)}) collective-permute-start(bf16[96,512]{1,0:T(8,128)(2,1)S(1)} %get-tuple-element.99), channel_id=1, source_target_pairs={{0,3},{1,0},{2,1},{3,2},{4,7},{5,4},{6,5},{7,6},{8,11},{9,8},{10,9... | collective-permute-start | bytes 294920 | tf_op jit(solution)/shard_map/ppermute | solution.py:38
  56.2 8.1 %collective-permute-start.26 = (bf16[96,512]{1,0:T(8,128)(2,1)S(1)}, bf16[96,512]{1,0:T(8,128)(2,1)S(1)}, u32[]{:S(2)}, u32[]{:S(2)}) collective-permute-start(bf16[96,512]{1,0:T(8,128)(2,1)S(1)} %add_convert_fusion.3), channel_id=1, source_target_pairs={{0,4},{1,5},{2,6},{3,7},{4,0},{5,1},{6,2},{7,3},{8,12},{9,13},{10,... | collective-permute-start | bytes 294920 | tf_op jit(solution)/shard_map/ppermute | solution.py:38
  60.5 7.9 %collective-permute-start.33 = (bf16[96,512]{1,0:T(8,128)(2,1)S(1)}, bf16[96,512]{1,0:T(8,128)(2,1)S(1)}, u32[]{:S(2)}, u32[]{:S(2)}) collective-permute-start(bf16[96,512]{1,0:T(8,128)(2,1)S(1)} %add_convert_fusion.1), channel_id=1, source_target_pairs={{0,4},{1,5},{2,6},{3,7},{4,0},{5,1},{6,2},{7,3},{8,12},{9,13},{10,... | collective-permute-start | bytes 294920 | tf_op jit(solution)/shard_map/ppermute | solution.py:38
  64.4 8.2 %collective-permute-start.29 = (bf16[96,512]{1,0:T(8,128)(2,1)S(1)}, bf16[96,512]{1,0:T(8,128)(2,1)S(1)}, u32[]{:S(2)}, u32[]{:S(2)}) collective-permute-start(bf16[96,512]{1,0:T(8,128)(2,1)S(1)} %add_convert_fusion.2.rest_0_), channel_id=1, source_target_pairs={{0,3},{1,0},{2,1},{3,2},{4,7},{5,4},{6,5},{7,6},{8,11},{9,8},{10,9... | collective-permute-start | bytes 294920 | tf_op jit(solution)/shard_map/ppermute | solution.py:38
  66.9 6.3 %collective-permute-start.28 = (bf16[96,512]{1,0:T(8,128)(2,1)S(1)}, bf16[96,512]{1,0:T(8,128)(2,1)S(1)}, u32[]{:S(2)}, u32[]{:S(2)}) collective-permute-start(bf16[96,512]{1,0:T(8,128)(2,1)S(1)} %add_convert_fusion.2.rest_0_), channel_id=1, source_target_pairs={{0,2},{1,3},{2,0},{3,1},{4,6},{5,7},{6,4},{7,5},{8,10},{9,11},{10,... | collective-permute-start | bytes 294920 | tf_op jit(solution)/shard_map/ppermute | solution.py:38
  67.9 7.6 %collective-permute-start.27 = (bf16[96,512]{1,0:T(8,128)(2,1)S(1)}, bf16[96,512]{1,0:T(8,128)(2,1)S(1)}, u32[]{:S(2)}, u32[]{:S(2)}) collective-permute-start(bf16[96,512]{1,0:T(8,128)(2,1)S(1)} %add_convert_fusion.2.rest_0_), channel_id=1, source_target_pairs={{0,1},{1,2},{2,3},{3,0},{4,5},{5,6},{6,7},{7,4},{8,9},{9,10},{10,1... | collective-permute-start | bytes 294920 | tf_op jit(solution)/shard_map/ppermute | solution.py:38
  68.3 7.2 %collective-permute-start.36 = (bf16[96,512]{1,0:T(8,128)(2,1)S(1)}, bf16[96,512]{1,0:T(8,128)(2,1)S(1)}, u32[]{:S(2)}, u32[]{:S(2)}) collective-permute-start(bf16[96,512]{1,0:T(8,128)(2,1)S(1)} %add_convert_fusion.rest_4_), channel_id=1, source_target_pairs={{0,3},{1,0},{2,1},{3,2},{4,7},{5,4},{6,5},{7,6},{8,11},{9,8},{10,9... | collective-permute-start | bytes 294920 | tf_op jit(solution)/shard_map/ppermute | solution.py:38
  71.3 6.1 %collective-permute-start.35 = (bf16[96,512]{1,0:T(8,128)(2,1)S(1)}, bf16[96,512]{1,0:T(8,128)(2,1)S(1)}, u32[]{:S(2)}, u32[]{:S(2)}) collective-permute-start(bf16[96,512]{1,0:T(8,128)(2,1)S(1)} %add_convert_fusion.rest_4_), channel_id=1, source_target_pairs={{0,2},{1,3},{2,0},{3,1},{4,6},{5,7},{6,4},{7,5},{8,10},{9,11},{10,... | collective-permute-start | bytes 294920 | tf_op jit(solution)/shard_map/ppermute | solution.py:38
  72.6 5.9 %collective-permute-start.34 = (bf16[96,512]{1,0:T(8,128)(2,1)S(1)}, bf16[96,512]{1,0:T(8,128)(2,1)S(1)}, u32[]{:S(2)}, u32[]{:S(2)}) collective-permute-start(bf16[96,512]{1,0:T(8,128)(2,1)S(1)} %add_convert_fusion.rest_4_), channel_id=1, source_target_pairs={{0,1},{1,2},{2,3},{3,0},{4,5},{5,6},{6,7},{7,4},{8,9},{9,10},{10,1... | collective-permute-start | bytes 294920 | tf_op jit(solution)/shard_map/ppermute | solution.py:38

commit v3 on v2

--- a/solution.py
+++ b/solution.py
@@ -8,7 +8,8 @@
 
 HD = 128
 PARTS = 2
-BRING_GRANT = 16
+ATTEND_GRANT = 24
+COPIES = 8
 QKV_GRANT = 56
 ROW_ORDER = (2, 3, 1)
 
@@ -92,52 +93,21 @@
     return lax.switch(root_zh, [branch(a) for a in range(N_ZH)], piece)
 
 
-def broadcast(keys, values, root, gain, beside):
+def broadcast(keys, values, root, beside):
     me = lax.axis_index("inst")
     core, zh, x = me % N_CORE, me // N_CORE % N_ZH, me // (N_CORE * N_ZH)
     root_core, root_zh, root_x = root % N_CORE, root // N_CORE % N_ZH, root // (N_CORE * N_ZH)
     has_keys = core == root_core
-    got_values, gain = lax.optimization_barrier((send(values, dcore=1), gain.reshape(1, -1)))
-    slabs = slabs_of(has_keys, keys, got_values)
+    slabs = slabs_of(has_keys, keys, send(values, dcore=1))
     got = [slabs[0]] + [send(slabs[d], dx=d) for d in (1, 2, 3)]
-    got, result = lax.optimization_barrier((got, beside(gain)))
+    got, result = lax.optimization_barrier((got, beside()))
     mine = pick(got, (x - root_x) % N_X)
     return over_rows(mine, zh, root_zh), has_keys, result
 
 
-def from_row(mine, projected, o_weight):
+def from_row(mine):
     row = [mine] + [send(mine, dx=dx) for dx in (1, 3, 2)]
-    other = [send(a, dcore=1) for a in row]
-    row, projected, o_weight = lax.optimization_barrier((row, projected, o_weight))
-    other, ready = lax.optimization_barrier((other, bring_in(projected, o_weight)))
-    return row, other, ready
-
-
-def bring_in(small, weight):
-    chunks = 8
-    size = weight.shape[0] // chunks
-
-    def kernel(*refs):
-        small_ref, weight_hbm, small_out, weight_out, sems = refs
-        gets = [
-            pltpu.make_async_copy(weight_hbm.at[pl.ds(i * size, size), :], weight_out.at[pl.ds(i * size, size), :], sems.at[i])
-            for i in range(chunks)
-        ]
-        for get in gets:
-            get.start()
-        small_out[...] = small_ref[...]
-        for get in gets:
-            get.wait()
-
-    return pl.pallas_call(
-        kernel,
-        in_specs=[VMEM, pl.BlockSpec(memory_space=pl.ANY)],
-        out_specs=[VMEM] * 2,
-        out_shape=[jax.ShapeDtypeStruct(a.shape, a.dtype) for a in (small, weight)],
-        scratch_shapes=[pltpu.SemaphoreType.DMA((chunks,))],
-        compiler_params=pltpu.CompilerParams(vmem_limit_bytes=BRING_GRANT * 2**20),
-        cost_estimate=pl.CostEstimate(flops=0, bytes_accessed=2 * weight.size, transcendentals=0),
-    )(small, weight)
+    return row, [send(a, dcore=1) for a in row]
 
 
 def project(new_states, attn_gain, q_weight, k_weight, v_weight, prompt_len):
@@ -175,9 +145,14 @@
         inv = lax.rsqrt(squares / feature_dim + epsilon)
         for i in range(chunks):
             part = slice(i * depth, (i + 1) * depth)
-            states = x[:, part].astype(jnp.float32)
-            gain = gain_ref[:, part].astype(jnp.float32)
-            normed = (states * inv * gain).astype(jnp.bfloat16)
+            gain = gain_ref[i * depth // 128 : (i + 1) * depth // 128].astype(jnp.float32)
+            normed = jnp.concatenate(
+                [
+                    (x[:, c * 128 : (c + 1) * 128].astype(jnp.float32) * inv * gain[c - i * depth // 128]).astype(jnp.bfloat16)
+                    for c in range(i * depth // 128, (i + 1) * depth // 128)
+                ],
+                axis=1,
+            )
             at_column = 0
             for get, w in zip(gets[i], (wq, wk, wv)):
                 get.wait()
@@ -203,7 +178,7 @@
         kernel,
         in_specs=[anywhere, VMEM, VMEM, VMEM, anywhere, anywhere, anywhere],
         out_specs=VMEM,
-        out_shape=jax.ShapeDtypeStruct((heads + 2, rows, head_dim), jnp.bfloat16),
+        out_shape=pltpu.VMEM((heads + 2, rows, head_dim), jnp.bfloat16),
         scratch_shapes=[
             pltpu.VMEM((rows, feature_dim), jnp.bfloat16),
             pltpu.VMEM((feature_dim, q_width), jnp.bfloat16),
@@ -220,7 +195,7 @@
         ),
     )(
         new_states.reshape(rows, feature_dim),
-        attn_gain,
+        attn_gain.reshape(feature_dim // 128, 128),
         cosine,
         sine,
         q_weight,
@@ -237,9 +212,16 @@
     scale = head_dim**-0.5
     pieces, positions = len(row), row[0].shape[0]
 
-    def kernel(place_ref, qkv_ref, o_ref, *rest):
+    def kernel(place_ref, qkv_ref, o_hbm, *rest):
         row_refs, other_refs, rest = rest[:pieces], rest[pieces : 2 * pieces], rest[2 * pieces :]
-        out_refs, (keys, values, scores) = rest[: PARTS * N_Y], rest[PARTS * N_Y :]
+        out_refs, (keys, values, scores, o_near, sems) = rest[: PARTS * N_Y], rest[PARTS * N_Y :]
+        parts = [pl.ds(i * o_near.shape[0] // COPIES, o_near.shape[0] // COPIES) for i in range(COPIES)]
+        gets = [
+            pltpu.make_async_copy(o_hbm.at[part, :], o_near.at[part, :], sems.at[i])
+            for i, part in enumerate(parts)
+        ]
+        for get in gets:
+            get.start()
 
         @pl.when(place_ref[1] == 1)
         def _():
@@ -287,30 +269,40 @@
                 numerator += e.astype(jnp.bfloat16).astype(jnp.float32) * values_of[u]
             attended.append((numerator / denominator).astype(jnp.bfloat16))
         attended = jnp.concatenate(attended, axis=1)
+        for get in gets:
+            get.wait()
         for i in range(PARTS * N_Y):
             column = lax.rem(place_ref[0] + i % N_Y, N_Y) * (PARTS * width) + i // N_Y * width
-            o_block = o_ref[:, pl.ds(pl.multiple_of(column, width), width)]
+            o_block = o_near[:, pl.ds(pl.multiple_of(column, width), width)]
             out_refs[i][...] = jnp.dot(attended, o_block, preferred_element_type=jnp.float32).astype(jnp.bfloat16)
 
     place = jnp.stack([lax.axis_index("tp") % N_Y, has_keys.astype(jnp.int32)])
     vmem = pl.BlockSpec(memory_space=pltpu.VMEM)
     return pl.pallas_call(
         kernel,
-        in_specs=[pl.BlockSpec(memory_space=pltpu.SMEM)] + [vmem] * (2 + 2 * pieces),
+        in_specs=[pl.BlockSpec(memory_space=pltpu.SMEM)] + [vmem, pl.BlockSpec(memory_space=pltpu.HBM)] + [vmem] * (2 * pieces),
         out_specs=[vmem] * (PARTS * N_Y),
         out_shape=[jax.ShapeDtypeStruct((rows, width), jnp.bfloat16)] * (PARTS * N_Y),
         scratch_shapes=[
             pltpu.VMEM((pieces, positions, head_dim), jnp.bfloat16),
             pltpu.VMEM((pieces, positions, head_dim), jnp.bfloat16),
             pltpu.VMEM((pieces, heads * rows, positions), jnp.float32),
+            pltpu.VMEM(o_weight.shape, jnp.bfloat16),
+            pltpu.SemaphoreType.DMA((COPIES,)),
         ],
-        compiler_params=pltpu.CompilerParams(vmem_limit_bytes=24 * 2**20),
+        compiler_params=pltpu.CompilerParams(vmem_limit_bytes=ATTEND_GRANT * 2**20),
         cost_estimate=pl.CostEstimate(
             flops=2 * rows * features * o_weight.shape[0] + 8 * heads * rows * pieces * positions * head_dim,
             bytes_accessed=2 * o_weight.size + 4 * pieces * row[0].size,
             transcendentals=0,
         ),
-    )(place, projected, o_weight, *row, *other)
+    )(
+        place,
+        pltpu.with_memory_space_constraint(projected, pltpu.VMEM),
+        pltpu.with_memory_space_constraint(o_weight, pltpu.HBM),
+        *row,
+        *other,
+    )
 
 
 def add_up(parts):
@@ -355,14 +347,14 @@
     owner_index,
 ):
     step_count, samples, _ = new_states.shape
-    project_all = lambda gain: project(
-        new_states, gain, q_weight, k_weight, v_weight, prompt_keys.shape[1]
+    project_all = lambda: project(
+        new_states, attn_gain, q_weight, k_weight, v_weight, prompt_keys.shape[1]
     )
     piece, has_keys, projected = broadcast(
-        prompt_keys[0], prompt_values[0], owner_index[0], attn_gain, project_all
-    )
-    row, other, (projected, o_near) = from_row(piece, projected, o_weight)
-    partial_blocks = attend(projected, row, other, has_keys, o_near, step_count)
+        prompt_keys[0], prompt_values[0], owner_index[0], project_all
+    )
+    row, other = from_row(piece)
+    partial_blocks = attend(projected, row, other, has_keys, o_weight, step_count)
     summed = lay_out(add_up([partial_blocks[i * N_Y : (i + 1) * N_Y] for i in range(PARTS)]))
     return summed.reshape(step_count, samples, o_weight.shape[1])
 

time: 79.2 us -> 76 us (0.960); the launches traced: 79.4 us -> 75.3 us
  waiting for transfers between devices: 16.3 us -> 32.6 us
  starting transfers between devices: 44.7 us -> 29.4 us
  local copies, waits for them, and re-layouts: 5.44 us -> 1.04 us
    ppermute x28, waiting for transfers between devices: 16.3 us -> 32.6 us  [send(): return lax.ppermute(block, AXES, pairs)]
    ppermute x28, starting transfers between devices: 44.7 us -> 29.4 us  [send(): return lax.ppermute(block, AXES, pairs)]
    unnamed x6 -> x2, local copies, waits for them, and re-layouts: 4.14 us -> 1.04 us
    reshape x1 -> x0, local copies, waits for them, and re-layouts: 1.3 us -> none  [broadcast(): gain.reshape(1, -1)]
  transfers between devices with their start and end apart: 28 -> 28, of which waited for: 10 -> 12; matrix products, arithmetic and copies ran while one was open for 2% -> 0% of each run, Pallas kernels for 9% -> 8%
where the time goes in v3:
time: 76 us; the launch traced here: 75.3 us
  waiting for transfers between devices  32.6 us (43%)
  starting transfers between devices  29.4 us (39%)
  Pallas kernels  11.1 us (15%)
  local copies, waits for them, and re-layouts  1.04 us (1%)
  between operations  0.8 us (1%)
    ppermute x28, waiting for transfers between devices, send(): return lax.ppermute(block, AXES, pairs)  32.6 us
    ppermute x28, starting transfers between devices, send(): return lax.ppermute(block, AXES, pairs)  29.4 us
    pallas_call x1, Pallas kernels, project(): pl.pallas_call(kernel, in_specs=[anywhere, VMEM, VMEM, VMEM, anywhere, an...  6.19 us
    pallas_call x1, Pallas kernels, attend(): pl.pallas_call(kernel, in_specs=[pl.BlockSpec(memory_space=pltpu.SMEM)] +...  3.88 us
  transfers between devices with their start and end apart: 28, of which 12 were waited for; matrix products, arithmetic and copies ran while one was open for 0% of the time, Pallas kernels for 8%

profile of v3, /device:TPU:32, one launch (start us, length us, event | category | flops | bytes accessed | tf_op | source)
XLA Modules:
  0.0 75.3 jit_solution(6843101616929762505)
XLA Ops:
  0.0 0.0 collective-permute-start.12
  0.7 1.4 %collective-permute-done.12.values_ref = bf16[2048,128]{1,0:T(8,128)(2,1)S(1)} collective-permute-done((bf16[2048,128]{1,0:T(8,128)(2,1)}, bf16[2048,128]{1,0:T(8,128)(2,1)S(1)}, u32[]{:S(2)}, u32[]{:S(2)}) %collective-permute-start.12) | collective-permute-done | bytes 524320 | tf_op jit(solution)/shard_map/ppermute | solution.py:39
  2.1 1.0 %copy-done = bf16[1,2048,128]{2,1,0:T(8,128)(2,1)S(1)} copy-done((bf16[1,2048,128]{2,1,0:T(8,128)(2,1)S(1)}, bf16[1,2048,128]{2,1,0:T(8,128)(2,1)}, u32[]{:S(2)}) %copy-start) | copy-done | bytes 524312
  3.2 1.6 %collective-permute-start.13 = (bf16[512,128]{1,0:T(8,128)(2,1)S(1)}, bf16[512,128]{1,0:T(8,128)(2,1)S(1)}, u32[]{:S(2)}, u32[]{:S(2)}) collective-permute-start(bf16[512,128]{1,0:T(8,128)(2,1)S(1)} %get-tuple-element.52), channel_id=1, source_target_pairs={{0,64},{1,65},{2,66},{3,67},{4,68},{5,69},{6,70},{7,71},{8,72},{9,... | collective-permute-start | bytes 393224 | tf_op jit(solution)/shard_map/ppermute | solution.py:39
  4.8 2.7 %collective-permute-start.14 = (bf16[512,128]{1,0:T(8,128)(2,1)S(1)}, bf16[512,128]{1,0:T(8,128)(2,1)S(1)}, u32[]{:S(2)}, u32[]{:S(2)}) collective-permute-start(bf16[512,128]{1,0:T(8,128)(2,1)S(1)} %get-tuple-element.53), channel_id=1, source_target_pairs={{0,128},{1,129},{2,130},{3,131},{4,132},{5,133},{6,134},{7,135},{8... | collective-permute-start | bytes 393224 | tf_op jit(solution)/shard_map/ppermute | solution.py:39
  7.5 1.4 %collective-permute-start.15 = (bf16[512,128]{1,0:T(8,128)(2,1)S(1)}, bf16[512,128]{1,0:T(8,128)(2,1)S(1)}, u32[]{:S(2)}, u32[]{:S(2)}) collective-permute-start(bf16[512,128]{1,0:T(8,128)(2,1)S(1)} %get-tuple-element.54), channel_id=1, source_target_pairs={{0,192},{1,193},{2,194},{3,195},{4,196},{5,197},{6,198},{7,199},{8... | collective-permute-start | bytes 393224 | tf_op jit(solution)/shard_map/ppermute | solution.py:39
  8.9 6.2 %shard_map.110.qkv_ref = bf16[6,96,128]{2,1,0:T(8,128)(2,1)S(1)} custom-call(bf16[96,4096]{1,0:T(8,128)(2,1)} %bitcast.19, bf16[32,128]{1,0:T(8,128)(2,1)} %bitcast.20, f32[96,128]{1,0:T(8,128)} %constant.141.clone.cos_ref, f32[96,128]{1,0:T(8,128)} %constant.142.clone.sin_ref, bf16[4096,512]{1,0:T(8,128)(2,1)} %wq_hbm.1, bf16[4096,128]{1,0:T(8,128)(2,1)} %wk_hbm.1, ...), custom_call_target="tpu_custom_call" | custom-call | flops 603979776 | bytes 7077888 | tf_op jit(solution)/shard_map/pallas_call | solution.py:177
  15.1 0.0 collective-permute-done.13.refs_1_
  15.2 0.0 collective-permute-done.14.refs_2_
  15.2 0.0 collective-permute-done.15.refs_3_
  15.2 15.3 %conditional.1 = (bf16[512,128]{1,0:T(8,128)(2,1)S(1)}) conditional(s32[]{:T(128)} %clamp.3, (s32[]{:T(128)}, bf16[512,128]{1,0:T(8,128)(2,1)S(1)}) %tuple.19, (s32[]{:T(128)}, bf16[512,128]{1,0:T(8,128)(2,1)S(1)}) %tuple.19, (s32[]{:T(128)}, bf16[512,128]{1,0:T(8,128)(2,1)S(1)}) %tuple.19, (s32[]{:T(128)}, ...), branch_computations={%region_0.1_spmd, %region_1.2_spmd, %region_2.3_spmd, %region_3.4_... | conditional | flops 8 | bytes 1573074 | solution.py:93
  15.3 1.3 %collective-permute-start.11 = (bf16[512,128]{1,0:T(8,128)(2,1)S(1)}, bf16[512,128]{1,0:T(8,128)(2,1)S(1)}, u32[]{:S(2)}, u32[]{:S(2)}) collective-permute-start(bf16[512,128]{1,0:T(8,128)(2,1)S(1)} %get-tuple-element.33.refs_0_), channel_id=1, source_target_pairs={{48,0},{49,1},{50,2},{51,3},{52,4},{53,5},{54,6},{55,7},{56,8},{57... | collective-permute-start | bytes 393224 | tf_op jit(solution)/shard_map/cond/branch_3_fun/ppermute | solution.py:39
  16.6 0.7 collective-permute-start.10
  17.2 0.7 collective-permute-start.9
  17.9 12.6 %collective-permute-done.11.refs_3_ = bf16[512,128]{1,0:T(8,128)(2,1)S(1)} collective-permute-done((bf16[512,128]{1,0:T(8,128)(2,1)S(1)}, bf16[512,128]{1,0:T(8,128)(2,1)S(1)}, u32[]{:S(2)}, u32[]{:S(2)}) %collective-permute-start.11) | collective-permute-done | bytes 131104 | tf_op jit(solution)/shard_map/cond/branch_3_fun/ppermute | solution.py:39
  30.5 0.0 collective-permute-done.10.refs_2_
  30.5 0.0 collective-permute-done.9.refs_1_
  30.5 1.1 %collective-permute-start.18 = (bf16[512,128]{1,0:T(8,128)(2,1)S(1)}, bf16[512,128]{1,0:T(8,128)(2,1)S(1)}, u32[]{:S(2)}, u32[]{:S(2)}) collective-permute-start(bf16[512,128]{1,0:T(8,128)(2,1)S(1)} %get-tuple-element.68.rest_0_), channel_id=1, source_target_pairs={{0,128},{1,129},{2,130},{3,131},{4,132},{5,133},{6,134},{7,135},{8... | collective-permute-start | bytes 393224 | tf_op jit(solution)/shard_map/ppermute | solution.py:39
  31.6 2.2 %collective-permute-start.17 = (bf16[512,128]{1,0:T(8,128)(2,1)S(1)}, bf16[512,128]{1,0:T(8,128)(2,1)S(1)}, u32[]{:S(2)}, u32[]{:S(2)}) collective-permute-start(bf16[512,128]{1,0:T(8,128)(2,1)S(1)} %get-tuple-element.68.rest_0_), channel_id=1, source_target_pairs={{0,192},{1,193},{2,194},{3,195},{4,196},{5,197},{6,198},{7,199},{8... | collective-permute-start | bytes 393224 | tf_op jit(solution)/shard_map/ppermute | solution.py:39
  33.9 0.0 collective-permute-start.16
  33.9 0.0 collective-permute-start.19
  33.9 4.6 %collective-permute-done.18.rest_3_ = bf16[512,128]{1,0:T(8,128)(2,1)S(1)} collective-permute-done((bf16[512,128]{1,0:T(8,128)(2,1)S(1)}, bf16[512,128]{1,0:T(8,128)(2,1)S(1)}, u32[]{:S(2)}, u32[]{:S(2)}) %collective-permute-start.18) | collective-permute-done | bytes 131104 | tf_op jit(solution)/shard_map/ppermute | solution.py:39
  38.5 0.0 collective-permute-start.22
  38.5 0.0 collective-permute-done.17.rest_2_
  38.5 0.5 collective-permute-start.21
  39.0 1.4 %collective-permute-done.16.rest_1_ = bf16[512,128]{1,0:T(8,128)(2,1)S(1)} collective-permute-done((bf16[512,128]{1,0:T(8,128)(2,1)S(1)}, bf16[512,128]{1,0:T(8,128)(2,1)S(1)}, u32[]{:S(2)}, u32[]{:S(2)}) %collective-permute-start.16) | collective-permute-done | bytes 131104 | tf_op jit(solution)/shard_map/ppermute | solution.py:39
  40.4 0.0 collective-permute-start.20
  40.4 0.1 pad_add_fusion.place_ref
  40.4 0.0 collective-permute-done.19.rest_4_
  40.4 0.0 collective-permute-done.22.rest_7_
  40.4 0.0 collective-permute-done.21.rest_6_
  40.5 1.3 %collective-permute-done.20.rest_5_ = bf16[512,128]{1,0:T(8,128)(2,1)S(1)} collective-permute-done((bf16[512,128]{1,0:T(8,128)(2,1)S(1)}, bf16[512,128]{1,0:T(8,128)(2,1)S(1)}, u32[]{:S(2)}, u32[]{:S(2)}) %collective-permute-start.20) | collective-permute-done | bytes 131104 | tf_op jit(solution)/shard_map/ppermute | solution.py:39
  41.7 3.9 %shard_map.112 = (bf16[96,512]{1,0:T(8,128)(2,1)S(1)}, bf16[96,512]{1,0:T(8,128)(2,1)S(1)}, bf16[96,512]{1,0:T(8,128)(2,1)S(1)}, bf16[96,512]{1,0:T(8,128)(2,1)S...) custom-call(s32[2]{0:T(128)S(1)} %pad_add_fusion.place_ref, ...), custom_call_target="tpu_custom_call" | custom-call | flops 1207959552 | bytes 5242880 | tf_op jit(solution)/shard_map/pallas_call | solution.py:281
  45.6 1.7 %collective-permute-start.23 = (bf16[96,512]{1,0:T(8,128)(2,1)S(1)}, bf16[96,512]{1,0:T(8,128)(2,1)S(1)}, u32[]{:S(2)}, u32[]{:S(2)}) collective-permute-start(bf16[96,512]{1,0:T(8,128)(2,1)S(1)} %get-tuple-element.61), channel_id=1, source_target_pairs={{0,1},{1,2},{2,3},{3,0},{4,5},{5,6},{6,7},{7,4},{8,9},{9,10},{10,1... | collective-permute-start | bytes 294920 | tf_op jit(solution)/shard_map/ppermute | solution.py:39
  47.3 2.9 %collective-permute-start.24 = (bf16[96,512]{1,0:T(8,128)(2,1)S(1)}, bf16[96,512]{1,0:T(8,128)(2,1)S(1)}, u32[]{:S(2)}, u32[]{:S(2)}) collective-permute-start(bf16[96,512]{1,0:T(8,128)(2,1)S(1)} %get-tuple-element.62), channel_id=1, source_target_pairs={{0,2},{1,3},{2,0},{3,1},{4,6},{5,7},{6,4},{7,5},{8,10},{9,11},{10,... | collective-permute-start | bytes 294920 | tf_op jit(solution)/shard_map/ppermute | solution.py:39
  50.2 1.3 %collective-permute-start.25 = (bf16[96,512]{1,0:T(8,128)(2,1)S(1)}, bf16[96,512]{1,0:T(8,128)(2,1)S(1)}, u32[]{:S(2)}, u32[]{:S(2)}) collective-permute-start(bf16[96,512]{1,0:T(8,128)(2,1)S(1)} %get-tuple-element.63), channel_id=1, source_target_pairs={{0,3},{1,0},{2,1},{3,2},{4,7},{5,4},{6,5},{7,6},{8,11},{9,8},{10,9... | collective-permute-start | bytes 294920 | tf_op jit(solution)/shard_map/ppermute | solution.py:39
  51.5 0.7 collective-permute-start.30
  52.2 0.8 %collective-permute-start.31 = (bf16[96,512]{1,0:T(8,128)(2,1)S(1)}, bf16[96,512]{1,0:T(8,128)(2,1)S(1)}, u32[]{:S(2)}, u32[]{:S(2)}) collective-permute-start(bf16[96,512]{1,0:T(8,128)(2,1)S(1)} %get-tuple-element.66), channel_id=1, source_target_pairs={{0,2},{1,3},{2,0},{3,1},{4,6},{5,7},{6,4},{7,5},{8,10},{9,11},{10,... | collective-permute-start | bytes 294920 | tf_op jit(solution)/shard_map/ppermute | solution.py:39
  53.0 0.0 collective-permute-done.23
  53.0 1.9 %collective-permute-start.32 = (bf16[96,512]{1,0:T(8,128)(2,1)S(1)}, bf16[96,512]{1,0:T(8,128)(2,1)S(1)}, u32[]{:S(2)}, u32[]{:S(2)}) collective-permute-start(bf16[96,512]{1,0:T(8,128)(2,1)S(1)} %get-tuple-element.67), channel_id=1, source_target_pairs={{0,3},{1,0},{2,1},{3,2},{4,7},{5,4},{6,5},{7,6},{8,11},{9,8},{10,9... | collective-permute-start | bytes 294920 | tf_op jit(solution)/shard_map/ppermute | solution.py:39
  54.9 1.0 %collective-permute-done.24 = bf16[96,512]{1,0:T(8,128)(2,1)S(1)} collective-permute-done((bf16[96,512]{1,0:T(8,128)(2,1)S(1)}, bf16[96,512]{1,0:T(8,128)(2,1)S(1)}, u32[]{:S(2)}, u32[]{:S(2)}) %collective-permute-start.24) | collective-permute-done | bytes 98336 | tf_op jit(solution)/shard_map/ppermute | solution.py:39
  55.9 0.0 collective-permute-done.25
  55.9 0.1 add_convert_fusion.3
  55.9 0.1 collective-permute-start.26
  56.0 3.4 %collective-permute-done.30 = bf16[96,512]{1,0:T(8,128)(2,1)S(1)} collective-permute-done((bf16[96,512]{1,0:T(8,128)(2,1)S(1)}, bf16[96,512]{1,0:T(8,128)(2,1)S(1)}, u32[]{:S(2)}, u32[]{:S(2)}) %collective-permute-start.30) | collective-permute-done | bytes 98336 | tf_op jit(solution)/shard_map/ppermute | solution.py:39
  59.5 0.0 collective-permute-done.31
  59.5 0.0 collective-permute-done.32
  59.5 0.1 add_convert_fusion.1
  59.5 0.1 collective-permute-start.33
  59.6 1.0 %collective-permute-done.26 = bf16[96,512]{1,0:T(8,128)(2,1)S(1)} collective-permute-done((bf16[96,512]{1,0:T(8,128)(2,1)S(1)}, bf16[96,512]{1,0:T(8,128)(2,1)S(1)}, u32[]{:S(2)}, u32[]{:S(2)}) %collective-permute-start.26) | collective-permute-done | bytes 98336 | tf_op jit(solution)/shard_map/ppermute | solution.py:39
  60.7 1.5 %collective-permute-start.29 = (bf16[96,512]{1,0:T(8,128)(2,1)S(1)}, bf16[96,512]{1,0:T(8,128)(2,1)S(1)}, u32[]{:S(2)}, u32[]{:S(2)}) collective-permute-start(bf16[96,512]{1,0:T(8,128)(2,1)S(1)} %add_convert_fusion.2.rest_0_), channel_id=1, source_target_pairs={{0,3},{1,0},{2,1},{3,2},{4,7},{5,4},{6,5},{7,6},{8,11},{9,8},{10,9... | collective-permute-start | bytes 294920 | tf_op jit(solution)/shard_map/ppermute | solution.py:39
  62.2 1.6 %collective-permute-start.28 = (bf16[96,512]{1,0:T(8,128)(2,1)S(1)}, bf16[96,512]{1,0:T(8,128)(2,1)S(1)}, u32[]{:S(2)}, u32[]{:S(2)}) collective-permute-start(bf16[96,512]{1,0:T(8,128)(2,1)S(1)} %add_convert_fusion.2.rest_0_), channel_id=1, source_target_pairs={{0,2},{1,3},{2,0},{3,1},{4,6},{5,7},{6,4},{7,5},{8,10},{9,11},{10,... | collective-permute-start | bytes 294920 | tf_op jit(solution)/shard_map/ppermute | solution.py:39
  63.8 1.3 %collective-permute-start.27 = (bf16[96,512]{1,0:T(8,128)(2,1)S(1)}, bf16[96,512]{1,0:T(8,128)(2,1)S(1)}, u32[]{:S(2)}, u32[]{:S(2)}) collective-permute-start(bf16[96,512]{1,0:T(8,128)(2,1)S(1)} %add_convert_fusion.2.rest_0_), channel_id=1, source_target_pairs={{0,1},{1,2},{2,3},{3,0},{4,5},{5,6},{6,7},{7,4},{8,9},{9,10},{10,1... | collective-permute-start | bytes 294920 | tf_op jit(solution)/shard_map/ppermute | solution.py:39
  65.1 0.0 collective-permute-done.33
  65.2 2.0 %collective-permute-start.36 = (bf16[96,512]{1,0:T(8,128)(2,1)S(1)}, bf16[96,512]{1,0:T(8,128)(2,1)S(1)}, u32[]{:S(2)}, u32[]{:S(2)}) collective-permute-start(bf16[96,512]{1,0:T(8,128)(2,1)S(1)} %add_convert_fusion.rest_4_), channel_id=1, source_target_pairs={{0,3},{1,0},{2,1},{3,2},{4,7},{5,4},{6,5},{7,6},{8,11},{9,8},{10,9... | collective-permute-start | bytes 294920 | tf_op jit(solution)/shard_map/ppermute | solution.py:39
  67.2 0.7 collective-permute-start.35
  67.9 0.0 collective-permute-done.29.rest_3_
  67.9 0.6 collective-permute-start.34
  68.4 0.5 collective-permute-done.28.rest_2_
  68.9 2.5 %collective-permute-done.27.rest_1_ = bf16[96,512]{1,0:T(8,128)(2,1)S(1)} collective-permute-done((bf16[96,512]{1,0:T(8,128)(2,1)S(1)}, bf16[96,512]{1,0:T(8,128)(2,1)S(1)}, u32[]{:S(2)}, u32[]{:S(2)}) %collective-permute-start.27) | collective-permute-done | bytes 98336 | tf_op jit(solution)/shard_map/ppermute | solution.py:39
  71.5 0.0 collective-permute-done.36.rest_7_
  71.5 1.9 %collective-permute-done.35.rest_6_ = bf16[96,512]{1,0:T(8,128)(2,1)S(1)} collective-permute-done((bf16[96,512]{1,0:T(8,128)(2,1)S(1)}, bf16[96,512]{1,0:T(8,128)(2,1)S(1)}, u32[]{:S(2)}, u32[]{:S(2)}) %collective-permute-start.35) | collective-permute-done | bytes 98336 | tf_op jit(solution)/shard_map/ppermute | solution.py:39
  73.4 1.0 %collective-permute-done.34.rest_5_ = bf16[96,512]{1,0:T(8,128)(2,1)S(1)} collective-permute-done((bf16[96,512]{1,0:T(8,128)(2,1)S(1)}, bf16[96,512]{1,0:T(8,128)(2,1)S(1)}, u32[]{:S(2)}, u32[]{:S(2)}) %collective-permute-start.34) | collective-permute-done | bytes 98336 | tf_op jit(solution)/shard_map/ppermute | solution.py:39
  74.3 0.9 %shard_map.113 = bf16[96,4096]{1,0:T(8,128)(2,1)} custom-call(s32[1]{0:T(128)S(6)} %select_n.46.y_ref, bf16[96,512]{1,0:T(8,128)(2,1)S(1)} %add_convert_fusion.2.rest_0_, bf16[96,512]{1,0:T(8,128)(2,1)S(1)} %collective-permute-done.27.rest_1_, bf16[96,512]{1,0:T(8,128)(2,1)S(1)} %collective-permute-done.28.rest_2_, ...), custom_call_target="tpu_custom_call" | custom-call | tf_op jit(solution)/shard_map/pallas_call | solution.py:329
  (6 shorter events, 0.1 us)
Async XLA Ops:
  0.0 2.1 %collective-permute-start.12 = (bf16[2048,128]{1,0:T(8,128)(2,1)}, bf16[2048,128]{1,0:T(8,128)(2,1)S(1)}, u32[]{:S(2)}, u32[]{:S(2)}) collective-permute-start(bf16[2048,128]{1,0:T(8,128)(2,1)} %bitcast.21), channel_id=1, source_target_pairs={{0,8},{1,9},{2,10},{3,11},{4,12},{5,13},{6,14},{7,15},{8,0},{9,1},... | collective-permute-start | bytes 1572872 | tf_op jit(solution)/shard_map/ppermute | solution.py:39
  2.1 1.0 %copy-start = (bf16[1,2048,128]{2,1,0:T(8,128)(2,1)S(1)}, bf16[1,2048,128]{2,1,0:T(8,128)(2,1)}, u32[]{:S(2)}) copy-start(bf16[1,2048,128]{2,1,0:T(8,128)(2,1)} %param.21) | copy-start | bytes 1572868
  3.2 11.9 %collective-permute-start.13 = (bf16[512,128]{1,0:T(8,128)(2,1)S(1)}, bf16[512,128]{1,0:T(8,128)(2,1)S(1)}, u32[]{:S(2)}, u32[]{:S(2)}) collective-permute-start(bf16[512,128]{1,0:T(8,128)(2,1)S(1)} %get-tuple-element.52), channel_id=1, source_target_pairs={{0,64},{1,65},{2,66},{3,67},{4,68},{5,69},{6,70},{7,71},{8,72},{9,... | collective-permute-start | bytes 393224 | tf_op jit(solution)/shard_map/ppermute | solution.py:39
  4.8 10.4 %collective-permute-start.14 = (bf16[512,128]{1,0:T(8,128)(2,1)S(1)}, bf16[512,128]{1,0:T(8,128)(2,1)S(1)}, u32[]{:S(2)}, u32[]{:S(2)}) collective-permute-start(bf16[512,128]{1,0:T(8,128)(2,1)S(1)} %get-tuple-element.53), channel_id=1, source_target_pairs={{0,128},{1,129},{2,130},{3,131},{4,132},{5,133},{6,134},{7,135},{8... | collective-permute-start | bytes 393224 | tf_op jit(solution)/shard_map/ppermute | solution.py:39
  7.5 7.7 %collective-permute-start.15 = (bf16[512,128]{1,0:T(8,128)(2,1)S(1)}, bf16[512,128]{1,0:T(8,128)(2,1)S(1)}, u32[]{:S(2)}, u32[]{:S(2)}) collective-permute-start(bf16[512,128]{1,0:T(8,128)(2,1)S(1)} %get-tuple-element.54), channel_id=1, source_target_pairs={{0,192},{1,193},{2,194},{3,195},{4,196},{5,197},{6,198},{7,199},{8... | collective-permute-start | bytes 393224 | tf_op jit(solution)/shard_map/ppermute | solution.py:39
  15.3 15.2 %collective-permute-start.11 = (bf16[512,128]{1,0:T(8,128)(2,1)S(1)}, bf16[512,128]{1,0:T(8,128)(2,1)S(1)}, u32[]{:S(2)}, u32[]{:S(2)}) collective-permute-start(bf16[512,128]{1,0:T(8,128)(2,1)S(1)} %get-tuple-element.33.refs_0_), channel_id=1, source_target_pairs={{48,0},{49,1},{50,2},{51,3},{52,4},{53,5},{54,6},{55,7},{56,8},{57... | collective-permute-start | bytes 393224 | tf_op jit(solution)/shard_map/cond/branch_3_fun/ppermute | solution.py:39
  16.6 13.9 %collective-permute-start.10 = (bf16[512,128]{1,0:T(8,128)(2,1)S(1)}, bf16[512,128]{1,0:T(8,128)(2,1)S(1)}, u32[]{:S(2)}, u32[]{:S(2)}) collective-permute-start(bf16[512,128]{1,0:T(8,128)(2,1)S(1)} %get-tuple-element.33.refs_0_), channel_id=1, source_target_pairs={{48,32},{49,33},{50,34},{51,35},{52,36},{53,37},{54,38},{55,39},{5... | collective-permute-start | bytes 393224 | tf_op jit(solution)/shard_map/cond/branch_3_fun/ppermute | solution.py:39
  17.2 13.3 %collective-permute-start.9 = (bf16[512,128]{1,0:T(8,128)(2,1)S(1)}, bf16[512,128]{1,0:T(8,128)(2,1)S(1)}, u32[]{:S(2)}, u32[]{:S(2)}) collective-permute-start(bf16[512,128]{1,0:T(8,128)(2,1)S(1)} %get-tuple-element.33.refs_0_), channel_id=1, source_target_pairs={{48,16},{49,17},{50,18},{51,19},{52,20},{53,21},{54,22},{55,23},{5... | collective-permute-start | bytes 393224 | tf_op jit(solution)/shard_map/cond/branch_3_fun/ppermute | solution.py:39
  30.5 7.9 %collective-permute-start.18 = (bf16[512,128]{1,0:T(8,128)(2,1)S(1)}, bf16[512,128]{1,0:T(8,128)(2,1)S(1)}, u32[]{:S(2)}, u32[]{:S(2)}) collective-permute-start(bf16[512,128]{1,0:T(8,128)(2,1)S(1)} %get-tuple-element.68.rest_0_), channel_id=1, source_target_pairs={{0,128},{1,129},{2,130},{3,131},{4,132},{5,133},{6,134},{7,135},{8... | collective-permute-start | bytes 393224 | tf_op jit(solution)/shard_map/ppermute | solution.py:39
  31.6 6.8 %collective-permute-start.17 = (bf16[512,128]{1,0:T(8,128)(2,1)S(1)}, bf16[512,128]{1,0:T(8,128)(2,1)S(1)}, u32[]{:S(2)}, u32[]{:S(2)}) collective-permute-start(bf16[512,128]{1,0:T(8,128)(2,1)S(1)} %get-tuple-element.68.rest_0_), channel_id=1, source_target_pairs={{0,192},{1,193},{2,194},{3,195},{4,196},{5,197},{6,198},{7,199},{8... | collective-permute-start | bytes 393224 | tf_op jit(solution)/shard_map/ppermute | solution.py:39
  33.9 6.5 %collective-permute-start.16 = (bf16[512,128]{1,0:T(8,128)(2,1)S(1)}, bf16[512,128]{1,0:T(8,128)(2,1)S(1)}, u32[]{:S(2)}, u32[]{:S(2)}) collective-permute-start(bf16[512,128]{1,0:T(8,128)(2,1)S(1)} %get-tuple-element.68.rest_0_), channel_id=1, source_target_pairs={{0,64},{1,65},{2,66},{3,67},{4,68},{5,69},{6,70},{7,71},{8,72},{9,... | collective-permute-start | bytes 393224 | tf_op jit(solution)/shard_map/ppermute | solution.py:39
  33.9 6.6 %collective-permute-start.19 = (bf16[512,128]{1,0:T(8,128)(2,1)S(1)}, bf16[512,128]{1,0:T(8,128)(2,1)S(1)}, u32[]{:S(2)}, u32[]{:S(2)}) collective-permute-start(bf16[512,128]{1,0:T(8,128)(2,1)S(1)} %get-tuple-element.68.rest_0_), channel_id=1, source_target_pairs={{0,8},{1,9},{2,10},{3,11},{4,12},{5,13},{6,14},{7,15},{8,0},{9,1},... | collective-permute-start | bytes 393224 | tf_op jit(solution)/shard_map/ppermute | solution.py:39
  38.5 2.0 %collective-permute-start.22 = (bf16[512,128]{1,0:T(8,128)(2,1)S(1)}, bf16[512,128]{1,0:T(8,128)(2,1)S(1)}, u32[]{:S(2)}, u32[]{:S(2)}) collective-permute-start(bf16[512,128]{1,0:T(8,128)(2,1)S(1)} %collective-permute-done.18.rest_3_), channel_id=1, source_target_pairs={{0,8},{1,9},{2,10},{3,11},{4,12},{5,13},{6,14},{7,15},{8,0},{9,1},... | collective-permute-start | bytes 393224 | tf_op jit(solution)/shard_map/ppermute | solution.py:39
  38.5 2.0 %collective-permute-start.21 = (bf16[512,128]{1,0:T(8,128)(2,1)S(1)}, bf16[512,128]{1,0:T(8,128)(2,1)S(1)}, u32[]{:S(2)}, u32[]{:S(2)}) collective-permute-start(bf16[512,128]{1,0:T(8,128)(2,1)S(1)} %collective-permute-done.17.rest_2_), channel_id=1, source_target_pairs={{0,8},{1,9},{2,10},{3,11},{4,12},{5,13},{6,14},{7,15},{8,0},{9,1},... | collective-permute-start | bytes 393224 | tf_op jit(solution)/shard_map/ppermute | solution.py:39
  40.4 1.3 %collective-permute-start.20 = (bf16[512,128]{1,0:T(8,128)(2,1)S(1)}, bf16[512,128]{1,0:T(8,128)(2,1)S(1)}, u32[]{:S(2)}, u32[]{:S(2)}) collective-permute-start(bf16[512,128]{1,0:T(8,128)(2,1)S(1)} %collective-permute-done.16.rest_1_), channel_id=1, source_target_pairs={{0,8},{1,9},{2,10},{3,11},{4,12},{5,13},{6,14},{7,15},{8,0},{9,1},... | collective-permute-start | bytes 393224 | tf_op jit(solution)/shard_map/ppermute | solution.py:39
  45.6 7.4 %collective-permute-start.23 = (bf16[96,512]{1,0:T(8,128)(2,1)S(1)}, bf16[96,512]{1,0:T(8,128)(2,1)S(1)}, u32[]{:S(2)}, u32[]{:S(2)}) collective-permute-start(bf16[96,512]{1,0:T(8,128)(2,1)S(1)} %get-tuple-element.61), channel_id=1, source_target_pairs={{0,1},{1,2},{2,3},{3,0},{4,5},{5,6},{6,7},{7,4},{8,9},{9,10},{10,1... | collective-permute-start | bytes 294920 | tf_op jit(solution)/shard_map/ppermute | solution.py:39
  47.3 8.6 %collective-permute-start.24 = (bf16[96,512]{1,0:T(8,128)(2,1)S(1)}, bf16[96,512]{1,0:T(8,128)(2,1)S(1)}, u32[]{:S(2)}, u32[]{:S(2)}) collective-permute-start(bf16[96,512]{1,0:T(8,128)(2,1)S(1)} %get-tuple-element.62), channel_id=1, source_target_pairs={{0,2},{1,3},{2,0},{3,1},{4,6},{5,7},{6,4},{7,5},{8,10},{9,11},{10,... | collective-permute-start | bytes 294920 | tf_op jit(solution)/shard_map/ppermute | solution.py:39
  50.2 5.7 %collective-permute-start.25 = (bf16[96,512]{1,0:T(8,128)(2,1)S(1)}, bf16[96,512]{1,0:T(8,128)(2,1)S(1)}, u32[]{:S(2)}, u32[]{:S(2)}) collective-permute-start(bf16[96,512]{1,0:T(8,128)(2,1)S(1)} %get-tuple-element.63), channel_id=1, source_target_pairs={{0,3},{1,0},{2,1},{3,2},{4,7},{5,4},{6,5},{7,6},{8,11},{9,8},{10,9... | collective-permute-start | bytes 294920 | tf_op jit(solution)/shard_map/ppermute | solution.py:39
  51.5 8.0 %collective-permute-start.30 = (bf16[96,512]{1,0:T(8,128)(2,1)S(1)}, bf16[96,512]{1,0:T(8,128)(2,1)S(1)}, u32[]{:S(2)}, u32[]{:S(2)}) collective-permute-start(bf16[96,512]{1,0:T(8,128)(2,1)S(1)} %get-tuple-element.65), channel_id=1, source_target_pairs={{0,1},{1,2},{2,3},{3,0},{4,5},{5,6},{6,7},{7,4},{8,9},{9,10},{10,1... | collective-permute-start | bytes 294920 | tf_op jit(solution)/shard_map/ppermute | solution.py:39
  52.2 7.3 %collective-permute-start.31 = (bf16[96,512]{1,0:T(8,128)(2,1)S(1)}, bf16[96,512]{1,0:T(8,128)(2,1)S(1)}, u32[]{:S(2)}, u32[]{:S(2)}) collective-permute-start(bf16[96,512]{1,0:T(8,128)(2,1)S(1)} %get-tuple-element.66), channel_id=1, source_target_pairs={{0,2},{1,3},{2,0},{3,1},{4,6},{5,7},{6,4},{7,5},{8,10},{9,11},{10,... | collective-permute-start | bytes 294920 | tf_op jit(solution)/shard_map/ppermute | solution.py:39
  53.0 6.5 %collective-permute-start.32 = (bf16[96,512]{1,0:T(8,128)(2,1)S(1)}, bf16[96,512]{1,0:T(8,128)(2,1)S(1)}, u32[]{:S(2)}, u32[]{:S(2)}) collective-permute-start(bf16[96,512]{1,0:T(8,128)(2,1)S(1)} %get-tuple-element.67), channel_id=1, source_target_pairs={{0,3},{1,0},{2,1},{3,2},{4,7},{5,4},{6,5},{7,6},{8,11},{9,8},{10,9... | collective-permute-start | bytes 294920 | tf_op jit(solution)/shard_map/ppermute | solution.py:39
  55.9 4.7 %collective-permute-start.26 = (bf16[96,512]{1,0:T(8,128)(2,1)S(1)}, bf16[96,512]{1,0:T(8,128)(2,1)S(1)}, u32[]{:S(2)}, u32[]{:S(2)}) collective-permute-start(bf16[96,512]{1,0:T(8,128)(2,1)S(1)} %add_convert_fusion.3), channel_id=1, source_target_pairs={{0,4},{1,5},{2,6},{3,7},{4,0},{5,1},{6,2},{7,3},{8,12},{9,13},{10,... | collective-permute-start | bytes 294920 | tf_op jit(solution)/shard_map/ppermute | solution.py:39
  59.5 5.6 %collective-permute-start.33 = (bf16[96,512]{1,0:T(8,128)(2,1)S(1)}, bf16[96,512]{1,0:T(8,128)(2,1)S(1)}, u32[]{:S(2)}, u32[]{:S(2)}) collective-permute-start(bf16[96,512]{1,0:T(8,128)(2,1)S(1)} %add_convert_fusion.1), channel_id=1, source_target_pairs={{0,4},{1,5},{2,6},{3,7},{4,0},{5,1},{6,2},{7,3},{8,12},{9,13},{10,... | collective-permute-start | bytes 294920 | tf_op jit(solution)/shard_map/ppermute | solution.py:39
  60.7 7.2 %collective-permute-start.29 = (bf16[96,512]{1,0:T(8,128)(2,1)S(1)}, bf16[96,512]{1,0:T(8,128)(2,1)S(1)}, u32[]{:S(2)}, u32[]{:S(2)}) collective-permute-start(bf16[96,512]{1,0:T(8,128)(2,1)S(1)} %add_convert_fusion.2.rest_0_), channel_id=1, source_target_pairs={{0,3},{1,0},{2,1},{3,2},{4,7},{5,4},{6,5},{7,6},{8,11},{9,8},{10,9... | collective-permute-start | bytes 294920 | tf_op jit(solution)/shard_map/ppermute | solution.py:39
  62.2 6.7 %collective-permute-start.28 = (bf16[96,512]{1,0:T(8,128)(2,1)S(1)}, bf16[96,512]{1,0:T(8,128)(2,1)S(1)}, u32[]{:S(2)}, u32[]{:S(2)}) collective-permute-start(bf16[96,512]{1,0:T(8,128)(2,1)S(1)} %add_convert_fusion.2.rest_0_), channel_id=1, source_target_pairs={{0,2},{1,3},{2,0},{3,1},{4,6},{5,7},{6,4},{7,5},{8,10},{9,11},{10,... | collective-permute-start | bytes 294920 | tf_op jit(solution)/shard_map/ppermute | solution.py:39
  63.8 7.7 %collective-permute-start.27 = (bf16[96,512]{1,0:T(8,128)(2,1)S(1)}, bf16[96,512]{1,0:T(8,128)(2,1)S(1)}, u32[]{:S(2)}, u32[]{:S(2)}) collective-permute-start(bf16[96,512]{1,0:T(8,128)(2,1)S(1)} %add_convert_fusion.2.rest_0_), channel_id=1, source_target_pairs={{0,1},{1,2},{2,3},{3,0},{4,5},{5,6},{6,7},{7,4},{8,9},{9,10},{10,1... | collective-permute-start | bytes 294920 | tf_op jit(solution)/shard_map/ppermute | solution.py:39
  65.2 6.3 %collective-permute-start.36 = (bf16[96,512]{1,0:T(8,128)(2,1)S(1)}, bf16[96,512]{1,0:T(8,128)(2,1)S(1)}, u32[]{:S(2)}, u32[]{:S(2)}) collective-permute-start(bf16[96,512]{1,0:T(8,128)(2,1)S(1)} %add_convert_fusion.rest_4_), channel_id=1, source_target_pairs={{0,3},{1,0},{2,1},{3,2},{4,7},{5,4},{6,5},{7,6},{8,11},{9,8},{10,9... | collective-permute-start | bytes 294920 | tf_op jit(solution)/shard_map/ppermute | solution.py:39
  67.2 6.2 %collective-permute-start.35 = (bf16[96,512]{1,0:T(8,128)(2,1)S(1)}, bf16[96,512]{1,0:T(8,128)(2,1)S(1)}, u32[]{:S(2)}, u32[]{:S(2)}) collective-permute-start(bf16[96,512]{1,0:T(8,128)(2,1)S(1)} %add_convert_fusion.rest_4_), channel_id=1, source_target_pairs={{0,2},{1,3},{2,0},{3,1},{4,6},{5,7},{6,4},{7,5},{8,10},{9,11},{10,... | collective-permute-start | bytes 294920 | tf_op jit(solution)/shard_map/ppermute | solution.py:39
  67.9 6.5 %collective-permute-start.34 = (bf16[96,512]{1,0:T(8,128)(2,1)S(1)}, bf16[96,512]{1,0:T(8,128)(2,1)S(1)}, u32[]{:S(2)}, u32[]{:S(2)}) collective-permute-start(bf16[96,512]{1,0:T(8,128)(2,1)S(1)} %add_convert_fusion.rest_4_), channel_id=1, source_target_pairs={{0,1},{1,2},{2,3},{3,0},{4,5},{5,6},{6,7},{7,4},{8,9},{9,10},{10,1... | collective-permute-start | bytes 294920 | tf_op jit(solution)/shard_map/ppermute | solution.py:39

commit v4 on v3

--- a/solution.py
+++ b/solution.py
@@ -60,6 +60,30 @@
     )(index.reshape(1), *pieces)
 
 
+def bring_in(array):
+    size = array.shape[0] // COPIES
+
+    def kernel(hbm, out, sems):
+        parts = [pl.ds(i * size, size) for i in range(COPIES)]
+        gets = [
+            pltpu.make_async_copy(hbm.at[part, :], out.at[part, :], sems.at[i])
+            for i, part in enumerate(parts)
+        ]
+        for get in gets:
+            get.start()
+        for get in gets:
+            get.wait()
+
+    return pl.pallas_call(
+        kernel,
+        in_specs=[pl.BlockSpec(memory_space=pltpu.HBM)],
+        out_specs=VMEM,
+        out_shape=pltpu.VMEM(array.shape, array.dtype),
+        scratch_shapes=[pltpu.SemaphoreType.DMA((COPIES,))],
+        compiler_params=pltpu.CompilerParams(vmem_limit_bytes=4 * 2**20),
+    )(pltpu.with_memory_space_constraint(array, pltpu.HBM))
+
+
 def slabs_of(first, keys, values):
     size, width = keys.shape[0] // N_X, keys.shape[1]
 
@@ -98,7 +122,8 @@
     core, zh, x = me % N_CORE, me // N_CORE % N_ZH, me // (N_CORE * N_ZH)
     root_core, root_zh, root_x = root % N_CORE, root // N_CORE % N_ZH, root // (N_CORE * N_ZH)
     has_keys = core == root_core
-    slabs = slabs_of(has_keys, keys, send(values, dcore=1))
+    got_values = send(values, dcore=1)
+    slabs = slabs_of(has_keys, bring_in(keys), got_values)
     got = [slabs[0]] + [send(slabs[d], dx=d) for d in (1, 2, 3)]
     got, result = lax.optimization_barrier((got, beside()))
     mine = pick(got, (x - root_x) % N_X)

time: 76 us -> 76.1 us (level)
  Pallas kernels: 11.1 us -> 12.2 us
  local copies, waits for them, and re-layouts: 1.04 us -> 0 us
    pallas_call x0 -> x1, Pallas kernels: none -> 1.13 us  [bring_in(): pl.pallas_call(kernel, in_specs=[pl.BlockSpec(memory_space=pltpu.HBM)], o...]
    unnamed x2 -> x0, local copies, waits for them, and re-layouts: 1.04 us -> none
  transfers between devices with their start and end apart: 28 -> 28, of which waited for: 12 -> 12; matrix products, arithmetic and copies ran while one was open for 0% -> 0% of each run, Pallas kernels for 8% -> 10%
where the time goes in v4:
time: 76.1 us; the launch traced here: 75.3 us
  waiting for transfers between devices  32.6 us (43%)
  starting transfers between devices  29.4 us (39%)
  Pallas kernels  12.2 us (16%)
  between operations  0.81 us (1%)
    ppermute x28, waiting for transfers between devices, send(): return lax.ppermute(block, AXES, pairs)  32.6 us
    ppermute x28, starting transfers between devices, send(): return lax.ppermute(block, AXES, pairs)  29.4 us
    pallas_call x1, Pallas kernels, project(): pl.pallas_call(kernel, in_specs=[anywhere, VMEM, VMEM, VMEM, anywhere, an...  6.19 us
    pallas_call x1, Pallas kernels, attend(): pl.pallas_call(kernel, in_specs=[pl.BlockSpec(memory_space=pltpu.SMEM)] +...  3.88 us
  transfers between devices with their start and end apart: 28, of which 12 were waited for; matrix products, arithmetic and copies ran while one was open for 0% of the time, Pallas kernels for 10%

profile of v4, /device:TPU:32, one launch (start us, length us, event | category | flops | bytes accessed | tf_op | source)
XLA Modules:
  0.0 75.3 jit_solution(6924845253776571190)
XLA Ops:
  0.0 0.0 collective-permute-start.12
  0.7 1.1 %shard_map.109.keys_ref = bf16[2048,128]{1,0:T(8,128)(2,1)S(1)} custom-call(bf16[2048,128]{1,0:T(8,128)(2,1)} %bitcast.19), custom_call_target="tpu_custom_call" | custom-call | tf_op jit(solution)/shard_map/pallas_call | solution.py:77
  1.8 0.3 collective-permute-done.12.values_ref
  2.2 1.6 %collective-permute-start.13 = (bf16[512,128]{1,0:T(8,128)(2,1)S(1)}, bf16[512,128]{1,0:T(8,128)(2,1)S(1)}, u32[]{:S(2)}, u32[]{:S(2)}) collective-permute-start(bf16[512,128]{1,0:T(8,128)(2,1)S(1)} %get-tuple-element.52), channel_id=1, source_target_pairs={{0,64},{1,65},{2,66},{3,67},{4,68},{5,69},{6,70},{7,71},{8,72},{9,... | collective-permute-start | bytes 393224 | tf_op jit(solution)/shard_map/ppermute | solution.py:39
  3.7 2.7 %collective-permute-start.14 = (bf16[512,128]{1,0:T(8,128)(2,1)S(1)}, bf16[512,128]{1,0:T(8,128)(2,1)S(1)}, u32[]{:S(2)}, u32[]{:S(2)}) collective-permute-start(bf16[512,128]{1,0:T(8,128)(2,1)S(1)} %get-tuple-element.53), channel_id=1, source_target_pairs={{0,128},{1,129},{2,130},{3,131},{4,132},{5,133},{6,134},{7,135},{8... | collective-permute-start | bytes 393224 | tf_op jit(solution)/shard_map/ppermute | solution.py:39
  6.5 1.4 %collective-permute-start.15 = (bf16[512,128]{1,0:T(8,128)(2,1)S(1)}, bf16[512,128]{1,0:T(8,128)(2,1)S(1)}, u32[]{:S(2)}, u32[]{:S(2)}) collective-permute-start(bf16[512,128]{1,0:T(8,128)(2,1)S(1)} %get-tuple-element.54), channel_id=1, source_target_pairs={{0,192},{1,193},{2,194},{3,195},{4,196},{5,197},{6,198},{7,199},{8... | collective-permute-start | bytes 393224 | tf_op jit(solution)/shard_map/ppermute | solution.py:39
  7.9 6.2 %shard_map.111.qkv_ref = bf16[6,96,128]{2,1,0:T(8,128)(2,1)S(1)} custom-call(bf16[96,4096]{1,0:T(8,128)(2,1)} %bitcast.18, bf16[32,128]{1,0:T(8,128)(2,1)} %bitcast.20, f32[96,128]{1,0:T(8,128)} %constant.141.clone.cos_ref, f32[96,128]{1,0:T(8,128)} %constant.142.clone.sin_ref, bf16[4096,512]{1,0:T(8,128)(2,1)} %wq_hbm.1, bf16[4096,128]{1,0:T(8,128)(2,1)} %wk_hbm.1, ...), custom_call_target="tpu_custom_call" | custom-call | flops 603979776 | bytes 7077888 | tf_op jit(solution)/shard_map/pallas_call | solution.py:202
  14.1 0.0 collective-permute-done.13.refs_1_
  14.1 0.0 collective-permute-done.14.refs_2_
  14.1 0.0 collective-permute-done.15.refs_3_
  14.2 16.7 %conditional.1 = (bf16[512,128]{1,0:T(8,128)(2,1)S(1)}) conditional(s32[]{:T(128)} %clamp.3, (s32[]{:T(128)}, bf16[512,128]{1,0:T(8,128)(2,1)S(1)}) %tuple.19, (s32[]{:T(128)}, bf16[512,128]{1,0:T(8,128)(2,1)S(1)}) %tuple.19, (s32[]{:T(128)}, bf16[512,128]{1,0:T(8,128)(2,1)S(1)}) %tuple.19, (s32[]{:T(128)}, ...), branch_computations={%region_0.1_spmd, %region_1.2_spmd, %region_2.3_spmd, %region_3.4_... | conditional | flops 8 | bytes 1573074 | solution.py:117
  14.2 0.7 collective-permute-start.8
  14.9 0.7 collective-permute-start.7
  15.6 1.3 %collective-permute-start.6 = (bf16[512,128]{1,0:T(8,128)(2,1)S(1)}, bf16[512,128]{1,0:T(8,128)(2,1)S(1)}, u32[]{:S(2)}, u32[]{:S(2)}) collective-permute-start(bf16[512,128]{1,0:T(8,128)(2,1)S(1)} %get-tuple-element.31.refs_0_), channel_id=1, source_target_pairs={{32,0},{33,1},{34,2},{35,3},{36,4},{37,5},{38,6},{39,7},{40,8},{41... | collective-permute-start | bytes 393224 | tf_op jit(solution)/shard_map/cond/branch_2_fun/ppermute | solution.py:39
  16.9 0.0 collective-permute-done.8.refs_3_
  16.9 0.0 collective-permute-done.7.refs_2_
  16.9 14.0 %collective-permute-done.6.refs_1_ = bf16[512,128]{1,0:T(8,128)(2,1)S(1)} collective-permute-done((bf16[512,128]{1,0:T(8,128)(2,1)S(1)}, bf16[512,128]{1,0:T(8,128)(2,1)S(1)}, u32[]{:S(2)}, u32[]{:S(2)}) %collective-permute-start.6) | collective-permute-done | bytes 131104 | tf_op jit(solution)/shard_map/cond/branch_2_fun/ppermute | solution.py:39
  30.9 1.2 %collective-permute-start.18 = (bf16[512,128]{1,0:T(8,128)(2,1)S(1)}, bf16[512,128]{1,0:T(8,128)(2,1)S(1)}, u32[]{:S(2)}, u32[]{:S(2)}) collective-permute-start(bf16[512,128]{1,0:T(8,128)(2,1)S(1)} %get-tuple-element.68.rest_0_), channel_id=1, source_target_pairs={{0,128},{1,129},{2,130},{3,131},{4,132},{5,133},{6,134},{7,135},{8... | collective-permute-start | bytes 393224 | tf_op jit(solution)/shard_map/ppermute | solution.py:39
  32.1 2.1 %collective-permute-start.17 = (bf16[512,128]{1,0:T(8,128)(2,1)S(1)}, bf16[512,128]{1,0:T(8,128)(2,1)S(1)}, u32[]{:S(2)}, u32[]{:S(2)}) collective-permute-start(bf16[512,128]{1,0:T(8,128)(2,1)S(1)} %get-tuple-element.68.rest_0_), channel_id=1, source_target_pairs={{0,192},{1,193},{2,194},{3,195},{4,196},{5,197},{6,198},{7,199},{8... | collective-permute-start | bytes 393224 | tf_op jit(solution)/shard_map/ppermute | solution.py:39
  34.2 0.0 collective-permute-start.16
  34.2 0.0 collective-permute-start.19
  34.2 3.4 %collective-permute-done.18.rest_3_ = bf16[512,128]{1,0:T(8,128)(2,1)S(1)} collective-permute-done((bf16[512,128]{1,0:T(8,128)(2,1)S(1)}, bf16[512,128]{1,0:T(8,128)(2,1)S(1)}, u32[]{:S(2)}, u32[]{:S(2)}) %collective-permute-start.18) | collective-permute-done | bytes 131104 | tf_op jit(solution)/shard_map/ppermute | solution.py:39
  37.7 0.0 collective-permute-start.22
  37.7 0.0 collective-permute-done.17.rest_2_
  37.7 0.5 collective-permute-start.21
  38.2 2.2 %collective-permute-done.16.rest_1_ = bf16[512,128]{1,0:T(8,128)(2,1)S(1)} collective-permute-done((bf16[512,128]{1,0:T(8,128)(2,1)S(1)}, bf16[512,128]{1,0:T(8,128)(2,1)S(1)}, u32[]{:S(2)}, u32[]{:S(2)}) %collective-permute-start.16) | collective-permute-done | bytes 131104 | tf_op jit(solution)/shard_map/ppermute | solution.py:39
  40.4 0.0 collective-permute-start.20
  40.4 0.1 pad_add_fusion.place_ref
  40.5 0.0 collective-permute-done.19.rest_4_
  40.5 0.0 collective-permute-done.22.rest_7_
  40.5 0.0 collective-permute-done.21.rest_6_
  40.5 1.3 %collective-permute-done.20.rest_5_ = bf16[512,128]{1,0:T(8,128)(2,1)S(1)} collective-permute-done((bf16[512,128]{1,0:T(8,128)(2,1)S(1)}, bf16[512,128]{1,0:T(8,128)(2,1)S(1)}, u32[]{:S(2)}, u32[]{:S(2)}) %collective-permute-start.20) | collective-permute-done | bytes 131104 | tf_op jit(solution)/shard_map/ppermute | solution.py:39
  41.8 3.9 %shard_map.113 = (bf16[96,512]{1,0:T(8,128)(2,1)S(1)}, bf16[96,512]{1,0:T(8,128)(2,1)S(1)}, bf16[96,512]{1,0:T(8,128)(2,1)S(1)}, bf16[96,512]{1,0:T(8,128)(2,1)S...) custom-call(s32[2]{0:T(128)S(1)} %pad_add_fusion.place_ref, ...), custom_call_target="tpu_custom_call" | custom-call | flops 1207959552 | bytes 5242880 | tf_op jit(solution)/shard_map/pallas_call | solution.py:306
  45.6 1.7 %collective-permute-start.23 = (bf16[96,512]{1,0:T(8,128)(2,1)S(1)}, bf16[96,512]{1,0:T(8,128)(2,1)S(1)}, u32[]{:S(2)}, u32[]{:S(2)}) collective-permute-start(bf16[96,512]{1,0:T(8,128)(2,1)S(1)} %get-tuple-element.61), channel_id=1, source_target_pairs={{0,1},{1,2},{2,3},{3,0},{4,5},{5,6},{6,7},{7,4},{8,9},{9,10},{10,1... | collective-permute-start | bytes 294920 | tf_op jit(solution)/shard_map/ppermute | solution.py:39
  47.3 2.9 %collective-permute-start.24 = (bf16[96,512]{1,0:T(8,128)(2,1)S(1)}, bf16[96,512]{1,0:T(8,128)(2,1)S(1)}, u32[]{:S(2)}, u32[]{:S(2)}) collective-permute-start(bf16[96,512]{1,0:T(8,128)(2,1)S(1)} %get-tuple-element.62), channel_id=1, source_target_pairs={{0,2},{1,3},{2,0},{3,1},{4,6},{5,7},{6,4},{7,5},{8,10},{9,11},{10,... | collective-permute-start | bytes 294920 | tf_op jit(solution)/shard_map/ppermute | solution.py:39
  50.2 1.3 %collective-permute-start.25 = (bf16[96,512]{1,0:T(8,128)(2,1)S(1)}, bf16[96,512]{1,0:T(8,128)(2,1)S(1)}, u32[]{:S(2)}, u32[]{:S(2)}) collective-permute-start(bf16[96,512]{1,0:T(8,128)(2,1)S(1)} %get-tuple-element.63), channel_id=1, source_target_pairs={{0,3},{1,0},{2,1},{3,2},{4,7},{5,4},{6,5},{7,6},{8,11},{9,8},{10,9... | collective-permute-start | bytes 294920 | tf_op jit(solution)/shard_map/ppermute | solution.py:39
  51.6 0.7 collective-permute-start.30
  52.2 0.8 %collective-permute-start.31 = (bf16[96,512]{1,0:T(8,128)(2,1)S(1)}, bf16[96,512]{1,0:T(8,128)(2,1)S(1)}, u32[]{:S(2)}, u32[]{:S(2)}) collective-permute-start(bf16[96,512]{1,0:T(8,128)(2,1)S(1)} %get-tuple-element.66), channel_id=1, source_target_pairs={{0,2},{1,3},{2,0},{3,1},{4,6},{5,7},{6,4},{7,5},{8,10},{9,11},{10,... | collective-permute-start | bytes 294920 | tf_op jit(solution)/shard_map/ppermute | solution.py:39
  53.0 0.0 collective-permute-done.23
  53.0 1.9 %collective-permute-start.32 = (bf16[96,512]{1,0:T(8,128)(2,1)S(1)}, bf16[96,512]{1,0:T(8,128)(2,1)S(1)}, u32[]{:S(2)}, u32[]{:S(2)}) collective-permute-start(bf16[96,512]{1,0:T(8,128)(2,1)S(1)} %get-tuple-element.67), channel_id=1, source_target_pairs={{0,3},{1,0},{2,1},{3,2},{4,7},{5,4},{6,5},{7,6},{8,11},{9,8},{10,9... | collective-permute-start | bytes 294920 | tf_op jit(solution)/shard_map/ppermute | solution.py:39
  54.9 1.0 %collective-permute-done.24 = bf16[96,512]{1,0:T(8,128)(2,1)S(1)} collective-permute-done((bf16[96,512]{1,0:T(8,128)(2,1)S(1)}, bf16[96,512]{1,0:T(8,128)(2,1)S(1)}, u32[]{:S(2)}, u32[]{:S(2)}) %collective-permute-start.24) | collective-permute-done | bytes 98336 | tf_op jit(solution)/shard_map/ppermute | solution.py:39
  55.9 0.0 collective-permute-done.25
  55.9 0.1 add_convert_fusion.3
  56.0 0.1 collective-permute-start.26
  56.1 3.4 %collective-permute-done.30 = bf16[96,512]{1,0:T(8,128)(2,1)S(1)} collective-permute-done((bf16[96,512]{1,0:T(8,128)(2,1)S(1)}, bf16[96,512]{1,0:T(8,128)(2,1)S(1)}, u32[]{:S(2)}, u32[]{:S(2)}) %collective-permute-start.30) | collective-permute-done | bytes 98336 | tf_op jit(solution)/shard_map/ppermute | solution.py:39
  59.5 0.0 collective-permute-done.31
  59.5 0.0 collective-permute-done.32
  59.5 0.1 add_convert_fusion.1
  59.6 0.1 collective-permute-start.33
  59.7 1.0 %collective-permute-done.26 = bf16[96,512]{1,0:T(8,128)(2,1)S(1)} collective-permute-done((bf16[96,512]{1,0:T(8,128)(2,1)S(1)}, bf16[96,512]{1,0:T(8,128)(2,1)S(1)}, u32[]{:S(2)}, u32[]{:S(2)}) %collective-permute-start.26) | collective-permute-done | bytes 98336 | tf_op jit(solution)/shard_map/ppermute | solution.py:39
  60.7 1.5 %collective-permute-start.29 = (bf16[96,512]{1,0:T(8,128)(2,1)S(1)}, bf16[96,512]{1,0:T(8,128)(2,1)S(1)}, u32[]{:S(2)}, u32[]{:S(2)}) collective-permute-start(bf16[96,512]{1,0:T(8,128)(2,1)S(1)} %add_convert_fusion.2.rest_0_), channel_id=1, source_target_pairs={{0,3},{1,0},{2,1},{3,2},{4,7},{5,4},{6,5},{7,6},{8,11},{9,8},{10,9... | collective-permute-start | bytes 294920 | tf_op jit(solution)/shard_map/ppermute | solution.py:39
  62.2 1.6 %collective-permute-start.28 = (bf16[96,512]{1,0:T(8,128)(2,1)S(1)}, bf16[96,512]{1,0:T(8,128)(2,1)S(1)}, u32[]{:S(2)}, u32[]{:S(2)}) collective-permute-start(bf16[96,512]{1,0:T(8,128)(2,1)S(1)} %add_convert_fusion.2.rest_0_), channel_id=1, source_target_pairs={{0,2},{1,3},{2,0},{3,1},{4,6},{5,7},{6,4},{7,5},{8,10},{9,11},{10,... | collective-permute-start | bytes 294920 | tf_op jit(solution)/shard_map/ppermute | solution.py:39
  63.9 1.3 %collective-permute-start.27 = (bf16[96,512]{1,0:T(8,128)(2,1)S(1)}, bf16[96,512]{1,0:T(8,128)(2,1)S(1)}, u32[]{:S(2)}, u32[]{:S(2)}) collective-permute-start(bf16[96,512]{1,0:T(8,128)(2,1)S(1)} %add_convert_fusion.2.rest_0_), channel_id=1, source_target_pairs={{0,1},{1,2},{2,3},{3,0},{4,5},{5,6},{6,7},{7,4},{8,9},{9,10},{10,1... | collective-permute-start | bytes 294920 | tf_op jit(solution)/shard_map/ppermute | solution.py:39
  65.2 0.0 collective-permute-done.33
  65.2 2.0 %collective-permute-start.36 = (bf16[96,512]{1,0:T(8,128)(2,1)S(1)}, bf16[96,512]{1,0:T(8,128)(2,1)S(1)}, u32[]{:S(2)}, u32[]{:S(2)}) collective-permute-start(bf16[96,512]{1,0:T(8,128)(2,1)S(1)} %add_convert_fusion.rest_4_), channel_id=1, source_target_pairs={{0,3},{1,0},{2,1},{3,2},{4,7},{5,4},{6,5},{7,6},{8,11},{9,8},{10,9... | collective-permute-start | bytes 294920 | tf_op jit(solution)/shard_map/ppermute | solution.py:39
  67.2 0.7 collective-permute-start.35
  67.9 0.0 collective-permute-done.29.rest_3_
  67.9 0.6 collective-permute-start.34
  68.5 0.5 collective-permute-done.28.rest_2_
  69.0 2.5 %collective-permute-done.27.rest_1_ = bf16[96,512]{1,0:T(8,128)(2,1)S(1)} collective-permute-done((bf16[96,512]{1,0:T(8,128)(2,1)S(1)}, bf16[96,512]{1,0:T(8,128)(2,1)S(1)}, u32[]{:S(2)}, u32[]{:S(2)}) %collective-permute-start.27) | collective-permute-done | bytes 98336 | tf_op jit(solution)/shard_map/ppermute | solution.py:39
  71.5 0.0 collective-permute-done.36.rest_7_
  71.5 1.9 %collective-permute-done.35.rest_6_ = bf16[96,512]{1,0:T(8,128)(2,1)S(1)} collective-permute-done((bf16[96,512]{1,0:T(8,128)(2,1)S(1)}, bf16[96,512]{1,0:T(8,128)(2,1)S(1)}, u32[]{:S(2)}, u32[]{:S(2)}) %collective-permute-start.35) | collective-permute-done | bytes 98336 | tf_op jit(solution)/shard_map/ppermute | solution.py:39
  73.4 1.0 %collective-permute-done.34.rest_5_ = bf16[96,512]{1,0:T(8,128)(2,1)S(1)} collective-permute-done((bf16[96,512]{1,0:T(8,128)(2,1)S(1)}, bf16[96,512]{1,0:T(8,128)(2,1)S(1)}, u32[]{:S(2)}, u32[]{:S(2)}) %collective-permute-start.34) | collective-permute-done | bytes 98336 | tf_op jit(solution)/shard_map/ppermute | solution.py:39
  74.4 0.9 %shard_map.114 = bf16[96,4096]{1,0:T(8,128)(2,1)} custom-call(s32[1]{0:T(128)S(6)} %select_n.46.y_ref, bf16[96,512]{1,0:T(8,128)(2,1)S(1)} %add_convert_fusion.2.rest_0_, bf16[96,512]{1,0:T(8,128)(2,1)S(1)} %collective-permute-done.27.rest_1_, bf16[96,512]{1,0:T(8,128)(2,1)S(1)} %collective-permute-done.28.rest_2_, ...), custom_call_target="tpu_custom_call" | custom-call | tf_op jit(solution)/shard_map/pallas_call | solution.py:354
  (5 shorter events, 0.2 us)
Async XLA Ops:
  0.0 2.1 %collective-permute-start.12 = (bf16[2048,128]{1,0:T(8,128)(2,1)}, bf16[2048,128]{1,0:T(8,128)(2,1)S(1)}, u32[]{:S(2)}, u32[]{:S(2)}) collective-permute-start(bf16[2048,128]{1,0:T(8,128)(2,1)} %bitcast.21), channel_id=1, source_target_pairs={{0,8},{1,9},{2,10},{3,11},{4,12},{5,13},{6,14},{7,15},{8,0},{9,1},... | collective-permute-start | bytes 1572872 | tf_op jit(solution)/shard_map/ppermute | solution.py:39
  2.2 11.9 %collective-permute-start.13 = (bf16[512,128]{1,0:T(8,128)(2,1)S(1)}, bf16[512,128]{1,0:T(8,128)(2,1)S(1)}, u32[]{:S(2)}, u32[]{:S(2)}) collective-permute-start(bf16[512,128]{1,0:T(8,128)(2,1)S(1)} %get-tuple-element.52), channel_id=1, source_target_pairs={{0,64},{1,65},{2,66},{3,67},{4,68},{5,69},{6,70},{7,71},{8,72},{9,... | collective-permute-start | bytes 393224 | tf_op jit(solution)/shard_map/ppermute | solution.py:39
  3.7 10.4 %collective-permute-start.14 = (bf16[512,128]{1,0:T(8,128)(2,1)S(1)}, bf16[512,128]{1,0:T(8,128)(2,1)S(1)}, u32[]{:S(2)}, u32[]{:S(2)}) collective-permute-start(bf16[512,128]{1,0:T(8,128)(2,1)S(1)} %get-tuple-element.53), channel_id=1, source_target_pairs={{0,128},{1,129},{2,130},{3,131},{4,132},{5,133},{6,134},{7,135},{8... | collective-permute-start | bytes 393224 | tf_op jit(solution)/shard_map/ppermute | solution.py:39
  6.5 7.7 %collective-permute-start.15 = (bf16[512,128]{1,0:T(8,128)(2,1)S(1)}, bf16[512,128]{1,0:T(8,128)(2,1)S(1)}, u32[]{:S(2)}, u32[]{:S(2)}) collective-permute-start(bf16[512,128]{1,0:T(8,128)(2,1)S(1)} %get-tuple-element.54), channel_id=1, source_target_pairs={{0,192},{1,193},{2,194},{3,195},{4,196},{5,197},{6,198},{7,199},{8... | collective-permute-start | bytes 393224 | tf_op jit(solution)/shard_map/ppermute | solution.py:39
  14.2 2.7 %collective-permute-start.8 = (bf16[512,128]{1,0:T(8,128)(2,1)S(1)}, bf16[512,128]{1,0:T(8,128)(2,1)S(1)}, u32[]{:S(2)}, u32[]{:S(2)}) collective-permute-start(bf16[512,128]{1,0:T(8,128)(2,1)S(1)} %get-tuple-element.31.refs_0_), channel_id=1, source_target_pairs={{32,48},{33,49},{34,50},{35,51},{36,52},{37,53},{38,54},{39,55},{4... | collective-permute-start | bytes 393224 | tf_op jit(solution)/shard_map/cond/branch_2_fun/ppermute | solution.py:39
  14.9 2.0 %collective-permute-start.7 = (bf16[512,128]{1,0:T(8,128)(2,1)S(1)}, bf16[512,128]{1,0:T(8,128)(2,1)S(1)}, u32[]{:S(2)}, u32[]{:S(2)}) collective-permute-start(bf16[512,128]{1,0:T(8,128)(2,1)S(1)} %get-tuple-element.31.refs_0_), channel_id=1, source_target_pairs={{32,16},{33,17},{34,18},{35,19},{36,20},{37,21},{38,22},{39,23},{4... | collective-permute-start | bytes 393224 | tf_op jit(solution)/shard_map/cond/branch_2_fun/ppermute | solution.py:39
  15.6 15.3 %collective-permute-start.6 = (bf16[512,128]{1,0:T(8,128)(2,1)S(1)}, bf16[512,128]{1,0:T(8,128)(2,1)S(1)}, u32[]{:S(2)}, u32[]{:S(2)}) collective-permute-start(bf16[512,128]{1,0:T(8,128)(2,1)S(1)} %get-tuple-element.31.refs_0_), channel_id=1, source_target_pairs={{32,0},{33,1},{34,2},{35,3},{36,4},{37,5},{38,6},{39,7},{40,8},{41... | collective-permute-start | bytes 393224 | tf_op jit(solution)/shard_map/cond/branch_2_fun/ppermute | solution.py:39
  30.9 6.8 %collective-permute-start.18 = (bf16[512,128]{1,0:T(8,128)(2,1)S(1)}, bf16[512,128]{1,0:T(8,128)(2,1)S(1)}, u32[]{:S(2)}, u32[]{:S(2)}) collective-permute-start(bf16[512,128]{1,0:T(8,128)(2,1)S(1)} %get-tuple-element.68.rest_0_), channel_id=1, source_target_pairs={{0,128},{1,129},{2,130},{3,131},{4,132},{5,133},{6,134},{7,135},{8... | collective-permute-start | bytes 393224 | tf_op jit(solution)/shard_map/ppermute | solution.py:39
  32.1 5.6 %collective-permute-start.17 = (bf16[512,128]{1,0:T(8,128)(2,1)S(1)}, bf16[512,128]{1,0:T(8,128)(2,1)S(1)}, u32[]{:S(2)}, u32[]{:S(2)}) collective-permute-start(bf16[512,128]{1,0:T(8,128)(2,1)S(1)} %get-tuple-element.68.rest_0_), channel_id=1, source_target_pairs={{0,192},{1,193},{2,194},{3,195},{4,196},{5,197},{6,198},{7,199},{8... | collective-permute-start | bytes 393224 | tf_op jit(solution)/shard_map/ppermute | solution.py:39
  34.2 6.2 %collective-permute-start.16 = (bf16[512,128]{1,0:T(8,128)(2,1)S(1)}, bf16[512,128]{1,0:T(8,128)(2,1)S(1)}, u32[]{:S(2)}, u32[]{:S(2)}) collective-permute-start(bf16[512,128]{1,0:T(8,128)(2,1)S(1)} %get-tuple-element.68.rest_0_), channel_id=1, source_target_pairs={{0,64},{1,65},{2,66},{3,67},{4,68},{5,69},{6,70},{7,71},{8,72},{9,... | collective-permute-start | bytes 393224 | tf_op jit(solution)/shard_map/ppermute | solution.py:39
  34.2 6.3 %collective-permute-start.19 = (bf16[512,128]{1,0:T(8,128)(2,1)S(1)}, bf16[512,128]{1,0:T(8,128)(2,1)S(1)}, u32[]{:S(2)}, u32[]{:S(2)}) collective-permute-start(bf16[512,128]{1,0:T(8,128)(2,1)S(1)} %get-tuple-element.68.rest_0_), channel_id=1, source_target_pairs={{0,8},{1,9},{2,10},{3,11},{4,12},{5,13},{6,14},{7,15},{8,0},{9,1},... | collective-permute-start | bytes 393224 | tf_op jit(solution)/shard_map/ppermute | solution.py:39
  37.7 2.8 %collective-permute-start.22 = (bf16[512,128]{1,0:T(8,128)(2,1)S(1)}, bf16[512,128]{1,0:T(8,128)(2,1)S(1)}, u32[]{:S(2)}, u32[]{:S(2)}) collective-permute-start(bf16[512,128]{1,0:T(8,128)(2,1)S(1)} %collective-permute-done.18.rest_3_), channel_id=1, source_target_pairs={{0,8},{1,9},{2,10},{3,11},{4,12},{5,13},{6,14},{7,15},{8,0},{9,1},... | collective-permute-start | bytes 393224 | tf_op jit(solution)/shard_map/ppermute | solution.py:39
  37.7 2.8 %collective-permute-start.21 = (bf16[512,128]{1,0:T(8,128)(2,1)S(1)}, bf16[512,128]{1,0:T(8,128)(2,1)S(1)}, u32[]{:S(2)}, u32[]{:S(2)}) collective-permute-start(bf16[512,128]{1,0:T(8,128)(2,1)S(1)} %collective-permute-done.17.rest_2_), channel_id=1, source_target_pairs={{0,8},{1,9},{2,10},{3,11},{4,12},{5,13},{6,14},{7,15},{8,0},{9,1},... | collective-permute-start | bytes 393224 | tf_op jit(solution)/shard_map/ppermute | solution.py:39
  40.4 1.3 %collective-permute-start.20 = (bf16[512,128]{1,0:T(8,128)(2,1)S(1)}, bf16[512,128]{1,0:T(8,128)(2,1)S(1)}, u32[]{:S(2)}, u32[]{:S(2)}) collective-permute-start(bf16[512,128]{1,0:T(8,128)(2,1)S(1)} %collective-permute-done.16.rest_1_), channel_id=1, source_target_pairs={{0,8},{1,9},{2,10},{3,11},{4,12},{5,13},{6,14},{7,15},{8,0},{9,1},... | collective-permute-start | bytes 393224 | tf_op jit(solution)/shard_map/ppermute | solution.py:39
  45.6 7.4 %collective-permute-start.23 = (bf16[96,512]{1,0:T(8,128)(2,1)S(1)}, bf16[96,512]{1,0:T(8,128)(2,1)S(1)}, u32[]{:S(2)}, u32[]{:S(2)}) collective-permute-start(bf16[96,512]{1,0:T(8,128)(2,1)S(1)} %get-tuple-element.61), channel_id=1, source_target_pairs={{0,1},{1,2},{2,3},{3,0},{4,5},{5,6},{6,7},{7,4},{8,9},{9,10},{10,1... | collective-permute-start | bytes 294920 | tf_op jit(solution)/shard_map/ppermute | solution.py:39
  47.3 8.6 %collective-permute-start.24 = (bf16[96,512]{1,0:T(8,128)(2,1)S(1)}, bf16[96,512]{1,0:T(8,128)(2,1)S(1)}, u32[]{:S(2)}, u32[]{:S(2)}) collective-permute-start(bf16[96,512]{1,0:T(8,128)(2,1)S(1)} %get-tuple-element.62), channel_id=1, source_target_pairs={{0,2},{1,3},{2,0},{3,1},{4,6},{5,7},{6,4},{7,5},{8,10},{9,11},{10,... | collective-permute-start | bytes 294920 | tf_op jit(solution)/shard_map/ppermute | solution.py:39
  50.2 5.7 %collective-permute-start.25 = (bf16[96,512]{1,0:T(8,128)(2,1)S(1)}, bf16[96,512]{1,0:T(8,128)(2,1)S(1)}, u32[]{:S(2)}, u32[]{:S(2)}) collective-permute-start(bf16[96,512]{1,0:T(8,128)(2,1)S(1)} %get-tuple-element.63), channel_id=1, source_target_pairs={{0,3},{1,0},{2,1},{3,2},{4,7},{5,4},{6,5},{7,6},{8,11},{9,8},{10,9... | collective-permute-start | bytes 294920 | tf_op jit(solution)/shard_map/ppermute | solution.py:39
  51.6 8.0 %collective-permute-start.30 = (bf16[96,512]{1,0:T(8,128)(2,1)S(1)}, bf16[96,512]{1,0:T(8,128)(2,1)S(1)}, u32[]{:S(2)}, u32[]{:S(2)}) collective-permute-start(bf16[96,512]{1,0:T(8,128)(2,1)S(1)} %get-tuple-element.65), channel_id=1, source_target_pairs={{0,1},{1,2},{2,3},{3,0},{4,5},{5,6},{6,7},{7,4},{8,9},{9,10},{10,1... | collective-permute-start | bytes 294920 | tf_op jit(solution)/shard_map/ppermute | solution.py:39
  52.2 7.3 %collective-permute-start.31 = (bf16[96,512]{1,0:T(8,128)(2,1)S(1)}, bf16[96,512]{1,0:T(8,128)(2,1)S(1)}, u32[]{:S(2)}, u32[]{:S(2)}) collective-permute-start(bf16[96,512]{1,0:T(8,128)(2,1)S(1)} %get-tuple-element.66), channel_id=1, source_target_pairs={{0,2},{1,3},{2,0},{3,1},{4,6},{5,7},{6,4},{7,5},{8,10},{9,11},{10,... | collective-permute-start | bytes 294920 | tf_op jit(solution)/shard_map/ppermute | solution.py:39
  53.0 6.5 %collective-permute-start.32 = (bf16[96,512]{1,0:T(8,128)(2,1)S(1)}, bf16[96,512]{1,0:T(8,128)(2,1)S(1)}, u32[]{:S(2)}, u32[]{:S(2)}) collective-permute-start(bf16[96,512]{1,0:T(8,128)(2,1)S(1)} %get-tuple-element.67), channel_id=1, source_target_pairs={{0,3},{1,0},{2,1},{3,2},{4,7},{5,4},{6,5},{7,6},{8,11},{9,8},{10,9... | collective-permute-start | bytes 294920 | tf_op jit(solution)/shard_map/ppermute | solution.py:39
  56.0 4.7 %collective-permute-start.26 = (bf16[96,512]{1,0:T(8,128)(2,1)S(1)}, bf16[96,512]{1,0:T(8,128)(2,1)S(1)}, u32[]{:S(2)}, u32[]{:S(2)}) collective-permute-start(bf16[96,512]{1,0:T(8,128)(2,1)S(1)} %add_convert_fusion.3), channel_id=1, source_target_pairs={{0,4},{1,5},{2,6},{3,7},{4,0},{5,1},{6,2},{7,3},{8,12},{9,13},{10,... | collective-permute-start | bytes 294920 | tf_op jit(solution)/shard_map/ppermute | solution.py:39
  59.6 5.6 %collective-permute-start.33 = (bf16[96,512]{1,0:T(8,128)(2,1)S(1)}, bf16[96,512]{1,0:T(8,128)(2,1)S(1)}, u32[]{:S(2)}, u32[]{:S(2)}) collective-permute-start(bf16[96,512]{1,0:T(8,128)(2,1)S(1)} %add_convert_fusion.1), channel_id=1, source_target_pairs={{0,4},{1,5},{2,6},{3,7},{4,0},{5,1},{6,2},{7,3},{8,12},{9,13},{10,... | collective-permute-start | bytes 294920 | tf_op jit(solution)/shard_map/ppermute | solution.py:39
  60.7 7.2 %collective-permute-start.29 = (bf16[96,512]{1,0:T(8,128)(2,1)S(1)}, bf16[96,512]{1,0:T(8,128)(2,1)S(1)}, u32[]{:S(2)}, u32[]{:S(2)}) collective-permute-start(bf16[96,512]{1,0:T(8,128)(2,1)S(1)} %add_convert_fusion.2.rest_0_), channel_id=1, source_target_pairs={{0,3},{1,0},{2,1},{3,2},{4,7},{5,4},{6,5},{7,6},{8,11},{9,8},{10,9... | collective-permute-start | bytes 294920 | tf_op jit(solution)/shard_map/ppermute | solution.py:39
  62.2 6.7 %collective-permute-start.28 = (bf16[96,512]{1,0:T(8,128)(2,1)S(1)}, bf16[96,512]{1,0:T(8,128)(2,1)S(1)}, u32[]{:S(2)}, u32[]{:S(2)}) collective-permute-start(bf16[96,512]{1,0:T(8,128)(2,1)S(1)} %add_convert_fusion.2.rest_0_), channel_id=1, source_target_pairs={{0,2},{1,3},{2,0},{3,1},{4,6},{5,7},{6,4},{7,5},{8,10},{9,11},{10,... | collective-permute-start | bytes 294920 | tf_op jit(solution)/shard_map/ppermute | solution.py:39
  63.9 7.7 %collective-permute-start.27 = (bf16[96,512]{1,0:T(8,128)(2,1)S(1)}, bf16[96,512]{1,0:T(8,128)(2,1)S(1)}, u32[]{:S(2)}, u32[]{:S(2)}) collective-permute-start(bf16[96,512]{1,0:T(8,128)(2,1)S(1)} %add_convert_fusion.2.rest_0_), channel_id=1, source_target_pairs={{0,1},{1,2},{2,3},{3,0},{4,5},{5,6},{6,7},{7,4},{8,9},{9,10},{10,1... | collective-permute-start | bytes 294920 | tf_op jit(solution)/shard_map/ppermute | solution.py:39
  65.2 6.3 %collective-permute-start.36 = (bf16[96,512]{1,0:T(8,128)(2,1)S(1)}, bf16[96,512]{1,0:T(8,128)(2,1)S(1)}, u32[]{:S(2)}, u32[]{:S(2)}) collective-permute-start(bf16[96,512]{1,0:T(8,128)(2,1)S(1)} %add_convert_fusion.rest_4_), channel_id=1, source_target_pairs={{0,3},{1,0},{2,1},{3,2},{4,7},{5,4},{6,5},{7,6},{8,11},{9,8},{10,9... | collective-permute-start | bytes 294920 | tf_op jit(solution)/shard_map/ppermute | solution.py:39
  67.2 6.2 %collective-permute-start.35 = (bf16[96,512]{1,0:T(8,128)(2,1)S(1)}, bf16[96,512]{1,0:T(8,128)(2,1)S(1)}, u32[]{:S(2)}, u32[]{:S(2)}) collective-permute-start(bf16[96,512]{1,0:T(8,128)(2,1)S(1)} %add_convert_fusion.rest_4_), channel_id=1, source_target_pairs={{0,2},{1,3},{2,0},{3,1},{4,6},{5,7},{6,4},{7,5},{8,10},{9,11},{10,... | collective-permute-start | bytes 294920 | tf_op jit(solution)/shard_map/ppermute | solution.py:39
  67.9 6.5 %collective-permute-start.34 = (bf16[96,512]{1,0:T(8,128)(2,1)S(1)}, bf16[96,512]{1,0:T(8,128)(2,1)S(1)}, u32[]{:S(2)}, u32[]{:S(2)}) collective-permute-start(bf16[96,512]{1,0:T(8,128)(2,1)S(1)} %add_convert_fusion.rest_4_), channel_id=1, source_target_pairs={{0,1},{1,2},{2,3},{3,0},{4,5},{5,6},{6,7},{7,4},{8,9},{9,10},{10,1... | collective-permute-start | bytes 294920 | tf_op jit(solution)/shard_map/ppermute | solution.py:39
